TPU v7x, 32 devices: a whole 2x2x4 slice. The times are simulated.
32 devices in a mesh: seq: 4 (over z), dp: 8 (over y, x, core).
Axes of the slice: x: 2, y: 2, z: 4, core: 2. Of those that a mesh axis runs over, the one named last changes fastest.
Arguments:
- layer_input: bfloat16 [8192, 1024], P(('dp', 'seq')), may hold values from -6 to 6
- out_grad: bfloat16 [8192, 1024], P(('dp', 'seq')), may hold values from -6 to 6
- lengths: int32 [8, 3], P('dp'), may hold values from 1 to 682, 1024 in all within a row
- item_owner: int32 [8192, 1], P(('dp', 'seq')), may hold values from 0 to 31; in each aligned block of 256 rows (0 to 255, 256 to 511, ...) at most 16 rows name the same one
- item_row: int32 [8192], P(('dp', 'seq')), may hold values from 0 to 511
- w_attn: bfloat16 [1024, 3072], replicated, may hold values from -0.1875 to 0.1875
- w_gate: bfloat16 [1024, 1024], replicated, may hold values from -0.1875 to 0.1875
- w_out: bfloat16 [1024, 1024], replicated, may hold values from -0.1875 to 0.1875
- emb_table: float32 [16384, 1024], P(('seq', 'dp')), may hold values from -6 to 6
- row_accum: float32 [16384], P(('seq', 'dp')), may hold values from 0.25 to 4
Outputs:
- grad_attn: float32 [1024, 3072], P('dp', 'seq')
- grad_gate: float32 [1024, 1024], P('dp', 'seq')
- grad_out: float32 [1024, 1024], P('dp', 'seq')
- new_table: float32 [16384, 1024], P(('seq', 'dp'))
- new_accum: float32 [16384], P(('seq', 'dp'))
Inputs may be any that keep to these rules, and one draw needn't show every extreme that they name: Each group's 3 lengths sum to 1024; the largest is exactly 682. `item_owner`: among the 256 events of one device at most 16 name one owner, a bound that some block reaches.
All inputs are finite; a program needn't handle non-finite values.
Results may differ from a plain program's by a relative error of at most 0.0092.
Values may be sent and summed in bfloat16 or wider, within the bound.
No kernel may reach another device: no remote copies, remote signals or barrier semaphores. Data moves between devices by JAX's collectives and lax.ppermute only.
A program may use at most 128 MiB of HBM per device.

v0:
```python
import jax
import jax.numpy as jnp
from jax import lax
from jax.sharding import PartitionSpec as P

D = 1024
H = 16
DH = 64


NORM_EPS = 1e-05
LEARN_RATE = 0.1


def silu_grad(pre_act):
    sigmoid = jax.nn.sigmoid(pre_act)
    return sigmoid * (1.0 + pre_act * (1.0 - sigmoid))


def segment_ids(length_row, positions):
    seg_ends = jnp.cumsum(length_row)
    places = jnp.arange(positions, dtype=jnp.int32)
    return jnp.sum((places[:, None] >= seg_ends[None, :]).astype(jnp.int32), axis=1)


def body(
    layer_input,
    out_grad,
    lengths,
    item_owner,
    item_row,
    w_attn,
    w_gate,
    w_out,
    emb_table,
    row_accum,
):
    seq_count = lax.axis_size("seq")
    devices = lax.axis_size(("seq", "dp"))
    tokens_dev = layer_input.shape[0]
    positions = tokens_dev * seq_count
    maxlen = 2 * positions // 3
    head_local = H // seq_count
    block = min(512, positions)
    blocks = positions // block
    scale = DH ** (-0.5)
    attn_pre = jnp.dot(layer_input, w_attn, preferred_element_type=jnp.float32)
    gate_pre = jnp.dot(layer_input, w_gate, preferred_element_type=jnp.float32)
    acts = jax.nn.silu(attn_pre).astype(jnp.bfloat16).reshape(tokens_dev, H // 2, 6 * DH)
    gate_act = jax.nn.silu(gate_pre)
    group_acts = lax.all_to_all(acts, "seq", split_axis=1, concat_axis=0, tiled=True).reshape(
        positions, head_local, 3, DH
    )
    values = group_acts[:, :, 0]
    queries = group_acts[:, :, 1]
    keys_head = group_acts[:, :, 2]
    segment = segment_ids(lengths[0], positions)
    places = jnp.arange(positions, dtype=jnp.int32)

    def block_terms(block_id):
        first = block_id * block
        query_block = lax.dynamic_slice_in_dim(queries, first, block, 0)
        seg_block = lax.dynamic_slice_in_dim(segment, first, block, 0)
        rows_here = first + jnp.arange(block, dtype=jnp.int32)
        allowed = (seg_block[:, None] == segment[None, :]) & (places[None, :] <= rows_here[:, None])
        scores = (
            jnp.einsum("qhd,khd->hqk", query_block, keys_head, preferred_element_type=jnp.float32)
            * scale
        )
        weights = jnp.where(allowed[None], jax.nn.silu(scores) / maxlen, 0.0).astype(jnp.bfloat16)
        return (first, query_block, allowed, scores, weights)

    def forward_block(state_acc, block_id):
        first, query_block, allowed, scores, weights = block_terms(block_id)
        out_block = jnp.einsum("hqk,khd->qhd", weights, values, preferred_element_type=jnp.float32)
        return (state_acc, out_block.astype(jnp.bfloat16))

    _, heads_out = lax.scan(forward_block, jnp.zeros((), jnp.float32), jnp.arange(blocks))
    heads_out = heads_out.reshape(positions, head_local // 2, 2 * DH)
    mixed_in = (
        lax.all_to_all(heads_out, "seq", split_axis=0, concat_axis=1, tiled=True)
        .reshape(tokens_dev, D)
        .astype(jnp.float32)
    )
    centred = mixed_in - jnp.mean(mixed_in, axis=1, keepdims=True)
    inv_dev = lax.rsqrt(jnp.mean(centred * centred, axis=1, keepdims=True) + NORM_EPS)
    normed = centred * inv_dev
    mixed = (normed * gate_act).astype(jnp.bfloat16)
    mixed_grad = jnp.dot(out_grad, w_out.T, preferred_element_type=jnp.float32)
    normed_grad = mixed_grad * gate_act
    gate_act_grad = mixed_grad * normed
    heads_grad = inv_dev * (
        normed_grad
        - jnp.mean(normed_grad, axis=1, keepdims=True)
        - normed * jnp.mean(normed_grad * normed, axis=1, keepdims=True)
    )
    heads_grad = heads_grad.astype(jnp.bfloat16).reshape(tokens_dev, H // 2, 2 * DH)
    grad_group = lax.all_to_all(heads_grad, "seq", split_axis=1, concat_axis=0, tiled=True).reshape(
        positions, head_local, DH
    )

    def backward_block(state_acc, block_id):
        values_acc, keys_acc = state_acc
        first, query_block, allowed, scores, weights = block_terms(block_id)
        grad_block = lax.dynamic_slice_in_dim(grad_group, first, block, 0)
        weight_grad = jnp.einsum(
            "qhd,khd->hqk", grad_block, values, preferred_element_type=jnp.float32
        )
        score_grad = jnp.where(
            allowed[None], weight_grad * silu_grad(scores) * (scale / maxlen), 0.0
        ).astype(jnp.bfloat16)
        values_acc = values_acc + jnp.einsum(
            "hqk,qhd->khd", weights, grad_block, preferred_element_type=jnp.float32
        )
        keys_acc = keys_acc + jnp.einsum(
            "hqk,qhd->khd", score_grad, query_block, preferred_element_type=jnp.float32
        )
        query_grad = jnp.einsum(
            "hqk,khd->qhd", score_grad, keys_head, preferred_element_type=jnp.float32
        )
        return ((values_acc, keys_acc), query_grad.astype(jnp.bfloat16))

    zero_acc = jnp.zeros((positions, head_local, DH), jnp.float32)
    (values_acc, keys_acc), query_grads = lax.scan(
        backward_block, (zero_acc, zero_acc), jnp.arange(blocks)
    )
    head_grads = jnp.stack(
        [
            values_acc.astype(jnp.bfloat16),
            query_grads.reshape(positions, head_local, DH),
            keys_acc.astype(jnp.bfloat16),
        ],
        axis=2,
    )
    acts_grad = lax.all_to_all(
        head_grads.reshape(positions, head_local // 2, 6 * DH),
        "seq",
        split_axis=0,
        concat_axis=1,
        tiled=True,
    ).reshape(tokens_dev, 3 * D)
    attn_grad = (acts_grad.astype(jnp.float32) * silu_grad(attn_pre)).astype(jnp.bfloat16)
    gate_grad = (gate_act_grad * silu_grad(gate_pre)).astype(jnp.bfloat16)
    input_grad = (
        jnp.dot(attn_grad, w_attn.T, preferred_element_type=jnp.float32)
        + jnp.dot(gate_grad, w_gate.T, preferred_element_type=jnp.float32)
        + out_grad.astype(jnp.float32)
    )
    grad_attn_part = jnp.dot(layer_input.T, attn_grad, preferred_element_type=jnp.float32)
    grad_gate_part = jnp.dot(layer_input.T, gate_grad, preferred_element_type=jnp.float32)
    grad_out_part = jnp.dot(mixed.T, out_grad, preferred_element_type=jnp.float32)
    partials = (grad_attn_part, grad_gate_part, grad_out_part)
    partials = (
        lax.psum_scatter(partials[0], "dp", scatter_dimension=0, tiled=True),
        lax.psum_scatter(partials[1], "dp", scatter_dimension=0, tiled=True),
        lax.psum_scatter(partials[2], "dp", scatter_dimension=0, tiled=True),
    )
    partials = (
        lax.psum_scatter(partials[0], "seq", scatter_dimension=1, tiled=True),
        lax.psum_scatter(partials[1], "seq", scatter_dimension=1, tiled=True),
        lax.psum_scatter(partials[2], "seq", scatter_dimension=1, tiled=True),
    )
    rows_own = emb_table.shape[0]
    capacity = max(2, 2 * tokens_dev // devices)
    owners = item_owner[:, 0]
    owner_hits = (owners[:, None] == jnp.arange(devices, dtype=jnp.int32)[None, :]).astype(
        jnp.int32
    )
    earlier = jnp.cumsum(owner_hits, axis=0) - owner_hits
    slots = jnp.sum(earlier * owner_hits, axis=1)
    flat_slot = owners * capacity + slots
    send_rows = jnp.zeros((devices * capacity, D), jnp.float32).at[flat_slot].set(input_grad)
    send_ids = jnp.full((devices * capacity,), rows_own, jnp.int32).at[flat_slot].set(item_row)
    got_rows, got_ids = (
        lax.all_to_all(
            send_rows.reshape(devices, capacity, D).astype(jnp.bfloat16),
            ("seq", "dp"),
            split_axis=0,
            concat_axis=0,
            tiled=True,
        ).astype(jnp.float32),
        lax.all_to_all(
            send_ids.reshape(devices, capacity),
            ("seq", "dp"),
            split_axis=0,
            concat_axis=0,
            tiled=True,
        ),
    )
    got_rows = got_rows.reshape(devices * capacity, D)
    got_ids = got_ids.reshape(devices * capacity)
    table_grad = jnp.zeros((rows_own, D), jnp.float32).at[got_ids].add(got_rows, mode="drop")
    new_accum = row_accum + jnp.mean(table_grad * table_grad, axis=1)
    new_table = emb_table - LEARN_RATE * table_grad * lax.rsqrt(new_accum)[:, None]
    return (partials[0], partials[1], partials[2], new_table, new_accum)


def solution(mesh):
    placed = (
        P(("dp", "seq"), None),
        P(("dp", "seq"), None),
        P("dp", None),
        P(("dp", "seq"), None),
        P(("dp", "seq")),
        P(),
        P(),
        P(),
        P(("seq", "dp"), None),
        P(("seq", "dp")),
    )
    return jax.shard_map(
        body,
        mesh=mesh,
        in_specs=placed,
        out_specs=(
            P("dp", "seq"),
            P("dp", "seq"),
            P("dp", "seq"),
            P(("seq", "dp"), None),
            P(("seq", "dp")),
        ),
        check_vma=False,
    )
```

profile of v0, /device:TPU:0, one launch (start us, length us, event | category | flops | bytes accessed | tf_op | source)
XLA Modules:
  0.0 501.7 jit_solution(2438503926686086169)
XLA Ops:
  7.2 6.7 %multiply_convert_fusion.1 = (bf16[256,3072]{1,0:T(8,128)(2,1)S(1)}, f32[256,3072]{1,0:T(8,128)}) fusion(bf16[256,1024]{1,0:T(8,128)(2,1)} %param.14, bf16[1024,3072]{1,0:T(8,128)(2,1)} %param.19), kind=kOutput, calls=%fused_computation.50 | convolution fusion | flops 1614544896 | bytes 11534336 | tf_op jit(solution)/shard_map/dot_general | solution.py:47
  15.2 6.3 %all-to-all-start = ((bf16[256,8,384]{2,0,1:T(8,128)(2,1)}), bf16[256,8,384]{2,0,1:T(8,128)(2,1)}, u32[]{:S(2)}, u32[]{:S(2)}) async-start(bf16[256,8,384]{2,0,1:T(8,128)(2,1)} %bitcast.145), calls=%async_computation | async-start | bytes 3145728 | tf_op jit(solution)/shard_map/all_to_all | solution.py:51
  21.8 36.8 %all-to-all-done = bf16[256,8,384]{2,0,1:T(8,128)(2,1)} async-done(((bf16[256,8,384]{2,0,1:T(8,128)(2,1)}), bf16[256,8,384]{2,0,1:T(8,128)(2,1)}, u32[]{:S(2)}, u32[]{:S(2)}) %all-to-all-start) | async-done | bytes 1572896 | tf_op jit(solution)/shard_map/all_to_all | solution.py:51
  69.3 17.1 %while.26 = (s32[]{:T(128)}, bf16[2,512,4,64]{1,3,2,0:T(8,128)(2,1)}, s32[2]{0:T(128)S(1)}, s32[1024]{0:T(1024)S(1)}, bf16[1024,4,64]{0,2,1:T(8,128)(2,1)S(1)}, ...) while((s32[]{:T(128)}, ...), condition=%wide.region_3.4_spmd.clone, body=%wide.region_2.3_spmd.clone.sunk | while | flops 555352576 | bytes 2635967 | solution.py:78
  72.0 5.8 %fusion.110 = bf16[2,512,4,64]{1,3,2,0:T(8,128)(2,1)} fusion(bf16[2,512,4,64]{1,3,2,0:T(8,128)(2,1)} %get-tuple-element.349, s32[]{:T(128)S(6)} %copy.92, bf16[1024,4,64]{0,2,1:T(8,128)(2,1)} %get-tuple-element.365, pred[512,1024]{1,0:T(8,128)(4,1)} %fusion.109, bf16[1024,4,64]{0,2,1:T(8,128)(2,1)S(1)} %get-tuple-element.364, ...), kind=kOutput, calls=%fused_computation.12.clone.1 | convolution fusion | flops 553779200 | bytes 2097160 | tf_op jit(solution)/shard_map/while/body/eval_jaxpr/hqk,khd->qhd/dot_general | solution.py:75
  80.6 5.8 %fusion.110 = bf16[2,512,4,64]{1,3,2,0:T(8,128)(2,1)} fusion(bf16[2,512,4,64]{1,3,2,0:T(8,128)(2,1)} %get-tuple-element.349, s32[]{:T(128)S(6)} %copy.92, bf16[1024,4,64]{0,2,1:T(8,128)(2,1)} %get-tuple-element.365, pred[512,1024]{1,0:T(8,128)(4,1)} %fusion.109, bf16[1024,4,64]{0,2,1:T(8,128)(2,1)S(1)} %get-tuple-element.364, ...), kind=kOutput, calls=%fused_computation.12.clone.1 | convolution fusion | flops 553779200 | bytes 2097160 | tf_op jit(solution)/shard_map/while/body/eval_jaxpr/hqk,khd->qhd/dot_general | solution.py:75
  91.8 4.3 all-to-all-start.1
  99.6 10.6 %all-to-all-done.1 = bf16[1024,2,128]{2,1,0:T(2,128)(2,1)} async-done(((bf16[1024,2,128]{2,1,0:T(2,128)(2,1)}), bf16[1024,2,128]{2,1,0:T(2,128)(2,1)}, u32[]{:S(2)}, u32[]{:S(2)}) %all-to-all-start.1) | async-done | bytes 524320 | tf_op jit(solution)/shard_map/all_to_all | solution.py:81
  125.0 4.1 all-to-all-start.2
  132.0 11.2 %all-to-all-done.2 = bf16[256,8,128]{2,0,1:T(8,128)(2,1)} async-done(((bf16[256,8,128]{2,0,1:T(8,128)(2,1)}), bf16[256,8,128]{2,0,1:T(8,128)(2,1)}, u32[]{:S(2)}, u32[]{:S(2)}) %all-to-all-start.2) | async-done | bytes 524320 | tf_op jit(solution)/shard_map/all_to_all | solution.py:98
  145.8 42.4 %while.27 = (s32[]{:T(128)}, f32[1024,4,64]{0,2,1:T(8,128)}, f32[1024,4,64]{0,2,1:T(8,128)S(1)}, bf16[2,512,4,64]{1,3,2,0:T(8,128)(2,1)S(1)}, s32[2]{0:T(128)S(1...) while((s32[]{:T(128)}, f32[1024,4,64]{0,2,1:T(8,128)}, ...), condition=%wide.region_10.11_spmd.clone, body=%wide.region_9.10_spmd.clone.sunk | while | flops 1386873344 | bytes 84162888 | solution.py:124
  147.1 4.5 fusion.120
  152.3 7.5 %fusion.122 = f32[1024,4,64]{0,2,1:T(8,128)} fusion(f32[4,512,1024]{2,1,0:T(8,128)} %fusion.120, pred[512,1024]{1,0:T(8,128)(4,1)S(1)} %fusion.121, f32[1024,4,64]{0,2,1:T(8,128)} %get-tuple-element.385, pred[]{:T(512)S(6)} %compare.3, bf16[1024,4,64]{0,2,1:T(8,128)(2,1)} %get-tuple-element.403, s32[]{:T(128)S(6)} %select_n.67), kind=kOutput, calls=%fused_computation.29.clone.1 | convolution fusion | flops 285736960 | bytes 11272197 | tf_op jit(solution)/shard_map/while/body/eval_jaxpr/hqk,qhd->khd/dot_general | solution.py:112
  159.8 4.7 select_convert_fusion.20
  168.2 4.5 fusion.120
  173.4 7.8 %fusion.122 = f32[1024,4,64]{0,2,1:T(8,128)} fusion(f32[4,512,1024]{2,1,0:T(8,128)} %fusion.120, pred[512,1024]{1,0:T(8,128)(4,1)S(1)} %fusion.121, f32[1024,4,64]{0,2,1:T(8,128)} %get-tuple-element.385, pred[]{:T(512)S(6)} %compare.3, bf16[1024,4,64]{0,2,1:T(8,128)(2,1)} %get-tuple-element.403, s32[]{:T(128)S(6)} %select_n.67), kind=kOutput, calls=%fused_computation.29.clone.1 | convolution fusion | flops 285736960 | bytes 11272197 | tf_op jit(solution)/shard_map/while/body/eval_jaxpr/hqk,qhd->khd/dot_general | solution.py:112
  181.2 4.7 select_convert_fusion.20
  192.0 4.3 copy.69
  196.3 39.1 %all_to_all.62 = bf16[1024,2,384]{2,1,0:T(2,128)(2,1)S(1)} all-to-all(bf16[1024,2,384]{2,1,0:T(2,128)(2,1)S(1)} %copy.69), channel_id=1, replica_groups=mesh['seq'=4,'dp'=8] {'seq'}, dimensions={0} | all-to-all | bytes 3145728 | tf_op jit(solution)/shard_map/all_to_all | solution.py:135
  235.9 4.1 copy.71
  240.0 5.5 %reshape.292 = f32[256,3072]{1,0:T(8,128)} reshape(f32[256,4,2,384]{3,2,1,0:T(2,128)} %copy.71) | data formatting | bytes 6291456 | tf_op jit(solution)/shard_map/convert_element_type | solution.py:142
  245.5 4.0 multiply_convert_fusion
  249.5 6.4 %convolution_bitcast_fusion.1 = f32[1024,3072]{0,1:T(8,128)} fusion(bf16[256,3072]{1,0:T(8,128)(2,1)S(1)} %multiply_convert_fusion, bf16[256,1024]{1,0:T(8,128)(2,1)S(1)} %copy-done.8), kind=kOutput, calls=%fused_computation.47 | convolution fusion | flops 1610612736 | bytes 14680064 | tf_op jit(solution)/shard_map/dot_general | solution.py:149
  261.7 85.9 %reduce-scatter.7.cloned.1.call-done = f32[128,3072]{0,1:T(8,128)} async-done(((f32[1024,3072]{0,1:T(8,128)}), f32[128,3072]{0,1:T(8,128)}) %reduce-scatter.7.cloned.1.call-update) | async-done | bytes 1572880 | tf_op jit(solution)/shard_map/reduce_scatter | solution.py:154
  350.2 4.8 all-to-all-start.4
  355.1 5.6 %fusion.63 = f32[256,1024]{1,0:T(8,128)S(1)} fusion(bf16[256,3072]{1,0:T(8,128)(2,1)} %copy-done.6, bf16[1024,3072]{1,0:T(8,128)(2,1)} %param.19), kind=kOutput, calls=%fused_computation.109 | convolution fusion | flops 1610612736 | bytes 8912896 | tf_op jit(solution)/shard_map/dot_general | solution.py:145
  364.6 6.1 %all-to-all-start.5 = ((bf16[32,16,1024]{2,1,0:T(8,128)(2,1)}), bf16[32,16,1024]{2,1,0:T(8,128)(2,1)S(1)}, u32[]{:S(2)}, u32[]{:S(2)}) async-start(bf16[32,16,1024]{2,1,0:T(8,128)(2,1)} %bitcast.25), calls=%async_computation.11 | async-start | bytes 2097152 | tf_op jit(solution)/shard_map/all_to_all | solution.py:175
  370.7 40.9 %reduce-scatter.15.cloned.1.call-done = f32[128,1024]{1,0:T(8,128)} async-done(((f32[1024,1024]{1,0:T(8,128)}), f32[128,1024]{1,0:T(8,128)}) %reduce-scatter.15.cloned.1.call-update) | async-done | bytes 524304 | tf_op jit(solution)/shard_map/reduce_scatter | solution.py:156
  412.9 5.3 %scatter_custom_fusion.2 = f32[512,1024]{1,0:T(8,128)S(1)} fusion(s32[512]{0:T(512)S(1)} %bitcast.153, bf16[512,1024]{1,0:T(8,128)(2,1)S(1)} %bitcast.148, f32[]{:T(128)} %constant.80.clone.1), kind=kCustom, calls=%fused_computation.53 | custom fusion | flops 1048576 | bytes 3145732 | tf_op jit(solution)/shard_map/scatter-add | solution.py:192
  424.4 11.0 %reduce-scatter.13.cloned.1.call-done = f32[128,256]{0,1:T(8,128)} async-done(((f32[128,1024]{0,1:T(8,128)}), f32[128,256]{0,1:T(8,128)}) %reduce-scatter.13.cloned.1.call-update) | async-done | bytes 131088 | tf_op jit(solution)/shard_map/reduce_scatter | solution.py:160
  437.0 34.0 %reduce-scatter.9.cloned.1.call-done = f32[128,768]{0,1:T(8,128)} async-done(((f32[128,3072]{0,1:T(8,128)}), f32[128,768]{0,1:T(8,128)}) %reduce-scatter.9.cloned.1.call-update) | async-done | bytes 393232 | tf_op jit(solution)/shard_map/reduce_scatter | solution.py:159
  473.0 21.4 %reduce-scatter.17.cloned.1.call-done = f32[128,256]{1,0:T(8,128)} async-done(((f32[128,1024]{1,0:T(8,128)}), f32[128,256]{1,0:T(8,128)}) %reduce-scatter.17.cloned.1.call-update) | async-done | bytes 131088 | tf_op jit(solution)/shard_map/reduce_scatter | solution.py:161
  (153 shorter events, 80.1 us)
Async XLA Ops:
  7.2 112.8 %copy-start = (bf16[1024,1024]{1,0:T(8,128)(2,1)S(1)}, bf16[1024,1024]{1,0:T(8,128)(2,1)}, u32[]{:S(2)}) copy-start(bf16[1024,1024]{1,0:T(8,128)(2,1)} %param.21) | copy-start | bytes 6291460
  13.9 7.6 %copy-start.25 = (s32[1,3]{1,0:T(1,128)S(1)}, s32[1,3]{1,0:T(1,128)}, u32[]{:S(2)}) copy-start(s32[1,3]{1,0:T(1,128)} %param.16) | copy-start | bytes 40
  15.2 43.4 %all-to-all-start = ((bf16[256,8,384]{2,0,1:T(8,128)(2,1)}), bf16[256,8,384]{2,0,1:T(8,128)(2,1)}, u32[]{:S(2)}, u32[]{:S(2)}) async-start(bf16[256,8,384]{2,0,1:T(8,128)(2,1)} %bitcast.145), calls=%async_computation | async-start | bytes 3145728 | tf_op jit(solution)/shard_map/all_to_all | solution.py:51
  91.8 18.4 %all-to-all-start.1 = ((bf16[1024,2,128]{2,1,0:T(2,128)(2,1)}), bf16[1024,2,128]{2,1,0:T(2,128)(2,1)}, u32[]{:S(2)}, u32[]{:S(2)}) async-start(bf16[1024,2,128]{2,1,0:T(2,128)(2,1)} %reshape.321), calls=%async_computation.1 | async-start | bytes 1048576 | tf_op jit(solution)/shard_map/all_to_all | solution.py:81
  118.5 5.3 %copy-start.19 = (f32[256]{0:T(256)}, f32[256]{0:T(256)S(1)}, u32[]{:S(2)}) copy-start(f32[256]{0:T(256)S(1)} %broadcast_multiply_fusion.2) | copy-start | bytes 3076
  120.0 3.8 copy-start.22
  120.0 3.8 copy-start.9
  123.8 5.4 %copy-start.7 = (bf16[256,1024]{1,0:T(8,128)(2,1)S(1)}, bf16[256,1024]{1,0:T(8,128)(2,1)}, u32[]{:S(2)}) copy-start(bf16[256,1024]{1,0:T(8,128)(2,1)} %param.14) | copy-start | bytes 1572868
  123.8 5.4 %copy-start.11 = (bf16[256,1024]{1,0:T(8,128)(2,1)S(1)}, bf16[256,1024]{1,0:T(8,128)(2,1)}, u32[]{:S(2)}) copy-start(bf16[256,1024]{1,0:T(8,128)(2,1)} %get-tuple-element.225) | copy-start | bytes 1572868
  125.0 18.2 %all-to-all-start.2 = ((bf16[256,8,128]{2,0,1:T(8,128)(2,1)}), bf16[256,8,128]{2,0,1:T(8,128)(2,1)}, u32[]{:S(2)}, u32[]{:S(2)}) async-start(bf16[256,8,128]{2,0,1:T(8,128)(2,1)} %copy_bitcast_fusion.1), calls=%async_computation.2 | async-start | bytes 1048576 | tf_op jit(solution)/shard_map/all_to_all | solution.py:98
  129.1 131.4 %reduce-scatter.11.cloned.1.call-start = ((), (), s32[]{:S(2)}) async-start(), calls=%async_computation.14 | async-start | bytes 4718592 | tf_op jit(solution)/shard_map/reduce_scatter | solution.py:155
  132.0 215.7 %reduce-scatter.7.cloned.1.call-start = ((), (), s32[]{:S(2)}) async-start(), calls=%async_computation.12 | async-start | bytes 14155776 | tf_op jit(solution)/shard_map/reduce_scatter | solution.py:154
  152.3 7.6 %copy-start.2 = (f32[4,512,1024]{2,1,0:T(8,128)S(1)}, f32[4,512,1024]{2,1,0:T(8,128)}, u32[]{:S(2)}) copy-start(f32[4,512,1024]{2,1,0:T(8,128)} %fusion.120) | copy-start | bytes 25165828 | tf_op jit(solution)/shard_map/while
  152.3 7.5 %copy-start.17 = (bf16[1024,4,64]{0,2,1:T(8,128)(2,1)S(1)}, bf16[1024,4,64]{0,2,1:T(8,128)(2,1)}, u32[]{:S(2)}) copy-start(bf16[1024,4,64]{0,2,1:T(8,128)(2,1)} %get-tuple-element.403) | copy-start | bytes 1572868 | tf_op jit(solution)/shard_map/while
  152.3 7.5 %copy-start.18 = (bf16[1024,4,64]{0,2,1:T(8,128)(2,1)S(1)}, bf16[1024,4,64]{0,2,1:T(8,128)(2,1)}, u32[]{:S(2)}) copy-start(bf16[1024,4,64]{0,2,1:T(8,128)(2,1)} %get-tuple-element.407) | copy-start | bytes 1572868 | tf_op jit(solution)/shard_map/while
  173.4 7.8 %copy-start.2 = (f32[4,512,1024]{2,1,0:T(8,128)S(1)}, f32[4,512,1024]{2,1,0:T(8,128)}, u32[]{:S(2)}) copy-start(f32[4,512,1024]{2,1,0:T(8,128)} %fusion.120) | copy-start | bytes 25165828 | tf_op jit(solution)/shard_map/while
  173.4 7.8 %copy-start.17 = (bf16[1024,4,64]{0,2,1:T(8,128)(2,1)S(1)}, bf16[1024,4,64]{0,2,1:T(8,128)(2,1)}, u32[]{:S(2)}) copy-start(bf16[1024,4,64]{0,2,1:T(8,128)(2,1)} %get-tuple-element.403) | copy-start | bytes 1572868 | tf_op jit(solution)/shard_map/while
  173.4 7.8 %copy-start.18 = (bf16[1024,4,64]{0,2,1:T(8,128)(2,1)S(1)}, bf16[1024,4,64]{0,2,1:T(8,128)(2,1)}, u32[]{:S(2)}) copy-start(bf16[1024,4,64]{0,2,1:T(8,128)(2,1)} %get-tuple-element.407) | copy-start | bytes 1572868 | tf_op jit(solution)/shard_map/while
  245.5 4.0 copy-start.8
  249.5 6.4 %copy-start.6 = (bf16[256,3072]{1,0:T(8,128)(2,1)}, bf16[256,3072]{1,0:T(8,128)(2,1)S(1)}, u32[]{:S(2)}) copy-start(bf16[256,3072]{1,0:T(8,128)(2,1)S(1)} %multiply_convert_fusion) | copy-start | bytes 4718596
  255.9 1.7 copy-start.15
  256.0 155.6 %reduce-scatter.15.cloned.1.call-start = ((), (), s32[]{:S(2)}) async-start(), calls=%async_computation.16 | async-start | bytes 4718592 | tf_op jit(solution)/shard_map/reduce_scatter | solution.py:156
  260.5 174.9 %reduce-scatter.13.cloned.1.call-start = ((), (), s32[]{:S(2)}) async-start(), calls=%async_computation.15 | async-start | bytes 655360 | tf_op jit(solution)/shard_map/reduce_scatter | solution.py:160
  261.1 210.0 %reduce-scatter.9.cloned.1.call-start = ((), (), s32[]{:S(2)}) async-start(), calls=%async_computation.13 | async-start | bytes 1966080 | tf_op jit(solution)/shard_map/reduce_scatter | solution.py:159
  350.2 14.4 %all-to-all-start.4 = ((s32[32,1,16]{2,1,0:T(1,128)}), s32[32,1,16]{2,1,0:T(1,128)S(1)}, u32[]{:S(2)}, u32[]{:S(2)}) async-start(s32[32,1,16]{2,1,0:T(1,128)} %bitcast.23), calls=%async_computation.10 | async-start | bytes 32768 | tf_op jit(solution)/shard_map/all_to_all | solution.py:182
  355.1 5.7 %copy-start.5 = (bf16[1024,1024]{1,0:T(8,128)(2,1)S(1)}, bf16[1024,1024]{1,0:T(8,128)(2,1)}, u32[]{:S(2)}) copy-start(bf16[1024,1024]{1,0:T(8,128)(2,1)} %param.20) | copy-start | bytes 6291460
  355.1 5.7 %copy-start.12 = (bf16[256,1024]{1,0:T(8,128)(2,1)S(1)}, bf16[256,1024]{1,0:T(8,128)(2,1)}, u32[]{:S(2)}) copy-start(bf16[256,1024]{1,0:T(8,128)(2,1)} %get-tuple-element.225) | copy-start | bytes 1572868
  355.1 5.7 %copy-start.16 = (bf16[256,1024]{1,0:T(8,128)(2,1)S(1)}, bf16[256,1024]{1,0:T(8,128)(2,1)}, u32[]{:S(2)}) copy-start(bf16[256,1024]{1,0:T(8,128)(2,1)} %param.15) | copy-start | bytes 1572868
  364.6 48.3 %all-to-all-start.5 = ((bf16[32,16,1024]{2,1,0:T(8,128)(2,1)}), bf16[32,16,1024]{2,1,0:T(8,128)(2,1)S(1)}, u32[]{:S(2)}, u32[]{:S(2)}) async-start(bf16[32,16,1024]{2,1,0:T(8,128)(2,1)} %bitcast.25), calls=%async_computation.11 | async-start | bytes 2097152 | tf_op jit(solution)/shard_map/all_to_all | solution.py:175
  370.7 49.1 %copy-start.24 = (f32[512]{0:T(512)S(1)}, f32[512]{0:T(512)}, u32[]{:S(2)}) copy-start(f32[512]{0:T(512)} %param.23) | copy-start | bytes 6148
  370.7 123.7 %reduce-scatter.17.cloned.1.call-start = ((), (), s32[]{:S(2)}) async-start(), calls=%async_computation.17 | async-start | bytes 655360 | tf_op jit(solution)/shard_map/reduce_scatter | solution.py:161
  420.4 74.1 %copy-start.1 = (bf16[1024,1024]{1,0:T(8,128)(2,1)S(1)}, bf16[1024,1024]{1,0:T(8,128)(2,1)}, u32[]{:S(2)}) copy-start(bf16[1024,1024]{1,0:T(8,128)(2,1)} %param.21) | copy-start | bytes 6291460
  (8 other events, 10.7 us)
Sparse Core Ops, SparseCore 0:
  133.3 52.7 reduce-scatter.10
  256.1 91.4 reduce-scatter.6
  351.4 60.1 reduce-scatter.14
  413.7 21.6 reduce-scatter.12
  437.5 33.4 reduce-scatter.8
  473.8 20.6 reduce-scatter.16
where the time goes:
time: 509 us; the launch traced here: 502 us
  waiting for transfers between devices  252 us (50%)
  matrix products  82.5 us (16%)
  local copies, waits for them, and re-layouts  57.2 us (11%)
  blocking collectives  39.1 us (8%)
  other arithmetic  26.9 us (5%)
  starting transfers between devices  25.9 us (5%)
  between operations  15 us (3%)
    reduce_scatter x1, waiting for transfers between devices, body(): lax.psum_scatter(partials[0], 'dp', scatter_dimension=0, tiled=True)  85.9 us
    reduce_scatter x1, waiting for transfers between devices, body(): lax.psum_scatter(partials[2], 'dp', scatter_dimension=0, tiled=True)  40.9 us
    all_to_all x1, blocking collectives, body(): lax.all_to_all(head_grads.reshape(positions, head_local // 2, 6 * DH), 's...  39.1 us
    all_to_all x1, waiting for transfers between devices, body(): lax.all_to_all(acts, 'seq', split_axis=1, concat_axis=0, tiled=True)  36.8 us
    reduce_scatter x1, waiting for transfers between devices, body(): lax.psum_scatter(partials[0], 'seq', scatter_dimension=1, tiled=True)  34 us
    reduce_scatter x1, waiting for transfers between devices, body(): lax.psum_scatter(partials[2], 'seq', scatter_dimension=1, tiled=True)  21.4 us
    dot_general x2, matrix products, backward_block(): jnp.einsum('hqk,qhd->khd', weights, grad_block, preferred_element_type=jn...  15.3 us
    dot_general x2, matrix products, forward_block(): jnp.einsum('hqk,khd->qhd', weights, values, preferred_element_type=jnp.fl...  11.7 us
  transfers between devices with their start and end apart: 11, of which 8 were waited for; matrix products, arithmetic and copies ran while one was open for 21% of the time, Pallas kernels for 0%

commit v1 on v0

v1 whole, which is shorter than its diff:
```python
import functools

import jax
import jax.numpy as jnp
from jax import lax
from jax.experimental import pallas as pl
from jax.experimental.pallas import tpu as pltpu
from jax.sharding import PartitionSpec as P

D = 1024
H = 16
DH = 64
PAIR = 2 * DH

NORM_EPS = 1e-05
LEARN_RATE = 0.1
VMEM_LIMIT = 56 * 1024 * 1024
BF = jnp.bfloat16
F32 = jnp.float32


def dot_nn(a, b):
    return lax.dot_general(a, b, (((1,), (0,)), ((), ())), preferred_element_type=F32)


def dot_nt(a, b):
    return lax.dot_general(a, b, (((1,), (1,)), ((), ())), preferred_element_type=F32)


def history_start(lengths_ref, users, place):
    start = jnp.zeros_like(place)
    end = jnp.int32(0)
    for user in range(users - 1):
        end = end + lengths_ref[0, user]
        start = jnp.where(place >= end, end, start)
    return start


def block_needed(lengths_ref, users, i, j, blk):
    return (j + 1) * blk > history_start(lengths_ref, users, i * blk)


def forward_kernel(
    lengths_ref, x_ref, w_ref, acts_ref, dact_ref, weights_ref, slope_ref, heads_ref, q_half, *, blk, users, maxlen
):
    i = pl.program_id(1)
    positions = x_ref.shape[0]
    blocks = positions // blk

    @pl.when(i == 0)
    def _():
        def rows(r, _):
            at = pl.ds(pl.multiple_of(r * blk, blk), blk)
            pre = dot_nn(x_ref[at, :], w_ref[...])
            half = 0.5 * pre
            t = jnp.tanh(half)
            p = half * t
            acts = (half + p).astype(BF)
            acts_ref[at, :] = acts
            dact_ref[at, :] = (0.5 * (1.0 + t) * (1.0 + half - p)).astype(BF)
            q_half[at, :] = acts[:, PAIR : 2 * PAIR] * jnp.asarray(0.5 * DH**-0.5, BF)
            return 0

        lax.fori_loop(0, blocks, rows, 0)

    at_i = pl.ds(pl.multiple_of(i * blk, blk), blk)
    q_i = q_half[at_i, :]
    row = i * blk + lax.broadcasted_iota(jnp.int32, (blk, blk), 0)
    col0 = lax.broadcasted_iota(jnp.int32, (blk, blk), 1)
    start = history_start(lengths_ref, users, row)

    def column(j, acc):
        at_j = pl.ds(pl.multiple_of(j * blk, blk), blk)
        col = col0 + j * blk
        allowed = (col <= row) & (col >= start)
        outs = []
        for h in range(2):
            lanes = slice(h * DH, (h + 1) * DH)
            k_j = acts_ref[at_j, 2 * PAIR + h * DH : 2 * PAIR + (h + 1) * DH]
            v_j = acts_ref[at_j, h * DH : (h + 1) * DH]
            half = dot_nt(q_i[:, lanes], k_j)
            half = jnp.where(allowed, half, -64.0)
            t = jnp.tanh(half)
            p = half * t
            weights = (half + p).astype(BF)
            slope = ((1.0 + t) * (1.0 + half - p)).astype(BF)
            weights_ref[h, :, at_j] = weights
            slope_ref[h, :, at_j] = slope
            outs.append(acc[h] + dot_nn(weights, v_j))
        return tuple(outs)

    first = history_start(lengths_ref, users, i * blk) // blk
    zero = jnp.zeros((blk, DH), F32)
    acc = lax.fori_loop(first, i + 1, column, (zero, zero))
    heads_ref[...] = (jnp.concatenate(acc, axis=1) * (1.0 / maxlen)).astype(BF)


def forward_attention(lengths, x_full, w_pairs, blk, maxlen):
    positions = x_full.shape[0]
    pairs = w_pairs.shape[1] // (3 * PAIR)
    users = lengths.shape[1]
    blocks = positions // blk
    elements = 2 * pairs * positions * positions // 2
    return pl.pallas_call(
        functools.partial(forward_kernel, blk=blk, users=users, maxlen=maxlen),
        grid=(pairs, blocks),
        in_specs=[
            pl.BlockSpec(memory_space=pltpu.SMEM),
            pl.BlockSpec((positions, D), lambda p, i: (0, 0)),
            pl.BlockSpec((D, 3 * PAIR), lambda p, i: (0, p)),
        ],
        out_specs=[
            pl.BlockSpec((positions, 3 * PAIR), lambda p, i: (0, p)),
            pl.BlockSpec((positions, 3 * PAIR), lambda p, i: (0, p)),
            pl.BlockSpec((2, blk, positions), lambda p, i: (p, i, 0)),
            pl.BlockSpec((2, blk, positions), lambda p, i: (p, i, 0)),
            pl.BlockSpec((blk, PAIR), lambda p, i: (i, p)),
        ],
        out_shape=[
            jax.ShapeDtypeStruct((positions, pairs * 3 * PAIR), BF),
            jax.ShapeDtypeStruct((positions, pairs * 3 * PAIR), BF),
            jax.ShapeDtypeStruct((2 * pairs, positions, positions), BF),
            jax.ShapeDtypeStruct((2 * pairs, positions, positions), BF),
            jax.ShapeDtypeStruct((positions, pairs * PAIR), BF),
        ],
        scratch_shapes=[pltpu.VMEM((positions, PAIR), BF)],
        compiler_params=pltpu.CompilerParams(vmem_limit_bytes=VMEM_LIMIT),
        cost_estimate=pl.CostEstimate(
            flops=2 * positions * D * pairs * 3 * PAIR + 4 * elements * 256,
            bytes_accessed=4 * positions * D + 4 * elements,
            transcendentals=elements,
        ),
        name="attention_forward",
    )(lengths, x_full, w_pairs)


def gate_kernel(x_ref, og_ref, wg_ref, wo_ref, heads_ref, gate_ref, ng_ref, u_ref, stats_ref):
    gate_pre = dot_nn(x_ref[...], wg_ref[...])
    mixed_grad = dot_nt(og_ref[...], wo_ref[...])
    half = 0.5 * gate_pre
    t = jnp.tanh(half)
    p = half * t
    gate = half + p
    gate_ref[...] = gate
    ng = mixed_grad * gate
    ng_ref[...] = ng
    u_ref[...] = mixed_grad * (0.5 * (1.0 + t) * (1.0 + half - p))
    heads = heads_ref[...].astype(F32)
    mean = jnp.mean(heads, axis=1, keepdims=True)
    centred = heads - mean
    square = jnp.sum(centred * centred, axis=1, keepdims=True)
    total = jnp.sum(ng, axis=1, keepdims=True)
    cross = jnp.sum(ng * centred, axis=1, keepdims=True)
    lane = lax.broadcasted_iota(jnp.int32, (heads.shape[0], 128), 1)
    packed = jnp.where(lane == 0, mean, jnp.where(lane == 1, square, jnp.where(lane == 2, total, cross)))
    stats_ref[...] = jnp.transpose(packed)[:8, :]


def gate_stats(x_full, og_full, w_gate_own, w_out_own, heads, blk):
    positions = x_full.shape[0]
    cols = heads.shape[1]
    return pl.pallas_call(
        gate_kernel,
        grid=(positions // blk,),
        in_specs=[
            pl.BlockSpec((blk, D), lambda i: (i, 0)),
            pl.BlockSpec((blk, D), lambda i: (i, 0)),
            pl.BlockSpec((D, cols), lambda i: (0, 0)),
            pl.BlockSpec((cols, D), lambda i: (0, 0)),
            pl.BlockSpec((blk, cols), lambda i: (i, 0)),
        ],
        out_specs=[
            pl.BlockSpec((blk, cols), lambda i: (i, 0)),
            pl.BlockSpec((blk, cols), lambda i: (i, 0)),
            pl.BlockSpec((blk, cols), lambda i: (i, 0)),
            pl.BlockSpec((8, blk), lambda i: (0, i)),
        ],
        out_shape=[
            jax.ShapeDtypeStruct((positions, cols), F32),
            jax.ShapeDtypeStruct((positions, cols), F32),
            jax.ShapeDtypeStruct((positions, cols), F32),
            jax.ShapeDtypeStruct((8, positions), F32),
        ],
        compiler_params=pltpu.CompilerParams(vmem_limit_bytes=VMEM_LIMIT),
        cost_estimate=pl.CostEstimate(
            flops=4 * positions * D * cols, bytes_accessed=4 * positions * D, transcendentals=positions * cols
        ),
        name="gate_and_stats",
    )(x_full, og_full, w_gate_own, w_out_own, heads)


def backward_kernel(
    lengths_ref,
    stats_ref,
    heads_ref,
    gate_ref,
    ng_ref,
    u_ref,
    acts_ref,
    dact_ref,
    weights_ref,
    slope_ref,
    grad_ref,
    gate_grad_ref,
    mixed_ref,
    o_ref,
    o_t,
    q_t,
    vg_t,
    kg_t,
    qg,
    *,
    blk,
    users,
    maxlen,
    shards,
    cols,
):
    i = pl.program_id(1)
    positions = heads_ref.shape[0]
    blocks = positions // blk
    scale = DH ** (-0.5)

    @pl.when(i == 0)
    def _():
        means = [stats_ref[8 * s : 8 * s + 1, :] for s in range(shards)]
        mean = sum(means) * (1.0 / shards)
        square = jnp.zeros_like(mean)
        total = jnp.zeros_like(mean)
        cross = jnp.zeros_like(mean)
        for s in range(shards):
            shift = means[s] - mean
            part = stats_ref[8 * s + 2 : 8 * s + 3, :]
            square = square + stats_ref[8 * s + 1 : 8 * s + 2, :] + cols * shift * shift
            total = total + part
            cross = cross + stats_ref[8 * s + 3 : 8 * s + 4, :] + shift * part
        inv_dev = lax.rsqrt(square * (1.0 / D) + NORM_EPS)
        row8 = lax.broadcasted_iota(jnp.int32, (128, positions), 0)
        packed = jnp.where(
            row8 == 0,
            mean,
            jnp.where(row8 == 1, inv_dev, jnp.where(row8 == 2, total * (1.0 / D), cross * inv_dev * (1.0 / D))),
        )
        per_event = jnp.transpose(packed)
        mean_c = per_event[:, 0:1]
        inv_c = per_event[:, 1:2]
        total_c = per_event[:, 2:3]
        cross_c = per_event[:, 3:4]
        normed = (heads_ref[...].astype(F32) - mean_c) * inv_c
        mixed_ref[...] = (normed * gate_ref[...]).astype(BF)
        gate_grad_ref[...] = (u_ref[...] * normed).astype(BF)
        o = (inv_c * (ng_ref[...] - total_c - normed * cross_c)).astype(BF)
        o_ref[...] = o
        o_t[...] = jnp.transpose(o)
        q_t[...] = jnp.transpose(acts_ref[:, PAIR : 2 * PAIR])
        vg_t[...] = jnp.zeros_like(vg_t)
        kg_t[...] = jnp.zeros_like(kg_t)

    at_i = pl.ds(pl.multiple_of(i * blk, blk), blk)

    def column(j, acc):
        at_j = pl.ds(pl.multiple_of(j * blk, blk), blk)
        outs = []
        for h in range(2):
            lanes = slice(h * DH, (h + 1) * DH)
            k_j = acts_ref[at_j, 2 * PAIR + h * DH : 2 * PAIR + (h + 1) * DH]
            v_j = acts_ref[at_j, h * DH : (h + 1) * DH]
            weight_grad = dot_nt(o_ref[at_i, lanes], v_j)
            score_grad = (weight_grad * slope_ref[h, :, at_j].astype(F32)).astype(BF)
            vg_t[lanes, at_j] += dot_nn(o_t[lanes, at_i], weights_ref[h, :, at_j])
            kg_t[lanes, at_j] += dot_nn(q_t[lanes, at_i], score_grad)
            outs.append(acc[h] + dot_nn(score_grad, k_j))
        return tuple(outs)

    first = history_start(lengths_ref, users, i * blk) // blk
    zero = jnp.zeros((blk, DH), F32)
    acc = lax.fori_loop(first, i + 1, column, (zero, zero))
    qg[at_i, :] = jnp.concatenate(acc, axis=1)

    @pl.when(i == blocks - 1)
    def _():
        factor = 0.5 * scale / maxlen
        v_grad = (jnp.transpose(vg_t[...]) * (1.0 / maxlen)).astype(BF).astype(F32)
        q_grad = (qg[...] * factor).astype(BF).astype(F32)
        k_grad = (jnp.transpose(kg_t[...]) * factor).astype(BF).astype(F32)
        grad_ref[:, :PAIR] = (v_grad * dact_ref[:, :PAIR].astype(F32)).astype(BF)
        grad_ref[:, PAIR : 2 * PAIR] = (q_grad * dact_ref[:, PAIR : 2 * PAIR].astype(F32)).astype(BF)
        grad_ref[:, 2 * PAIR :] = (k_grad * dact_ref[:, 2 * PAIR :].astype(F32)).astype(BF)


def backward_attention(lengths, stats, heads, gate, ng, u, acts, dact, weights, slope, blk, maxlen, shards):
    positions, cols = heads.shape
    pairs = cols // PAIR
    users = lengths.shape[1]
    elements = 2 * pairs * positions * positions // 2
    whole = lambda p, i: (0, p)
    return pl.pallas_call(
        functools.partial(backward_kernel, blk=blk, users=users, maxlen=maxlen, shards=shards, cols=cols),
        grid=(pairs, positions // blk),
        in_specs=[
            pl.BlockSpec(memory_space=pltpu.SMEM),
            pl.BlockSpec((8 * shards, positions), lambda p, i: (0, 0)),
            pl.BlockSpec((positions, PAIR), whole),
            pl.BlockSpec((positions, PAIR), whole),
            pl.BlockSpec((positions, PAIR), whole),
            pl.BlockSpec((positions, PAIR), whole),
            pl.BlockSpec((positions, 3 * PAIR), whole),
            pl.BlockSpec((positions, 3 * PAIR), whole),
            pl.BlockSpec((2, blk, positions), lambda p, i: (p, i, 0)),
            pl.BlockSpec((2, blk, positions), lambda p, i: (p, i, 0)),
        ],
        out_specs=[
            pl.BlockSpec((positions, 3 * PAIR), whole),
            pl.BlockSpec((positions, PAIR), whole),
            pl.BlockSpec((positions, PAIR), whole),
        ],
        out_shape=[
            jax.ShapeDtypeStruct((positions, pairs * 3 * PAIR), BF),
            jax.ShapeDtypeStruct((positions, cols), BF),
            jax.ShapeDtypeStruct((positions, cols), BF),
        ],
        scratch_shapes=[
            pltpu.VMEM((positions, PAIR), BF),
            pltpu.VMEM((PAIR, positions), BF),
            pltpu.VMEM((PAIR, positions), BF),
            pltpu.VMEM((PAIR, positions), F32),
            pltpu.VMEM((PAIR, positions), F32),
            pltpu.VMEM((positions, PAIR), F32),
        ],
        compiler_params=pltpu.CompilerParams(vmem_limit_bytes=VMEM_LIMIT),
        cost_estimate=pl.CostEstimate(
            flops=8 * elements * 256, bytes_accessed=4 * elements + 20 * positions * cols, transcendentals=0
        ),
        name="attention_backward",
    )(lengths, stats, heads, gate, ng, u, acts, dact, weights, slope)


def update_kernel(ids_ref, rows_ref, table_ref, accum_ref, new_table_ref, new_accum_ref):
    i = pl.program_id(0)
    blk = table_ref.shape[0]
    slots = rows_ref.shape[0]
    row = i * blk + lax.broadcasted_iota(jnp.int32, (blk, slots), 0)
    hits = jnp.where(row == ids_ref[...], 1.0, 0.0).astype(BF)
    grad = dot_nn(hits, rows_ref[...])
    accum = accum_ref[...] + jnp.mean(grad * grad, axis=1, keepdims=True)
    new_accum_ref[...] = accum
    new_table_ref[...] = table_ref[...] - LEARN_RATE * grad * lax.rsqrt(accum)


def update_rows(got_ids, got_rows, emb_table, row_accum):
    rows_own = emb_table.shape[0]
    slots = got_rows.shape[0]
    blk = min(128, rows_own)
    new_table, new_accum = pl.pallas_call(
        update_kernel,
        grid=(rows_own // blk,),
        in_specs=[
            pl.BlockSpec((1, slots), lambda i: (0, 0)),
            pl.BlockSpec((slots, D), lambda i: (0, 0)),
            pl.BlockSpec((blk, D), lambda i: (i, 0)),
            pl.BlockSpec((blk, 1), lambda i: (i, 0)),
        ],
        out_specs=[
            pl.BlockSpec((blk, D), lambda i: (i, 0)),
            pl.BlockSpec((blk, 1), lambda i: (i, 0)),
        ],
        out_shape=[
            jax.ShapeDtypeStruct((rows_own, D), F32),
            jax.ShapeDtypeStruct((rows_own, 1), F32),
        ],
        compiler_params=pltpu.CompilerParams(vmem_limit_bytes=VMEM_LIMIT),
        cost_estimate=pl.CostEstimate(
            flops=2 * rows_own * slots * D, bytes_accessed=8 * rows_own * D + 2 * slots * D, transcendentals=rows_own
        ),
        name="update_rows",
    )(got_ids.reshape(1, slots), got_rows, emb_table, row_accum[:, None])
    return new_table, new_accum[:, 0]


def body(
    layer_input,
    out_grad,
    lengths,
    item_owner,
    item_row,
    w_attn,
    w_gate,
    w_out,
    emb_table,
    row_accum,
):
    seq_count = lax.axis_size("seq")
    dp_count = lax.axis_size("dp")
    devices = seq_count * dp_count
    seq_id = lax.axis_index("seq")
    tokens_dev = layer_input.shape[0]
    positions = tokens_dev * seq_count
    maxlen = 2 * positions // 3
    blk = min(256, positions)
    cols = D // seq_count
    pairs = cols // PAIR

    w_attn_own = lax.dynamic_slice_in_dim(w_attn, seq_id * 3 * cols, 3 * cols, 1)
    w_attn_own = w_attn_own.reshape(D, pairs, 2, 3, DH).transpose(0, 1, 3, 2, 4).reshape(D, 3 * cols)
    w_gate_own = lax.dynamic_slice_in_dim(w_gate, seq_id * cols, cols, 1)
    w_out_own = lax.dynamic_slice_in_dim(w_out, seq_id * cols, cols, 0)

    rows_own = emb_table.shape[0]
    capacity = max(2, 2 * tokens_dev // devices)
    owners = item_owner[:, 0]
    owner_hits = (owners[:, None] == jnp.arange(devices, dtype=jnp.int32)[None, :]).astype(F32)
    before = (
        jnp.arange(tokens_dev, dtype=jnp.int32)[:, None] > jnp.arange(tokens_dev, dtype=jnp.int32)[None, :]
    ).astype(F32)
    slots = jnp.sum(jnp.dot(before, owner_hits) * owner_hits, axis=1).astype(jnp.int32)
    flat_slot = owners * capacity + slots
    slot_hits = jnp.arange(devices * capacity, dtype=jnp.int32)[:, None] == flat_slot[None, :]
    send_ids = jnp.min(jnp.where(slot_hits, item_row[None, :], rows_own), axis=1).astype(jnp.int32)
    got_ids = lax.all_to_all(
        send_ids.reshape(devices, capacity), ("seq", "dp"), split_axis=0, concat_axis=0, tiled=True
    ).reshape(devices * capacity)
    slot_matrix = slot_hits.astype(BF)

    x_full = lax.all_gather(layer_input, "seq", axis=0, tiled=True)
    og_full = lax.all_gather(out_grad, "seq", axis=0, tiled=True)

    acts, dact, weights, slope, heads = forward_attention(lengths, x_full, w_attn_own, blk, maxlen)
    gate, ng, u, stats_own = gate_stats(x_full, og_full, w_gate_own, w_out_own, heads, blk)
    stats = lax.all_gather(stats_own, "seq", axis=0, tiled=True)
    attn_grad, gate_grad, mixed = backward_attention(
        lengths, stats, heads, gate, ng, u, acts, dact, weights, slope, blk, maxlen, seq_count
    )

    input_part = (dot_nt(attn_grad, w_attn_own) + dot_nt(gate_grad, w_gate_own)).astype(BF)
    got = lax.all_to_all(
        input_part.reshape(seq_count, tokens_dev, D), "seq", split_axis=0, concat_axis=0, tiled=True
    )
    input_grad = jnp.sum(got.astype(F32), axis=0) + out_grad.astype(F32)
    send_rows = jnp.dot(slot_matrix, input_grad.astype(BF), preferred_element_type=F32).astype(BF)
    got_rows = lax.all_to_all(
        send_rows.reshape(devices, capacity, D), ("seq", "dp"), split_axis=0, concat_axis=0, tiled=True
    ).reshape(devices * capacity, D)
    new_table, new_accum = update_rows(got_ids, got_rows, emb_table, row_accum)

    tn = (((0,), (0,)), ((), ()))
    attn_part = lax.dot_general(x_full, attn_grad, tn, preferred_element_type=F32).astype(BF)
    gate_part = lax.dot_general(x_full, gate_grad, tn, preferred_element_type=F32).astype(BF)
    out_part = lax.dot_general(mixed, og_full, tn, preferred_element_type=F32).astype(BF)
    share = dp_count // seq_count
    out_part = (
        out_part.reshape(share, D // dp_count, seq_count, cols).transpose(0, 2, 1, 3).reshape(D, cols)
    )
    merged = jnp.concatenate([attn_part, gate_part, out_part], axis=1)
    merged = lax.psum_scatter(merged, "dp", scatter_dimension=0, tiled=True)
    grad_attn = (
        merged[:, : 3 * cols]
        .astype(F32)
        .reshape(D // dp_count, pairs, 3, 2, DH)
        .transpose(0, 1, 3, 2, 4)
        .reshape(D // dp_count, 3 * cols)
    )
    grad_gate = merged[:, 3 * cols : 4 * cols].astype(F32)
    pairs_perm = []
    for s in range(seq_count):
        for piece in range(dp_count):
            part, target = divmod(piece, seq_count)
            pairs_perm.append((s * dp_count + piece, target * dp_count + s * share + part))
    grad_out = lax.ppermute(merged[:, 4 * cols :], ("seq", "dp"), pairs_perm).astype(F32)
    return (grad_attn, grad_gate, grad_out, new_table, new_accum)


def solution(mesh):
    placed = (
        P(("dp", "seq"), None),
        P(("dp", "seq"), None),
        P("dp", None),
        P(("dp", "seq"), None),
        P(("dp", "seq")),
        P(),
        P(),
        P(),
        P(("seq", "dp"), None),
        P(("seq", "dp")),
    )
    return jax.shard_map(
        body,
        mesh=mesh,
        in_specs=placed,
        out_specs=(
            P("dp", "seq"),
            P("dp", "seq"),
            P("dp", "seq"),
            P(("seq", "dp"), None),
            P(("seq", "dp")),
        ),
        check_vma=False,
    )
```

time: 509 us -> 256 us (0.50); the launches traced: 502 us -> 254 us
  waiting for transfers between devices: 252 us -> 115 us
  matrix products: 82.5 us -> 11.1 us
  Pallas kernels: 0 us -> 52 us
  local copies, waits for them, and re-layouts: 57.2 us -> 30.1 us
  blocking collectives: 39.1 us -> 14.3 us
  other arithmetic: 26.9 us -> 5.08 us
  starting transfers between devices: 25.9 us -> 11.9 us
    reduce_scatter x6 -> x0, waiting for transfers between devices: 193 us -> none  [the longest x1 85.9 us: body(): lax.psum_scatter(partials[0], 'dp', scatter_dimension=0, tiled=True)]
    dot_general x20 -> x7, matrix products: 82.5 us -> 11.1 us  [the longest x2 5.36 us: dot_nt(): lax.dot_general(a, b, (((1,), (1,)), ((), ())), preferred_element_type=F32)]
    all_gather x0 -> x2, waiting for transfers between devices: none -> 60.4 us  [the longest x1 36.2 us: body(): x_full = lax.all_gather(layer_input, 'seq', axis=0, tiled=True)]
    pallas_call x0 -> x4, Pallas kernels: none -> 52 us  [the longest x1 22 us: forward_attention(): pl.pallas_call(functools.partial(forward_kernel, blk=blk, users=users, ma...]
    all_to_all x1 -> x0, blocking collectives: 39.1 us -> none  [body(): lax.all_to_all(head_grads.reshape(positions, head_local // 2, 6 * DH), 's...]
    convert_element_type x4 -> x0, local copies, waits for them, and re-layouts: 14.5 us -> none  [the longest x2 9.6 us: body(): acts_grad.astype(jnp.float32) * silu_grad(attn_pre)]
    all_gather x0 -> x1, blocking collectives: none -> 14.3 us  [body(): stats = lax.all_gather(stats_own, 'seq', axis=0, tiled=True)]
    all_to_all x4 -> x2, starting transfers between devices: 20.8 us -> 7.37 us  [the longest x1 4.72 us: body(): lax.all_to_all(input_part.reshape(seq_count, tokens_dev, D), 'seq', split...]
  transfers between devices with their start and end apart: 11 -> 7, of which waited for: 8 -> 5; matrix products, arithmetic and copies ran while one was open for 21% -> 14% of each run, Pallas kernels for 0% -> 9%
where the time goes in v1:
time: 256 us; the launch traced here: 254 us
  waiting for transfers between devices  115 us (45%)
  Pallas kernels  52 us (20%)
  local copies, waits for them, and re-layouts  30.1 us (12%)
  blocking collectives  14.3 us (6%)
  between operations  14 us (5%)
  starting transfers between devices  11.9 us (5%)
  matrix products  11.1 us (4%)
  other arithmetic  5.08 us (2%)
    all_gather x1, waiting for transfers between devices, body(): x_full = lax.all_gather(layer_input, 'seq', axis=0, tiled=True)  36.2 us
    all_to_all x1, waiting for transfers between devices, body(): lax.all_to_all(input_part.reshape(seq_count, tokens_dev, D), 'seq', split...  30.6 us
    all_gather x1, waiting for transfers between devices, body(): og_full = lax.all_gather(out_grad, 'seq', axis=0, tiled=True)  24.2 us
    pallas_call x1, Pallas kernels, forward_attention(): pl.pallas_call(functools.partial(forward_kernel, blk=blk, users=users, ma...  22 us
    all_to_all x1, waiting for transfers between devices, body(): lax.all_to_all(send_rows.reshape(devices, capacity, D), ('seq', 'dp'), sp...  19.9 us
    pallas_call x1, Pallas kernels, backward_attention(): pl.pallas_call(functools.partial(backward_kernel, blk=blk, users=users, m...  18.9 us
    all_gather x1, blocking collectives, body(): stats = lax.all_gather(stats_own, 'seq', axis=0, tiled=True)  14.3 us
    unnamed x36, local copies, waits for them, and re-layouts  10.5 us
  transfers between devices with their start and end apart: 7, of which 5 were waited for; matrix products, arithmetic and copies ran while one was open for 14% of the time, Pallas kernels for 9%

profile of v1, /device:TPU:0, one launch (start us, length us, event | category | flops | bytes accessed | tf_op | source)
XLA Modules:
  0.0 254.0 jit_solution(18253861372291460222)
XLA Ops:
  8.7 2.7 %constant_dynamic-slice_fusion = bf16[1024,768]{1,0:T(8,128)(2,1)} fusion(bf16[1024,3072]{1,0:T(8,128)(2,1)} %param.15, s32[]{:T(128)S(6)} %select_n.12), kind=kLoop, calls=%fused_computation.20 | loop fusion | bytes 3145732 | tf_op jit(solution)/shard_map/dynamic_slice | solution.py:403
  11.3 2.6 %copy.59 = bf16[1024,768]{0,1:T(8,128)(2,1)} copy(bf16[1024,768]{1,0:T(8,128)(2,1)} %constant_dynamic-slice_fusion) | data formatting | bytes 3145728
  13.9 2.7 %copy.48 = bf16[1024,2,3,2,64]{0,4,3,2,1:T(8,128)(2,1)} copy(bf16[1024,2,3,2,64]{0,4,2,3,1:T(8,128)(2,1)} %bitcast.35) | data formatting | bytes 3145728 | tf_op jit(solution)/shard_map/transpose | solution.py:404
  16.6 2.6 %copy.49.w_ref = bf16[1024,768]{1,0:T(8,128)(2,1)} copy(bf16[1024,768]{0,1:T(8,128)(2,1)} %bitcast.33) | data formatting | bytes 3145728 | tf_op jit(solution)/shard_map/reshape | solution.py:404
  20.1 1.9 constant_dynamic-slice_fusion.1.wo_ref
  22.0 36.2 %all-gather.3.cloned.1.call-done.x_ref = bf16[1024,1024]{1,0:T(8,128)(2,1)} async-done(((bf16[256,1024]{1,0:T(8,128)(2,1)}), bf16[1024,1024]{1,0:T(8,128)(2,1)}) %all-gather.3.cloned.1.call-update) | async-done | bytes 2097168 | tf_op jit(solution)/shard_map/all_gather | solution.py:424
  58.3 22.0 %attention_forward.1 = (bf16[1024,768]{1,0:T(8,128)(2,1)}, bf16[1024,768]{1,0:T(8,128)(2,1)}, bf16[4,1024,1024]{2,1,0:T(8,128)(2,1)}, bf16[4,1024,1024]{2,1,0:T(8,128)(2,1)}, bf16[1024,256]{1,0:T(8,128)(2,1)}) custom-call(s32[1,3]{1,0:T(1,128)} %lengths_ref.3, bf16[1024,1024]{1,0:T(8,128)(2,1)} %all-gather.3.cloned.1.call-done.x_ref, ...), custom_call_target="tpu_custom_call" | custom-call | flops 3758096384 | bytes 12582912 | tf_op jit(solution)/shard_map/attention_forward/pallas_call | solution.py:104
  80.3 24.2 %all-gather.5.cloned.1.call-done.og_ref = bf16[1024,1024]{1,0:T(8,128)(2,1)} async-done(((bf16[256,1024]{1,0:T(8,128)(2,1)}), bf16[1024,1024]{1,0:T(8,128)(2,1)}) %all-gather.5.cloned.1.call-update) | async-done | bytes 2097168 | tf_op jit(solution)/shard_map/all_gather | solution.py:425
  104.5 5.8 %gate_and_stats.1 = (f32[1024,256]{1,0:T(8,128)}, f32[1024,256]{1,0:T(8,128)}, f32[1024,256]{1,0:T(8,128)}, f32[8,1024]{1,0:T(8,128)}) custom-call(bf16[1024,1024]{1,0:T(8,128)(2,1)} %all-gather.3.cloned.1.call-done.x_ref, bf16[1024,1024]{1,0:T(8,128)(2,1)} %all-gather.5.cloned.1.call-done.og_ref, bf16[1024,256]{1,0:T(8,128)(2,1)} %constant_dynamic-slice_fusion.2.wg_ref, ...), custom_call_target="tpu_custom_call" | custom-call | flops 1073741824 | bytes 4194304 | tf_op jit(solution)/shard_map/gate_and_stats/pallas_call | solution.py:162
  110.3 14.3 %all_gather.11.stats_ref = f32[32,1024]{1,0:T(8,128)} all-gather(f32[8,1024]{1,0:T(8,128)} %get-tuple-element.20), channel_id=1, replica_groups=mesh['seq'=4,'dp'=8] {'seq'}, dimensions={0}, use_global_device_ids=true | all-gather | bytes 163840 | tf_op jit(solution)/shard_map/all_gather | solution.py:429
  124.6 18.9 %attention_backward.1 = (bf16[1024,768]{1,0:T(8,128)(2,1)}, bf16[1024,256]{1,0:T(8,128)(2,1)}, bf16[1024,256]{1,0:T(8,128)(2,1)}) custom-call(s32[1,3]{1,0:T(1,128)} %lengths_ref.3, f32[32,1024]{1,0:T(8,128)} %all_gather.11.stats_ref, bf16[1024,256]{1,0:T(8,128)(2,1)} %get-tuple-element.19.heads_ref, f32[1024,256]{1,0:T(8,128)} %get-tuple-element.21.gate_ref, ...), custom_call_target="tpu_custom_call" | custom-call | flops 4294967296 | bytes 13631488 | tf_op jit(solution)/shard_map/attention_backward/pallas_call | solution.py:297
  143.6 3.3 %fusion.6 = f32[1024,1024]{1,0:T(8,128)S(1)} fusion(bf16[1024,768]{1,0:T(8,128)(2,1)} %get-tuple-element.28, bf16[1024,768]{0,1:T(8,128)(2,1)S(1)} %bitcast.34), kind=kOutput, calls=%fused_computation.24 | convolution fusion | flops 1610612736 | bytes 7340032 | tf_op jit(solution)/shard_map/dot_general | solution.py:27
  146.9 2.1 add_convert_fusion
  149.0 4.7 %all-to-all-start.1 = ((bf16[4,256,1024]{2,1,0:T(8,128)(2,1)}), bf16[4,256,1024]{2,1,0:T(8,128)(2,1)}, u32[]{:S(2)}, u32[]{:S(2)}) async-start(bf16[4,256,1024]{2,1,0:T(8,128)(2,1)} %bitcast.11), calls=%async_computation.1 | async-start | bytes 4194304 | tf_op jit(solution)/shard_map/all_to_all | solution.py:435
  153.8 1.5 convolution_convert_fusion.2
  155.3 1.6 reshape.58
  156.9 1.3 copy.50
  158.2 1.4 reshape.59
  161.0 1.8 fusion
  163.1 2.7 %copy.57 = bf16[1024,1280]{1,0:T(8,128)(2,1)} copy(bf16[1024,1280]{0,1:T(8,128)(2,1)S(1)} %pad_maximum_fusion) | data formatting | bytes 5242880
  167.6 30.6 %all-to-all-done.1 = bf16[4,256,1024]{2,1,0:T(8,128)(2,1)} async-done(((bf16[4,256,1024]{2,1,0:T(8,128)(2,1)}), bf16[4,256,1024]{2,1,0:T(8,128)(2,1)}, u32[]{:S(2)}, u32[]{:S(2)}) %all-to-all-start.1) | async-done | bytes 2097184 | tf_op jit(solution)/shard_map/all_to_all | solution.py:435
  198.2 3.8 %all-to-all-start = ((s32[32,1,16]{2,1,0:T(1,128)}), s32[32,1,16]{2,1,0:T(1,128)S(1)}, u32[]{:S(2)}, u32[]{:S(2)}) async-start(s32[32,1,16]{2,1,0:T(1,128)} %bitcast.10), calls=%async_computation | async-start | bytes 32768 | tf_op jit(solution)/shard_map/all_to_all | solution.py:419
  202.0 2.3 convert_reduce_fusion
  204.3 1.4 convolution_convert_fusion.1
  205.7 3.1 %all-to-all-done = s32[32,1,16]{2,1,0:T(1,128)S(1)} async-done(((s32[32,1,16]{2,1,0:T(1,128)}), s32[32,1,16]{2,1,0:T(1,128)S(1)}, u32[]{:S(2)}, u32[]{:S(2)}) %all-to-all-start) | async-done | bytes 2080 | tf_op jit(solution)/shard_map/all_to_all | solution.py:419
  208.9 2.6 %all-to-all-start.2 = ((bf16[32,16,1024]{2,1,0:T(8,128)(2,1)}), bf16[32,16,1024]{2,1,0:T(8,128)(2,1)S(1)}, u32[]{:S(2)}, u32[]{:S(2)}) async-start(bf16[32,16,1024]{2,1,0:T(8,128)(2,1)} %bitcast.12), calls=%async_computation.2 | async-start | bytes 2097152 | tf_op jit(solution)/shard_map/all_to_all | solution.py:440
  214.3 0.9 slice.12
  217.2 0.9 copy.54
  219.7 19.9 %all-to-all-done.2 = bf16[32,16,1024]{2,1,0:T(8,128)(2,1)S(1)} async-done(((bf16[32,16,1024]{2,1,0:T(8,128)(2,1)}), bf16[32,16,1024]{2,1,0:T(8,128)(2,1)S(1)}, u32[]{:S(2)}, u32[]{:S(2)}) %all-to-all-start.2) | async-done | bytes 1048608 | tf_op jit(solution)/shard_map/all_to_all | solution.py:440
  239.6 1.0 copy-done.6
  240.6 5.2 %update_rows.1 = (f32[512,1024]{1,0:T(8,128)}, f32[512,1]{1,0:T(8,128)}) custom-call(s32[1,512]{1,0:T(1,128)} %reshape_reshape.3.ids_ref, bf16[512,1024]{1,0:T(8,128)(2,1)} %bitcast.36, f32[512,1024]{1,0:T(8,128)} %table_ref.1, f32[512,1]{1,0:T(8,128)} %copy.53.accum_ref), custom_call_target="tpu_custom_call" | custom-call | flops 536870912 | bytes 5242880 | tf_op jit(solution)/shard_map/update_rows/pallas_call | solution.py:354
  245.8 1.7 reduce.1
  (55 shorter events, 12.0 us)
Async XLA Ops:
  7.2 12.1 %copy-start = (bf16[1024,1024]{1,0:T(8,128)(2,1)S(1)}, bf16[1024,1024]{1,0:T(8,128)(2,1)}, u32[]{:S(2)}) copy-start(bf16[1024,1024]{1,0:T(8,128)(2,1)} %param.16) | copy-start | bytes 6291460
  7.2 51.1 %all-gather.3.cloned.1.call-start = ((), (), s32[]{:S(2)}) async-start(), calls=%async_computation.4 | async-start | bytes 2621440 | tf_op jit(solution)/shard_map/all_gather | solution.py:424
  7.9 96.6 %all-gather.5.cloned.1.call-start = ((), (), s32[]{:S(2)}) async-start(), calls=%async_computation.5 | async-start | bytes 2621440 | tf_op jit(solution)/shard_map/all_gather | solution.py:425
  124.6 18.9 %copy-start.4 = (bf16[1024,2,3,2,64]{0,4,3,2,1:T(8,128)(2,1)S(1)}, bf16[1024,2,3,2,64]{0,4,3,2,1:T(8,128)(2,1)}, u32[]{:S(2)}) copy-start(bf16[1024,2,3,2,64]{0,4,3,2,1:T(8,128)(2,1)} %copy.48) | copy-start | bytes 4718596
  143.6 3.3 %copy-start.5 = (bf16[1024,256]{1,0:T(8,128)(2,1)S(1)}, bf16[1024,256]{1,0:T(8,128)(2,1)}, u32[]{:S(2)}) copy-start(bf16[1024,256]{1,0:T(8,128)(2,1)} %constant_dynamic-slice_fusion.2.wg_ref) | copy-start | bytes 1572868
  143.6 3.3 %copy-start.7 = (bf16[1024,256]{1,0:T(8,128)(2,1)S(1)}, bf16[1024,256]{1,0:T(8,128)(2,1)}, u32[]{:S(2)}) copy-start(bf16[1024,256]{1,0:T(8,128)(2,1)} %get-tuple-element.29) | copy-start | bytes 1572868
  149.0 4.8 %copy-start.3 = (bf16[1024,1024]{1,0:T(8,128)(2,1)S(1)}, bf16[1024,1024]{1,0:T(8,128)(2,1)}, u32[]{:S(2)}) copy-start(bf16[1024,1024]{1,0:T(8,128)(2,1)} %all-gather.5.cloned.1.call-done.og_ref) | copy-start | bytes 6291460
  149.0 4.8 %copy-start.9 = (bf16[1024,256]{1,0:T(8,128)(2,1)S(1)}, bf16[1024,256]{1,0:T(8,128)(2,1)}, u32[]{:S(2)}) copy-start(bf16[1024,256]{1,0:T(8,128)(2,1)} %get-tuple-element.30) | copy-start | bytes 1572868
  149.0 49.2 %all-to-all-start.1 = ((bf16[4,256,1024]{2,1,0:T(8,128)(2,1)}), bf16[4,256,1024]{2,1,0:T(8,128)(2,1)}, u32[]{:S(2)}, u32[]{:S(2)}) async-start(bf16[4,256,1024]{2,1,0:T(8,128)(2,1)} %bitcast.11), calls=%async_computation.1 | async-start | bytes 4194304 | tf_op jit(solution)/shard_map/all_to_all | solution.py:435
  153.7 60.6 %reduce-scatter.4.cloned.1.call-start = ((), (), s32[]{:S(2)}) async-start(), calls=%async_computation.6 | async-start | bytes 2949120
  155.3 4.3 %copy-start.2 = (bf16[1024,1024]{1,0:T(8,128)(2,1)S(1)}, bf16[1024,1024]{1,0:T(8,128)(2,1)}, u32[]{:S(2)}) copy-start(bf16[1024,1024]{1,0:T(8,128)(2,1)} %all-gather.3.cloned.1.call-done.x_ref) | copy-start | bytes 6291460
  159.6 1.4 copy-start.13
  165.9 0.7 copy-start.11
  165.9 0.9 copy-start.12
  165.9 38.4 %copy-start.8 = (bf16[256,1024]{1,0:T(8,128)(2,1)S(1)}, bf16[256,1024]{1,0:T(8,128)(2,1)}, u32[]{:S(2)}) copy-start(bf16[256,1024]{1,0:T(8,128)(2,1)} %param.11) | copy-start | bytes 1572868
  198.2 10.7 %all-to-all-start = ((s32[32,1,16]{2,1,0:T(1,128)}), s32[32,1,16]{2,1,0:T(1,128)S(1)}, u32[]{:S(2)}, u32[]{:S(2)}) async-start(s32[32,1,16]{2,1,0:T(1,128)} %bitcast.10), calls=%async_computation | async-start | bytes 32768 | tf_op jit(solution)/shard_map/all_to_all | solution.py:419
  204.3 7.3 %copy-start.10 = (f32[512]{0:T(512)S(1)}, f32[512]{0:T(512)}, u32[]{:S(2)}) copy-start(f32[512]{0:T(512)} %param.19) | copy-start | bytes 6148
  208.9 30.7 %all-to-all-start.2 = ((bf16[32,16,1024]{2,1,0:T(8,128)(2,1)}), bf16[32,16,1024]{2,1,0:T(8,128)(2,1)S(1)}, u32[]{:S(2)}, u32[]{:S(2)}) async-start(bf16[32,16,1024]{2,1,0:T(8,128)(2,1)} %bitcast.12), calls=%async_computation.2 | async-start | bytes 2097152 | tf_op jit(solution)/shard_map/all_to_all | solution.py:440
  216.4 2.6 %collective-permute-start = (bf16[128,256]{0,1:T(8,128)(2,1)S(1)}, bf16[128,256]{0,1:T(8,128)(2,1)S(1)}, u32[]{:S(2)}, u32[]{:S(2)}) collective-permute-start(bf16[128,256]{0,1:T(8,128)(2,1)S(1)} %copy.62), channel_id=1, source_target_pairs={{0,0},{1,8},{2,16},{3,24},{4,1},{5,9},{6,17},{7,25},{8,2},{9,10},{... | collective-permute-start | bytes 196616 | tf_op jit(solution)/shard_map/ppermute | solution.py:468
  218.1 29.4 %copy-start.1 = (bf16[1024,1024]{1,0:T(8,128)(2,1)S(1)}, bf16[1024,1024]{1,0:T(8,128)(2,1)}, u32[]{:S(2)}) copy-start(bf16[1024,1024]{1,0:T(8,128)(2,1)} %param.16) | copy-start | bytes 6291460
  239.6 1.0 copy-start.6
Sparse Core Ops, SparseCore 0:
  9.6 48.6 all-gather.2
  59.8 44.6 all-gather.4
  166.0 43.5 reduce-scatter.3

commit v2 on v1

v2 whole, which is shorter than its diff:
```python
import functools

import jax
import jax.numpy as jnp
from jax import lax
from jax.experimental import pallas as pl
from jax.experimental.pallas import tpu as pltpu
from jax.sharding import PartitionSpec as P

D = 1024
H = 16
DH = 64
PAIR = 2 * DH

NORM_EPS = 1e-05
LEARN_RATE = 0.1
VMEM_LIMIT = 56 * 1024 * 1024
BF = jnp.bfloat16
F32 = jnp.float32


def dot_nn(a, b):
    return lax.dot_general(a, b, (((1,), (0,)), ((), ())), preferred_element_type=F32)


def dot_nt(a, b):
    return lax.dot_general(a, b, (((1,), (1,)), ((), ())), preferred_element_type=F32)


def history_start(lengths_ref, users, place):
    start = jnp.zeros_like(place)
    end = jnp.int32(0)
    for user in range(users - 1):
        end = end + lengths_ref[0, user]
        start = jnp.where(place >= end, end, start)
    return start


def block_needed(lengths_ref, users, i, j, blk):
    return (j + 1) * blk > history_start(lengths_ref, users, i * blk)


def forward_kernel(*refs, blk, users, maxlen, count):
    lengths_ref, order_ref = refs[:2]
    x_refs = refs[2 : 2 + count]
    w_ref, x_out_ref, acts_ref, slopes_ref, gate_ref, weights_ref, score_slope_ref, heads_ref, q_half = refs[2 + count :]
    i = pl.program_id(1)
    block_rows = x_refs[0].shape[0]

    @pl.when((i == 0) & (pl.program_id(0) == 0))
    def _():
        for b in range(count):
            at = pl.ds(pl.multiple_of(order_ref[b] * block_rows, block_rows), block_rows)
            x_out_ref[at, :] = x_refs[b][...]

    @pl.when(i == 0)
    def _():
        for b in range(count):
            for r in range(block_rows // blk):
                at = pl.ds(pl.multiple_of(order_ref[b] * block_rows + r * blk, blk), blk)
                pre = dot_nn(x_refs[b][r * blk : (r + 1) * blk, :], w_ref[...])
                half = 0.5 * pre
                t = jnp.tanh(half)
                p = half * t
                silu = half + p
                acts = silu[:, : 3 * PAIR].astype(BF)
                acts_ref[at, :] = acts
                gate_ref[at, :] = silu[:, 3 * PAIR :]
                slopes_ref[at, :] = (0.5 * (1.0 + t) * (1.0 + half - p)).astype(BF)
                q_half[at, :] = acts[:, PAIR : 2 * PAIR] * jnp.asarray(0.5 * DH**-0.5, BF)

    at_i = pl.ds(pl.multiple_of(i * blk, blk), blk)
    q_i = q_half[at_i, :]
    row = i * blk + lax.broadcasted_iota(jnp.int32, (blk, blk), 0)
    col0 = lax.broadcasted_iota(jnp.int32, (blk, blk), 1)
    start = history_start(lengths_ref, users, row)

    def column(j, acc):
        at_j = pl.ds(pl.multiple_of(j * blk, blk), blk)
        col = col0 + j * blk
        allowed = (col <= row) & (col >= start)
        outs = []
        for h in range(2):
            lanes = slice(h * DH, (h + 1) * DH)
            k_j = acts_ref[at_j, 2 * PAIR + h * DH : 2 * PAIR + (h + 1) * DH]
            v_j = acts_ref[at_j, h * DH : (h + 1) * DH]
            half = dot_nt(q_i[:, lanes], k_j)
            half = jnp.where(allowed, half, -64.0)
            t = jnp.tanh(half)
            p = half * t
            weights = (half + p).astype(BF)
            weights_ref[h, :, at_j] = weights
            score_slope_ref[h, :, at_j] = ((1.0 + t) * (1.0 + half - p)).astype(BF)
            outs.append(acc[h] + dot_nn(weights, v_j))
        return tuple(outs)

    first = history_start(lengths_ref, users, i * blk) // blk
    zero = jnp.zeros((blk, DH), F32)
    acc = lax.fori_loop(first, i + 1, column, (zero, zero))
    heads_ref[...] = (jnp.concatenate(acc, axis=1) * (1.0 / maxlen)).astype(BF)


def forward_attention(lengths, order, x_blocks, w_own, blk, maxlen):
    count = len(x_blocks)
    block_rows = x_blocks[0].shape[0]
    positions = count * block_rows
    pairs = w_own.shape[1] // (4 * PAIR)
    users = lengths.shape[1]
    elements = pairs * positions * positions
    return pl.pallas_call(
        functools.partial(forward_kernel, blk=blk, users=users, maxlen=maxlen, count=count),
        grid=(pairs, positions // blk),
        in_specs=[pl.BlockSpec(memory_space=pltpu.SMEM), pl.BlockSpec(memory_space=pltpu.SMEM)]
        + [pl.BlockSpec((block_rows, D), lambda p, i: (0, 0))] * count
        + [pl.BlockSpec((D, 4 * PAIR), lambda p, i: (0, p))],
        out_specs=[
            pl.BlockSpec((positions, D), lambda p, i: (0, 0)),
            pl.BlockSpec((positions, 3 * PAIR), lambda p, i: (0, p)),
            pl.BlockSpec((positions, 4 * PAIR), lambda p, i: (0, p)),
            pl.BlockSpec((positions, PAIR), lambda p, i: (0, p)),
            pl.BlockSpec((2, blk, positions), lambda p, i: (p, i, 0)),
            pl.BlockSpec((2, blk, positions), lambda p, i: (p, i, 0)),
            pl.BlockSpec((blk, PAIR), lambda p, i: (i, p)),
        ],
        out_shape=[
            jax.ShapeDtypeStruct((positions, D), BF),
            jax.ShapeDtypeStruct((positions, pairs * 3 * PAIR), BF),
            jax.ShapeDtypeStruct((positions, pairs * 4 * PAIR), BF),
            jax.ShapeDtypeStruct((positions, pairs * PAIR), F32),
            jax.ShapeDtypeStruct((2 * pairs, positions, positions), BF),
            jax.ShapeDtypeStruct((2 * pairs, positions, positions), BF),
            jax.ShapeDtypeStruct((positions, pairs * PAIR), BF),
        ],
        scratch_shapes=[pltpu.VMEM((positions, PAIR), BF)],
        compiler_params=pltpu.CompilerParams(vmem_limit_bytes=VMEM_LIMIT),
        cost_estimate=pl.CostEstimate(
            flops=2 * positions * D * pairs * 4 * PAIR + 4 * elements * 256,
            bytes_accessed=4 * positions * D + 4 * elements,
            transcendentals=elements,
        ),
        name="attention_forward",
    )(lengths, order, *x_blocks, w_own)


def stats_kernel(*refs, count):
    order_ref = refs[0]
    mg_refs = refs[1 : 1 + count]
    gate_ref, heads_ref, mg_out_ref, stats_ref = refs[1 + count :]
    block_rows = mg_refs[0].shape[0]
    step = min(256, block_rows)
    for b in range(count):
        for r in range(block_rows // step):
            at = pl.ds(pl.multiple_of(order_ref[b] * block_rows + r * step, step), step)
            mg = mg_refs[b][r * step : (r + 1) * step, :]
            mg_out_ref[at, :] = mg
            ng = mg.astype(F32) * gate_ref[at, :]
            heads = heads_ref[at, :].astype(F32)
            mean = jnp.mean(heads, axis=1, keepdims=True)
            centred = heads - mean
            square = jnp.sum(centred * centred, axis=1, keepdims=True)
            total = jnp.sum(ng, axis=1, keepdims=True)
            cross = jnp.sum(ng * centred, axis=1, keepdims=True)
            lane = lax.broadcasted_iota(jnp.int32, (step, 128), 1)
            packed = jnp.where(lane == 0, mean, jnp.where(lane == 1, square, jnp.where(lane == 2, total, cross)))
            stats_ref[:, at] = jnp.transpose(packed)[:8, :]


def event_stats(order, mg_blocks, gate, heads):
    positions, cols = heads.shape
    count = len(mg_blocks)
    vmem = pl.BlockSpec(memory_space=pltpu.VMEM)
    return pl.pallas_call(
        functools.partial(stats_kernel, count=count),
        in_specs=[pl.BlockSpec(memory_space=pltpu.SMEM)] + [vmem] * (count + 2),
        out_specs=[vmem, vmem],
        out_shape=[
            jax.ShapeDtypeStruct((positions, cols), BF),
            jax.ShapeDtypeStruct((8, positions), F32),
        ],
        compiler_params=pltpu.CompilerParams(vmem_limit_bytes=VMEM_LIMIT),
        cost_estimate=pl.CostEstimate(flops=10 * positions * cols, bytes_accessed=10 * positions * cols, transcendentals=0),
        name="event_stats",
    )(order, *mg_blocks, gate, heads)


def backward_kernel(*refs, blk, users, maxlen, shards, cols):
    lengths_ref = refs[0]
    stats_refs = refs[1 : 1 + shards]
    heads_ref, gate_ref, mg_ref, acts_ref, slopes_ref, weights_ref, score_slope_ref = refs[1 + shards : 8 + shards]
    grad_ref, mixed_ref, o_ref, o_t, q_t, vg_t, kg_t, qg = refs[8 + shards :]
    i = pl.program_id(1)
    positions = heads_ref.shape[0]
    blocks = positions // blk
    scale = DH ** (-0.5)

    @pl.when(i == 0)
    def _():
        means = [ref[0:1, :] for ref in stats_refs]
        mean = sum(means) * (1.0 / shards)
        square = jnp.zeros_like(mean)
        total = jnp.zeros_like(mean)
        cross = jnp.zeros_like(mean)
        for s, ref in enumerate(stats_refs):
            shift = means[s] - mean
            part = ref[2:3, :]
            square = square + ref[1:2, :] + cols * shift * shift
            total = total + part
            cross = cross + ref[3:4, :] + shift * part
        inv_dev = lax.rsqrt(square * (1.0 / D) + NORM_EPS)
        row8 = lax.broadcasted_iota(jnp.int32, (128, positions), 0)
        packed = jnp.where(
            row8 == 0,
            mean,
            jnp.where(row8 == 1, inv_dev, jnp.where(row8 == 2, total * (1.0 / D), cross * inv_dev * (1.0 / D))),
        )
        per_event = jnp.transpose(packed)
        mean_c = per_event[:, 0:1]
        inv_c = per_event[:, 1:2]
        total_c = per_event[:, 2:3]
        cross_c = per_event[:, 3:4]
        normed = (heads_ref[...].astype(F32) - mean_c) * inv_c
        gate = gate_ref[...]
        mg = mg_ref[...].astype(F32)
        mixed_ref[...] = (normed * gate).astype(BF)
        grad_ref[:, 3 * PAIR :] = (mg * normed * slopes_ref[:, 3 * PAIR :].astype(F32)).astype(BF)
        o = (inv_c * (mg * gate - total_c - normed * cross_c)).astype(BF)
        o_ref[...] = o
        o_t[...] = jnp.transpose(o)
        q_t[...] = jnp.transpose(acts_ref[:, PAIR : 2 * PAIR])
        vg_t[...] = jnp.zeros_like(vg_t)
        kg_t[...] = jnp.zeros_like(kg_t)

    at_i = pl.ds(pl.multiple_of(i * blk, blk), blk)

    def column(j, acc):
        at_j = pl.ds(pl.multiple_of(j * blk, blk), blk)
        outs = []
        for h in range(2):
            lanes = slice(h * DH, (h + 1) * DH)
            k_j = acts_ref[at_j, 2 * PAIR + h * DH : 2 * PAIR + (h + 1) * DH]
            v_j = acts_ref[at_j, h * DH : (h + 1) * DH]
            weight_grad = dot_nt(o_ref[at_i, lanes], v_j)
            score_grad = (weight_grad * score_slope_ref[h, :, at_j].astype(F32)).astype(BF)
            vg_t[lanes, at_j] += dot_nn(o_t[lanes, at_i], weights_ref[h, :, at_j])
            kg_t[lanes, at_j] += dot_nn(q_t[lanes, at_i], score_grad)
            outs.append(acc[h] + dot_nn(score_grad, k_j))
        return tuple(outs)

    first = history_start(lengths_ref, users, i * blk) // blk
    zero = jnp.zeros((blk, DH), F32)
    acc = lax.fori_loop(first, i + 1, column, (zero, zero))
    qg[at_i, :] = jnp.concatenate(acc, axis=1)

    @pl.when(i == blocks - 1)
    def _():
        factor = 0.5 * scale / maxlen
        v_grad = (jnp.transpose(vg_t[...]) * (1.0 / maxlen)).astype(BF).astype(F32)
        q_grad = (qg[...] * factor).astype(BF).astype(F32)
        k_grad = (jnp.transpose(kg_t[...]) * factor).astype(BF).astype(F32)
        grad_ref[:, :PAIR] = (v_grad * slopes_ref[:, :PAIR].astype(F32)).astype(BF)
        grad_ref[:, PAIR : 2 * PAIR] = (q_grad * slopes_ref[:, PAIR : 2 * PAIR].astype(F32)).astype(BF)
        grad_ref[:, 2 * PAIR : 3 * PAIR] = (k_grad * slopes_ref[:, 2 * PAIR : 3 * PAIR].astype(F32)).astype(BF)


def backward_attention(lengths, stats, heads, gate, mg, acts, slopes, weights, score_slope, blk, maxlen):
    positions, cols = heads.shape
    pairs = cols // PAIR
    shards = len(stats)
    users = lengths.shape[1]
    elements = pairs * positions * positions
    whole = lambda p, i: (0, p)
    return pl.pallas_call(
        functools.partial(backward_kernel, blk=blk, users=users, maxlen=maxlen, shards=shards, cols=cols),
        grid=(pairs, positions // blk),
        in_specs=[pl.BlockSpec(memory_space=pltpu.SMEM)]
        + [pl.BlockSpec((8, positions), lambda p, i: (0, 0))] * shards
        + [
            pl.BlockSpec((positions, PAIR), whole),
            pl.BlockSpec((positions, PAIR), whole),
            pl.BlockSpec((positions, PAIR), whole),
            pl.BlockSpec((positions, 3 * PAIR), whole),
            pl.BlockSpec((positions, 4 * PAIR), whole),
            pl.BlockSpec((2, blk, positions), lambda p, i: (p, i, 0)),
            pl.BlockSpec((2, blk, positions), lambda p, i: (p, i, 0)),
        ],
        out_specs=[
            pl.BlockSpec((positions, 4 * PAIR), whole),
            pl.BlockSpec((positions, PAIR), whole),
        ],
        out_shape=[
            jax.ShapeDtypeStruct((positions, pairs * 4 * PAIR), BF),
            jax.ShapeDtypeStruct((positions, cols), BF),
        ],
        scratch_shapes=[
            pltpu.VMEM((positions, PAIR), BF),
            pltpu.VMEM((PAIR, positions), BF),
            pltpu.VMEM((PAIR, positions), BF),
            pltpu.VMEM((PAIR, positions), F32),
            pltpu.VMEM((PAIR, positions), F32),
            pltpu.VMEM((positions, PAIR), F32),
        ],
        compiler_params=pltpu.CompilerParams(vmem_limit_bytes=VMEM_LIMIT),
        cost_estimate=pl.CostEstimate(
            flops=8 * elements * 256, bytes_accessed=4 * elements + 16 * positions * cols, transcendentals=0
        ),
        name="attention_backward",
    )(lengths, *stats, heads, gate, mg, acts, slopes, weights, score_slope)


def update_kernel(ids_ref, rows_ref, table_ref, accum_ref, new_table_ref, new_accum_ref):
    i = pl.program_id(0)
    blk = table_ref.shape[0]
    slots = rows_ref.shape[0]
    row = i * blk + lax.broadcasted_iota(jnp.int32, (blk, slots), 0)
    hits = jnp.where(row == ids_ref[...], 1.0, 0.0).astype(BF)
    grad = dot_nn(hits, rows_ref[...])
    accum_rows = jnp.broadcast_to(accum_ref[...], (128, blk))
    accum = jnp.transpose(accum_rows)[:, :1] + jnp.mean(grad * grad, axis=1, keepdims=True)
    new_accum_ref[...] = jnp.transpose(jnp.broadcast_to(accum, (blk, 128)))[:1, :]
    new_table_ref[...] = table_ref[...] - LEARN_RATE * grad * lax.rsqrt(accum)


def update_rows(got_ids, got_rows, emb_table, row_accum):
    rows_own = emb_table.shape[0]
    slots = got_rows.shape[0]
    blk = min(128, rows_own)
    new_table, new_accum = pl.pallas_call(
        update_kernel,
        grid=(rows_own // blk,),
        in_specs=[
            pl.BlockSpec((1, slots), lambda i: (0, 0)),
            pl.BlockSpec((slots, D), lambda i: (0, 0)),
            pl.BlockSpec((blk, D), lambda i: (i, 0)),
            pl.BlockSpec((1, blk), lambda i: (0, i)),
        ],
        out_specs=[
            pl.BlockSpec((blk, D), lambda i: (i, 0)),
            pl.BlockSpec((1, blk), lambda i: (0, i)),
        ],
        out_shape=[
            jax.ShapeDtypeStruct((rows_own, D), F32),
            jax.ShapeDtypeStruct((1, rows_own), F32),
        ],
        compiler_params=pltpu.CompilerParams(vmem_limit_bytes=VMEM_LIMIT),
        cost_estimate=pl.CostEstimate(
            flops=2 * rows_own * slots * D, bytes_accessed=8 * rows_own * D + 2 * slots * D, transcendentals=rows_own
        ),
        name="update_rows",
    )(got_ids.reshape(1, slots), got_rows, emb_table, row_accum.reshape(1, rows_own))
    return new_table, new_accum.reshape(rows_own)


def own_weights(w_attn, w_gate, part, cols):
    pairs = cols // PAIR
    slices = jnp.concatenate(
        [
            lax.dynamic_slice_in_dim(w_attn, part * 3 * cols, 3 * cols, 1),
            lax.dynamic_slice_in_dim(w_gate, part * cols, cols, 1),
        ],
        axis=1,
    )
    place = jnp.arange(4 * cols, dtype=jnp.int32)
    pair, kind, head, entry = place // (4 * PAIR), place // PAIR % 4, place // DH % 2, place % DH
    source = jnp.where(
        kind < 3, pair * 3 * PAIR + head * 3 * DH + kind * DH + entry, 3 * cols + pair * PAIR + head * DH + entry
    )
    pick = (place[:, None] == source[None, :]).astype(BF)
    return jnp.dot(slices, pick, preferred_element_type=F32).astype(BF)


def split_columns(part, cols):
    rows = part.shape[0]
    pairs = cols // PAIR
    part = part.reshape(rows, pairs, 4, 2, DH)
    attn = part[:, :, :3].transpose(0, 1, 3, 2, 4).reshape(rows, 3 * cols)
    return attn, part[:, :, 3].reshape(rows, cols)


def row_slots(owners, rows, rows_own, devices, capacity):
    events = owners.shape[0]
    owner_hits = (owners[:, None] == jnp.arange(devices, dtype=jnp.int32)[None, :]).astype(F32)
    place = jnp.arange(events, dtype=jnp.int32)
    before = (place[:, None] > place[None, :]).astype(F32)
    slots = jnp.sum(jnp.dot(before, owner_hits) * owner_hits, axis=1).astype(jnp.int32)
    flat_slot = owners * capacity + slots
    slot_hits = jnp.arange(devices * capacity, dtype=jnp.int32)[:, None] == flat_slot[None, :]
    send_ids = jnp.min(jnp.where(slot_hits, rows[None, :], rows_own), axis=1).astype(jnp.int32)
    return slot_hits.astype(BF), send_ids


def to_owners(rows, devices, capacity):
    shape = (devices, capacity) + rows.shape[1:]
    got = lax.all_to_all(rows.reshape(shape), ("seq", "dp"), split_axis=0, concat_axis=0, tiled=True)
    return got.reshape(rows.shape)


TN = (((0,), (0,)), ((), ()))


def body_whole(
    layer_input, out_grad, lengths, item_owner, item_row, w_attn, w_gate, w_out, emb_table, row_accum
):
    seq_count = lax.axis_size("seq")
    dp_count = lax.axis_size("dp")
    devices = seq_count * dp_count
    seq_id = lax.axis_index("seq")
    tokens_dev = layer_input.shape[0]
    positions = tokens_dev * seq_count
    maxlen = 2 * positions // 3
    blk = min(256, positions)
    cols = D // seq_count
    rows_own = emb_table.shape[0]
    capacity = max(2, 2 * tokens_dev // devices)

    w_own = own_weights(w_attn, w_gate, seq_id, cols)
    w_out_own = lax.dynamic_slice_in_dim(w_out, seq_id * cols, cols, 0)
    slot_matrix, send_ids = row_slots(item_owner[:, 0], item_row, rows_own, devices, capacity)
    got_ids = to_owners(send_ids, devices, capacity)

    x_full = lax.all_gather(layer_input, "seq", axis=0, tiled=True)
    og_full = lax.all_gather(out_grad, "seq", axis=0, tiled=True)
    order = jnp.zeros((1,), jnp.int32)
    x_full, acts, slopes, gate, weights, score_slope, heads = forward_attention(
        lengths, order, [x_full], w_own, blk, maxlen
    )
    mg = dot_nt(og_full, w_out_own).astype(BF)
    mg, stats_own = event_stats(order, [mg], gate, heads)
    stats = lax.all_gather(stats_own, "seq", axis=0, tiled=False)
    grads, mixed = backward_attention(
        lengths, [stats[s] for s in range(seq_count)], heads, gate, mg, acts, slopes, weights, score_slope, blk, maxlen
    )

    input_part = dot_nt(grads, w_own).astype(BF)
    got = lax.all_to_all(
        input_part.reshape(seq_count, tokens_dev, D), "seq", split_axis=0, concat_axis=0, tiled=True
    )
    input_grad = jnp.sum(got.astype(F32), axis=0) + out_grad.astype(F32)
    send_rows = jnp.dot(slot_matrix, input_grad.astype(BF), preferred_element_type=F32).astype(BF)
    got_rows = to_owners(send_rows, devices, capacity)
    new_table, new_accum = update_rows(got_ids, got_rows, emb_table, row_accum)

    proj_part = lax.dot_general(x_full, grads, TN, preferred_element_type=F32).astype(BF)
    out_part = lax.dot_general(mixed, og_full, TN, preferred_element_type=F32).astype(BF)
    share = dp_count // seq_count
    out_part = out_part.reshape(share, D // dp_count, seq_count, cols).transpose(0, 2, 1, 3).reshape(D, cols)
    merged = jnp.concatenate([proj_part, out_part], axis=1)
    merged = lax.psum_scatter(merged, "dp", scatter_dimension=0, tiled=True)
    grad_attn, grad_gate = split_columns(merged[:, : 4 * cols].astype(F32), cols)
    steps = []
    for s in range(seq_count):
        for piece in range(dp_count):
            part, target = divmod(piece, seq_count)
            steps.append((s * dp_count + piece, target * dp_count + s * share + part))
    grad_out = lax.ppermute(merged[:, 4 * cols :], ("seq", "dp"), steps).astype(F32)
    return (grad_attn, grad_gate, grad_out, new_table, new_accum)


SEQ = 4
PLANE = 4


def send(array, target):
    steps = []
    for s in range(SEQ):
        for e in range(PLANE):
            for c in range(2):
                to = target(s, e, c)
                if to is not None:
                    steps.append((s * 2 * PLANE + 2 * e + c, to[0] * 2 * PLANE + 2 * to[1] + to[2]))
    return lax.ppermute(array, ("seq", "dp"), steps)


def home(s, c):
    return c == s // 2


def swap_far(array):
    return send(array, lambda s, e, c: None if home(s, c) else (3 - s, e, 1 - c))


def swap_near_home(array):
    return send(array, lambda s, e, c: (s ^ 1, e, c) if home(s, c) else None)


def swap_near_far(array):
    return send(array, lambda s, e, c: None if home(s, c) else (s ^ 1, e, c))


def swap_near(array):
    return send(array, lambda s, e, c: (s ^ 1, e, c))


def swap_core(array):
    return send(array, lambda s, e, c: (s, e, 1 - c))


def swap_x(array):
    return send(array, lambda s, e, c: (s, e ^ 1, c))


def swap_y(array):
    return send(array, lambda s, e, c: (s, e ^ 2, c))


def after(array, *others):
    return lax.optimization_barrier((array,) + others)[0]


def body_pairs(
    layer_input, out_grad, lengths, item_owner, item_row, w_attn, w_gate, w_out, emb_table, row_accum
):
    devices = 2 * PLANE * SEQ
    s = lax.axis_index("seq")
    d = lax.axis_index("dp")
    e, c = d // 2, d % 2
    tokens_dev = layer_input.shape[0]
    positions = tokens_dev * SEQ
    maxlen = 2 * positions // 3
    blk = min(256, positions)
    cols = D // SEQ
    rows_own = emb_table.shape[0]
    capacity = max(2, 2 * tokens_dev // devices)
    at_home = c == s // 2
    part = 2 * (s % 2) + c

    def block_of(seq, core):
        return jnp.where(core == seq // 2, seq, 3 - seq)

    mine_at, near_at = block_of(s, c), block_of(s ^ 1, c)
    core_at, diag_at = block_of(s, 1 - c), block_of(s ^ 1, 1 - c)
    order = jnp.stack([mine_at, near_at, core_at, diag_at]).astype(jnp.int32)

    x_far = swap_far(layer_input)
    x_near_home = swap_near_home(layer_input)
    x_mine = jnp.where(at_home, layer_input, x_far)
    x_near_far = swap_near_far(x_mine)
    x_core = swap_core(x_mine)
    x_near = jnp.where(at_home, x_near_home, x_near_far)
    x_diag = swap_core(x_near)

    users = lengths.shape[1]
    other_lengths = swap_core(lengths)
    lengths = jnp.where(at_home, lengths, other_lengths)
    keys = (item_owner[:, 0] * rows_own + item_row).reshape(1, tokens_dev)
    keys = jnp.where(at_home, keys, swap_far(keys)).reshape(tokens_dev)
    slot_matrix, send_ids = row_slots(keys // rows_own, keys % rows_own, rows_own, devices, capacity)
    got_ids = to_owners(send_ids, devices, capacity)
    w_own = own_weights(w_attn, w_gate, part, cols)
    mg_own = dot_nt(out_grad, w_out).astype(BF)
    mg_own = after(mg_own, x_near, got_ids)
    mg_blocks = []
    mg_order = []
    for k in range(SEQ):
        piece = lax.dynamic_slice_in_dim(mg_own, (s + k) % SEQ * cols, cols, 1)
        mg_blocks.append(send(piece, lambda s, e, c: (2 * c + (s + k) % SEQ // 2, e, (s + k) % SEQ % 2)))
        mg_order.append((part - k) % SEQ)
    mg_order = jnp.stack(mg_order).astype(jnp.int32)

    x_full, acts, slopes, gate, weights, score_slope, heads = forward_attention(
        lengths, order, [x_mine, x_near, x_core, x_diag], w_own, blk, maxlen
    )

    og_own = after(out_grad, heads)
    og_far = swap_far(og_own)
    og_near_home = swap_near_home(og_own)

    mg, stats_own = event_stats(mg_order, mg_blocks, gate, heads)
    stats = [
        stats_own,
        swap_core(stats_own),
        swap_near(stats_own),
        send(stats_own, lambda s, e, c: (s ^ 1, e, 1 - c)),
    ]
    og_mine = jnp.where(at_home, out_grad, og_far)
    og_near_far = swap_near_far(og_mine)
    og_core = swap_core(og_mine)

    grads, mixed = backward_attention(
        lengths, stats, heads, gate, mg, acts, slopes, weights, score_slope, blk, maxlen
    )
    og_near = jnp.where(at_home, og_near_home, og_near_far)
    og_diag = swap_core(og_near)

    def input_part(block):
        rows = lax.dynamic_slice_in_dim(grads, block * tokens_dev, tokens_dev, 0)
        return dot_nt(rows, w_own)

    from_diag = swap_core(input_part(diag_at).astype(BF))
    near_sum = input_part(near_at) + from_diag.astype(F32)
    from_near = swap_near(near_sum.astype(BF))
    from_core = swap_core(input_part(core_at).astype(BF))
    input_grad = input_part(mine_at) + from_core.astype(F32) + og_mine.astype(F32)
    input_grad = input_grad + from_near.astype(F32)
    send_rows = jnp.dot(slot_matrix, input_grad.astype(BF), preferred_element_type=F32).astype(BF)
    got_rows = to_owners(send_rows, devices, capacity)
    new_table, new_accum = update_rows(got_ids, got_rows, emb_table, row_accum)

    proj_part = lax.dot_general(x_full, grads, TN, preferred_element_type=F32).astype(BF)
    out_part = jnp.zeros((cols, D), F32)
    for at, og_block in ((mine_at, og_mine), (near_at, og_near), (core_at, og_core), (diag_at, og_diag)):
        rows = lax.dynamic_slice_in_dim(mixed, at * tokens_dev, tokens_dev, 0)
        out_part = out_part + lax.dot_general(rows, og_block, TN, preferred_element_type=F32)
    out_part = out_part.astype(BF).reshape(cols, SEQ, cols).transpose(1, 0, 2).reshape(D, cols)
    chip_rows = D // PLANE
    merged = jnp.concatenate([proj_part, out_part], axis=1).reshape(2, 2, chip_rows, 5 * cols)
    half = 5 * cols // 2
    y, x = e // 2, e % 2

    def halves(array, bit, axis):
        kept = lax.dynamic_index_in_dim(array, bit, axis, keepdims=False)
        sent = lax.dynamic_index_in_dim(array, 1 - bit, axis, keepdims=False)
        return kept, sent

    a_kept, a_sent = halves(merged[..., :half], x, 1)
    b_kept, b_sent = halves(merged[..., half:], y, 0)
    a = (a_kept.astype(F32) + swap_x(a_sent).astype(F32)).astype(BF)
    b = (b_kept.astype(F32) + swap_y(b_sent).astype(F32)).astype(BF)
    a_kept, a_sent = halves(a, y, 0)
    b_kept, b_sent = halves(b, x, 0)
    a = a_kept.astype(F32) + swap_y(a_sent).astype(F32)
    b = b_kept.astype(F32) + swap_x(b_sent).astype(F32)
    plane_sum = jnp.concatenate([a, b], axis=1).astype(BF).reshape(2, chip_rows // 2, 5 * cols)

    first, second = halves(plane_sum, s // 2, 0)
    proj = send(first[:, : 4 * cols], lambda s, e, c: (2 * (s % 2) + c, e, s // 2)).astype(F32)
    proj = proj + send(second[:, : 4 * cols], lambda s, e, c: (2 * (s % 2) + c, e, 1 - s // 2)).astype(F32)
    out = send(first[:, 4 * cols :], lambda s, e, c: (e, 2 * (s % 2) + c, s // 2)).astype(F32)
    out = out + send(second[:, 4 * cols :], lambda s, e, c: (e, 2 * (s % 2) + c, 1 - s // 2)).astype(F32)
    grad_attn, grad_gate = split_columns(proj, cols)
    return (grad_attn, grad_gate, out, new_table, new_accum)


def solution(mesh):
    placed = (
        P(("dp", "seq"), None),
        P(("dp", "seq"), None),
        P("dp", None),
        P(("dp", "seq"), None),
        P(("dp", "seq")),
        P(),
        P(),
        P(),
        P(("seq", "dp"), None),
        P(("seq", "dp")),
    )
    paired = mesh.shape["seq"] == SEQ and mesh.shape["dp"] == 2 * PLANE
    return jax.shard_map(
        body_pairs if paired else body_whole,
        mesh=mesh,
        in_specs=placed,
        out_specs=(
            P("dp", "seq"),
            P("dp", "seq"),
            P("dp", "seq"),
            P(("seq", "dp"), None),
            P(("seq", "dp")),
        ),
        check_vma=False,
    )
```

time: 256 us -> 196 us (0.77)
  waiting for transfers between devices: 115 us -> 24.3 us
  starting transfers between devices: 11.9 us -> 70.4 us
  blocking collectives: 14.3 us -> 0 us
  matrix products: 11.1 us -> 24.8 us
  local copies, waits for them, and re-layouts: 30.1 us -> 16.7 us
  between operations: 14 us -> 1.68 us
  other arithmetic: 5.08 us -> 11.8 us
  Pallas kernels: 52 us -> 45.9 us
    all_gather x2 -> x0, waiting for transfers between devices: 60.4 us -> none  [the longest x1 36.2 us: body(): x_full = lax.all_gather(layer_input, 'seq', axis=0, tiled=True)]
    ppermute x1 -> x30, starting transfers between devices: 0.66 us -> 59.9 us  [send(): return lax.ppermute(array, ('seq', 'dp'), steps)]
    all_to_all x3 -> x2, waiting for transfers between devices: 53.6 us -> 0.01 us  [to_owners(): lax.all_to_all(rows.reshape(shape), ('seq', 'dp'), split_axis=0, concat_a...]
    ppermute x1 -> x30, waiting for transfers between devices: 0.01 us -> 24.3 us  [send(): return lax.ppermute(array, ('seq', 'dp'), steps)]
    all_gather x1 -> x0, blocking collectives: 14.3 us -> none  [body(): stats = lax.all_gather(stats_own, 'seq', axis=0, tiled=True)]
    dot_general x5 -> x8, matrix products: 5.77 us -> 14 us  [the longest x1 4.8 us: own_weights(): return jnp.dot(slices, pick, preferred_element_type=F32).astype(BF)]
    dot_general x2 -> x4, matrix products: 5.36 us -> 10.8 us  [dot_nt(): lax.dot_general(a, b, (((1,), (1,)), ((), ())), preferred_element_type=F32)]
    unnamed x36 -> x55, local copies, waits for them, and re-layouts: 10.5 us -> 5.46 us
  transfers between devices with their start and end apart: 7 -> 32, of which waited for: 5 -> 5; matrix products, arithmetic and copies ran while one was open for 14% -> 25% of each run, Pallas kernels for 9% -> 19%
where the time goes in v2:
time: 196 us
  starting transfers between devices  70.4 us (36%)
  Pallas kernels  45.9 us (23%)
  matrix products  24.8 us (13%)
  waiting for transfers between devices  24.3 us (12%)
  local copies, waits for them, and re-layouts  16.7 us (9%)
  other arithmetic  11.8 us (6%)
    ppermute x30, starting transfers between devices, send(): return lax.ppermute(array, ('seq', 'dp'), steps)  59.9 us
    ppermute x30, waiting for transfers between devices, send(): return lax.ppermute(array, ('seq', 'dp'), steps)  24.3 us
    pallas_call x1, Pallas kernels, forward_attention(): pl.pallas_call(functools.partial(forward_kernel, blk=blk, users=users, ma...  20.4 us
    pallas_call x1, Pallas kernels, backward_attention(): pl.pallas_call(functools.partial(backward_kernel, blk=blk, users=users, m...  17.2 us
    dot_general x4, matrix products, dot_nt(): lax.dot_general(a, b, (((1,), (1,)), ((), ())), preferred_element_type=F32)  10.8 us
    all_to_all x2, starting transfers between devices, to_owners(): lax.all_to_all(rows.reshape(shape), ('seq', 'dp'), split_axis=0, concat_a...  10.5 us
    unnamed x55, local copies, waits for them, and re-layouts  5.46 us
    pallas_call x1, Pallas kernels, update_rows(): pl.pallas_call(update_kernel, grid=(rows_own // blk,), in_specs=[pl.Block...  5.15 us
  transfers between devices with their start and end apart: 32, of which 5 were waited for; matrix products, arithmetic and copies ran while one was open for 25% of the time, Pallas kernels for 19%

profile of v2, /device:TPU:0, one launch (start us, length us, event | category | flops | bytes accessed | tf_op | source)
XLA Modules:
  0.0 195.7 jit_solution(4403630610208775237)
XLA Ops:
  1.5 4.9 %collective-permute-start.2 = (bf16[256,1024]{1,0:T(8,128)(2,1)}, bf16[256,1024]{1,0:T(8,128)(2,1)S(1)}, u32[]{:S(2)}, u32[]{:S(2)}) collective-permute-start(bf16[256,1024]{1,0:T(8,128)(2,1)} %param.10), channel_id=1, source_target_pairs={{0,8},{2,10},{4,12},{6,14},{8,0},{10,2},{12,4},{14,6},{17,25},{19,... | collective-permute-start | bytes 1572872 | tf_op jit(solution)/shard_map/ppermute | solution.py:470
  6.4 2.2 %collective-permute-start = (s32[1,3]{1,0:T(1,128)}, s32[1,3]{1,0:T(1,128)S(1)}, u32[]{:S(2)}, u32[]{:S(2)}) collective-permute-start(s32[1,3]{1,0:T(1,128)} %param.12), channel_id=1, source_target_pairs={{0,1},{1,0},{2,3},{3,2},{4,5},{5,4},{6,7},{7,6},{8,9},{9,8},{10,11... | collective-permute-start | bytes 44 | tf_op jit(solution)/shard_map/ppermute | solution.py:470
  10.9 2.7 %constant_dynamic-slice_fusion.5 = bf16[1024,768]{1,0:T(8,128)(2,1)} fusion(bf16[1024,3072]{1,0:T(8,128)(2,1)} %param.15, s32[]{:T(128)S(6)} %select_n.264), kind=kLoop, calls=%fused_computation.102 | loop fusion | bytes 3145732 | tf_op jit(solution)/shard_map/dynamic_slice | solution.py:357
  14.5 3.4 %convolution_convert_fusion.4 = bf16[256,1024]{1,0:T(8,128)(2,1)} fusion(bf16[256,1024]{1,0:T(8,128)(2,1)} %param.11, bf16[1024,1024]{1,0:T(8,128)(2,1)} %param.17), kind=kOutput, calls=%fused_computation.24 | convolution fusion | flops 537133056 | bytes 3145728 | tf_op jit(solution)/shard_map/dot_general | solution.py:27
  18.5 4.8 %fusion.5.refs_6_ = bf16[1024,1024]{1,0:T(8,128)(2,1)} fusion(s32[1024]{0:T(1024)S(1)} %fusion.64, bf16[1024,256]{1,0:T(8,128)(2,1)} %constant_dynamic-slice_fusion.4, bf16[1024,768]{1,0:T(8,128)(2,1)S(1)} %copy-done.7), kind=kOutput, calls=%fused_computation.6 | convolution fusion | flops 2153775104 | bytes 4198400 | tf_op jit(solution)/shard_map/dot_general | solution.py:368
  25.4 2.9 %collective-permute-start.4 = (bf16[256,1024]{1,0:T(8,128)(2,1)S(1)}, bf16[256,1024]{1,0:T(8,128)(2,1)S(1)}, u32[]{:S(2)}, u32[]{:S(2)}) collective-permute-start(bf16[256,1024]{1,0:T(8,128)(2,1)S(1)} %broadcast_select_fusion.3.refs_2_), channel_id=1, source_target_pairs={{0,1},{1,0},{2,3},{3,2},{4,5},{5,4},{6,7},{7,6},{8,9},{9,8},{10,11... | collective-permute-start | bytes 1572872 | tf_op jit(solution)/shard_map/ppermute | solution.py:470
  28.4 6.4 %collective-permute-start.5 = (bf16[256,1024]{1,0:T(8,128)(2,1)S(1)}, bf16[256,1024]{1,0:T(8,128)(2,1)S(1)}, u32[]{:S(2)}, u32[]{:S(2)}) collective-permute-start(bf16[256,1024]{1,0:T(8,128)(2,1)S(1)} %broadcast_select_fusion.2.refs_3_), channel_id=1, source_target_pairs={{0,1},{1,0},{2,3},{3,2},{4,5},{5,4},{6,7},{7,6},{8,9},{9,8},{10,11... | collective-permute-start | bytes 1572872 | tf_op jit(solution)/shard_map/ppermute | solution.py:470
  35.8 6.4 %collective-permute-start.7 = (bf16[256,256]{1,0:T(8,128)(2,1)S(1)}, bf16[256,256]{1,0:T(8,128)(2,1)S(1)}, u32[]{:S(2)}, u32[]{:S(2)}) collective-permute-start(bf16[256,256]{1,0:T(8,128)(2,1)S(1)} %get-tuple-element.56), channel_id=1, source_target_pairs={{0,1},{1,17},{2,3},{3,19},{4,5},{5,21},{6,7},{7,23},{8,8},{9,24},{... | collective-permute-start | bytes 393224 | tf_op jit(solution)/shard_map/ppermute | solution.py:470
  42.3 3.5 %collective-permute-start.9 = (bf16[256,256]{1,0:T(8,128)(2,1)S(1)}, bf16[256,256]{1,0:T(8,128)(2,1)S(1)}, u32[]{:S(2)}, u32[]{:S(2)}) collective-permute-start(bf16[256,256]{1,0:T(8,128)(2,1)S(1)} %get-tuple-element.54), channel_id=1, source_target_pairs={{0,9},{1,25},{2,11},{3,27},{4,13},{5,29},{6,15},{7,31},{8,0},{9,16... | collective-permute-start | bytes 393224 | tf_op jit(solution)/shard_map/ppermute | solution.py:470
  46.7 20.4 %attention_forward.1 = (bf16[1024,1024]{1,0:T(8,128)(2,1)}, bf16[1024,768]{1,0:T(8,128)(2,1)}, bf16[1024,1024]{1,0:T(8,128)(2,1)}, f32[1024,256]{1,0:T(8,128)}, ...) custom-call(s32[1,3]{1,0:T(1,128)} %broadcast_select_fusion.5.refs_0_, ...), custom_call_target="tpu_custom_call" | custom-call | flops 4294967296 | bytes 12582912 | tf_op jit(solution)/shard_map/attention_forward/pallas_call | solution.py:110
  67.9 3.2 %event_stats.1 = (bf16[1024,256]{1,0:T(8,128)(2,1)}, f32[8,1024]{1,0:T(8,128)}) custom-call(s32[4]{0:T(128)} %pad_add_fusion.1.refs_0_, bf16[256,256]{1,0:T(8,128)(2,1)} %copy-done.13, bf16[256,256]{1,0:T(8,128)(2,1)} %copy-done.14, bf16[256,256]{1,0:T(8,128)(2,1)} %copy-done.15, bf16[256,256]{1,0:T(8,128)(2,1)} %copy-done.16, ...), custom_call_target="tpu_custom_call" | custom-call | flops 2621440 | bytes 2621440 | tf_op jit(solution)/shard_map/event_stats/pallas_call | solution.py:172
  74.5 6.9 %all-to-all-start = ((s32[32,1,16]{2,1,0:T(1,128)}), s32[32,1,16]{2,1,0:T(1,128)S(1)}, u32[]{:S(2)}, u32[]{:S(2)}) async-start(s32[32,1,16]{2,1,0:T(1,128)} %bitcast.33), calls=%async_computation | async-start | bytes 32768 | tf_op jit(solution)/shard_map/all_to_all | solution.py:393
  82.2 3.9 %collective-permute-start.16 = (bf16[256,1024]{1,0:T(8,128)(2,1)}, bf16[256,1024]{1,0:T(8,128)(2,1)S(1)}, u32[]{:S(2)}, u32[]{:S(2)}) collective-permute-start(bf16[256,1024]{1,0:T(8,128)(2,1)} %param.11), channel_id=1, source_target_pairs={{0,8},{2,10},{4,12},{6,14},{8,0},{10,2},{12,4},{14,6},{17,25},{19,... | collective-permute-start | bytes 1572872 | tf_op jit(solution)/shard_map/ppermute | solution.py:470
  86.7 17.2 %attention_backward.1 = (bf16[1024,1024]{1,0:T(8,128)(2,1)}, bf16[1024,256]{1,0:T(8,128)(2,1)}) custom-call(s32[1,3]{1,0:T(1,128)} %broadcast_select_fusion.5.refs_0_, f32[8,1024]{1,0:T(8,128)} %get-tuple-element.24.refs_1_, f32[8,1024]{1,0:T(8,128)} %copy-done.17, f32[8,1024]{1,0:T(8,128)} %copy-done.18, f32[8,1024]{1,0:T(8,128)} %copy-done.19, ...), custom_call_target="tpu_custom_call" | custom-call | flops 4294967296 | bytes 12582912 | tf_op jit(solution)/shard_map/attention_backward/pallas_call | solution.py:272
  103.9 2.6 %convolution_convert_fusion.2 = bf16[256,1024]{1,0:T(8,128)(2,1)S(1)} fusion(bf16[1024,1024]{1,0:T(8,128)(2,1)} %fusion.5.refs_6_, bf16[1024,1024]{1,0:T(8,128)(2,1)} %get-tuple-element.30, s32[]{:T(128)S(6)} %select_n.297), kind=kOutput, calls=%fused_computation.22 | convolution fusion | flops 537133056 | bytes 3145732 | tf_op jit(solution)/shard_map/dot_general | solution.py:27
  106.6 2.0 %collective-permute-start.28 = (bf16[256,1024]{1,0:T(8,128)(2,1)S(1)}, bf16[256,1024]{1,0:T(8,128)(2,1)S(1)}, u32[]{:S(2)}, u32[]{:S(2)}) collective-permute-start(bf16[256,1024]{1,0:T(8,128)(2,1)S(1)} %convolution_convert_fusion.2), channel_id=1, source_target_pairs={{0,1},{1,0},{2,3},{3,2},{4,5},{5,4},{6,7},{7,6},{8,9},{9,8},{10,11... | collective-permute-start | bytes 1572872 | tf_op jit(solution)/shard_map/ppermute | solution.py:470
  108.6 3.2 %convolution_convert_fusion.3 = bf16[256,1024]{1,0:T(8,128)(2,1)} fusion(bf16[1024,1024]{1,0:T(8,128)(2,1)} %fusion.5.refs_6_, bf16[1024,1024]{1,0:T(8,128)(2,1)S(1)} %copy-done.21, s32[]{:T(128)S(6)} %select_n.296), kind=kOutput, calls=%fused_computation.23 | convolution fusion | flops 537133056 | bytes 3145732 | tf_op jit(solution)/shard_map/dot_general | solution.py:27
  113.8 2.4 %convolution_convert_fusion = bf16[1024,1024]{1,0:T(8,128)(2,1)S(1)} fusion(bf16[1024,1024]{1,0:T(8,128)(2,1)S(1)} %copy-done.25, bf16[1024,1024]{1,0:T(8,128)(2,1)S(1)} %copy-done.21), kind=kOutput, calls=%fused_computation.7 | convolution fusion | flops 2148532224 | bytes 6291456 | tf_op jit(solution)/shard_map/dot_general | solution.py:598
  120.6 1.7 collective-permute-start.29
  125.9 2.2 %reshape.170 = bf16[256,4,256]{2,1,0:T(4,128)(2,1)} reshape(bf16[256,1024]{1,0:T(8,128)(2,1)} %fusion.16) | data formatting | bytes 1048576 | tf_op jit(solution)/shard_map/reshape | solution.py:603
  130.3 3.0 %collective-permute-start.20 = (bf16[2,256,640]{2,1,0:T(8,128)(2,1)}, bf16[2,256,640]{2,1,0:T(8,128)(2,1)}, u32[]{:S(2)}, u32[]{:S(2)}) collective-permute-start(bf16[2,256,640]{2,1,0:T(8,128)(2,1)} %fusion.22), channel_id=1, source_target_pairs={{0,4},{1,5},{2,6},{3,7},{4,0},{5,1},{6,2},{7,3},{8,12},{9,13},{10,... | collective-permute-start | bytes 1966088 | tf_op jit(solution)/shard_map/ppermute | solution.py:470
  134.8 2.1 %fusion.13 = bf16[2,256,640]{2,1,0:T(8,128)(2,1)} fusion(bf16[2,256,640]{2,1,0:T(8,128)(2,1)} %collective-permute-done.13, bf16[2,2,256,640]{3,2,1,0:T(8,128)(2,1)S(1)} %slice.33, s32[]{:T(128)S(6)} %select_n.287), kind=kLoop, calls=%fused_computation.21 | loop fusion | flops 1310720 | bytes 1966084 | tf_op jit(solution)/shard_map/convert_element_type | solution.py:616
  136.9 4.4 %convolution_convert_fusion.1 = bf16[512,1024]{1,0:T(8,128)(2,1)} fusion(bf16[1024,1024]{1,0:T(8,128)(2,1)} %fusion.5.refs_6_, bf16[256,1024]{1,0:T(8,128)(2,1)} %collective-permute-done.29, bf16[256,1024]{1,0:T(8,128)(2,1)} %copy-done.6, bf16[256,1024]{1,0:T(8,128)(2,1)} %collective-permute-done.27, bf16[1024,1024]{1,0:T(8,128)(2,1)} %get-tuple-element.30, ...), kind=kOutput, calls=%fused_computation.10 | convolution fusion | flops 807796736 | bytes 5243908 | tf_op jit(solution)/shard_map/dot_general | solution.py:594
  141.3 3.6 %all-to-all-start.1 = ((bf16[32,16,1024]{2,1,0:T(8,128)(2,1)}), bf16[32,16,1024]{2,1,0:T(8,128)(2,1)}, u32[]{:S(2)}, u32[]{:S(2)}) async-start(bf16[32,16,1024]{2,1,0:T(8,128)(2,1)} %bitcast.78), calls=%async_computation.1 | async-start | bytes 2097152 | tf_op jit(solution)/shard_map/all_to_all | solution.py:393
  145.7 2.8 %collective-permute-start.14 = (bf16[256,640]{1,0:T(8,128)(2,1)}, bf16[256,640]{1,0:T(8,128)(2,1)}, u32[]{:S(2)}, u32[]{:S(2)}) collective-permute-start(bf16[256,640]{1,0:T(8,128)(2,1)} %dynamic-slice_bitcast_fusion.2), channel_id=1, source_target_pairs={{0,4},{1,5},{2,6},{3,7},{4,0},{5,1},{6,2},{7,3},{8,12},{9,13},{10,... | collective-permute-start | bytes 983048 | tf_op jit(solution)/shard_map/ppermute | solution.py:470
  148.4 4.3 %collective-permute-done.20 = bf16[2,256,640]{2,1,0:T(8,128)(2,1)} collective-permute-done((bf16[2,256,640]{2,1,0:T(8,128)(2,1)}, bf16[2,256,640]{2,1,0:T(8,128)(2,1)}, u32[]{:S(2)}, u32[]{:S(2)}) %collective-permute-start.20) | collective-permute-done | bytes 655392 | tf_op jit(solution)/shard_map/ppermute | solution.py:470
  154.8 1.7 collective-permute-start.21
  156.5 8.9 %collective-permute-done.14 = bf16[256,640]{1,0:T(8,128)(2,1)} collective-permute-done((bf16[256,640]{1,0:T(8,128)(2,1)}, bf16[256,640]{1,0:T(8,128)(2,1)}, u32[]{:S(2)}, u32[]{:S(2)}) %collective-permute-start.14) | collective-permute-done | bytes 327712 | tf_op jit(solution)/shard_map/ppermute | solution.py:470
  168.7 2.1 %collective-permute-start.25 = (bf16[128,256]{0,1:T(8,128)(2,1)S(1)}, bf16[128,256]{0,1:T(8,128)(2,1)S(1)}, u32[]{:S(2)}, u32[]{:S(2)}) collective-permute-start(bf16[128,256]{0,1:T(8,128)(2,1)S(1)} %slice.39), channel_id=1, source_target_pairs={{0,1},{1,3},{2,9},{3,11},{4,17},{5,19},{6,25},{7,27},{8,5},{9,7},{... | collective-permute-start | bytes 196616 | tf_op jit(solution)/shard_map/ppermute | solution.py:470
  171.6 5.5 %collective-permute-start.23 = (bf16[128,1024]{0,1:T(8,128)(2,1)S(1)}, bf16[128,1024]{0,1:T(8,128)(2,1)S(1)}, u32[]{:S(2)}, u32[]{:S(2)}) collective-permute-start(bf16[128,1024]{0,1:T(8,128)(2,1)S(1)} %slice.35), channel_id=1, source_target_pairs={{0,1},{1,9},{2,3},{3,11},{4,5},{5,13},{6,7},{7,15},{8,17},{9,25},{... | collective-permute-start | bytes 786440 | tf_op jit(solution)/shard_map/ppermute | solution.py:470
  179.8 8.7 %collective-permute-done.23 = bf16[128,1024]{0,1:T(8,128)(2,1)S(1)} collective-permute-done((bf16[128,1024]{0,1:T(8,128)(2,1)S(1)}, bf16[128,1024]{0,1:T(8,128)(2,1)S(1)}, u32[]{:S(2)}, u32[]{:S(2)}) %collective-permute-start.23) | collective-permute-done | bytes 262176 | tf_op jit(solution)/shard_map/ppermute | solution.py:470
  190.3 5.2 %update_rows.1 = (f32[512,1024]{1,0:T(8,128)}, f32[1,512]{1,0:T(1,128)}) custom-call(s32[1,512]{1,0:T(1,128)} %reshape_reshape.3.ids_ref, bf16[512,1024]{1,0:T(8,128)(2,1)} %bitcast.35.rows_ref, f32[512,1024]{1,0:T(8,128)} %table_ref.1, f32[1,512]{1,0:T(1,128)} %bitcast.88), custom_call_target="tpu_custom_call" | custom-call | flops 536870912 | bytes 5242880 | tf_op jit(solution)/shard_map/update_rows/pallas_call | solution.py:327
  (148 shorter events, 38.6 us)
Async XLA Ops:
  0.6 22.6 %collective-permute-start.1 = (bf16[256,1024]{1,0:T(8,128)(2,1)}, bf16[256,1024]{1,0:T(8,128)(2,1)S(1)}, u32[]{:S(2)}, u32[]{:S(2)}) collective-permute-start(bf16[256,1024]{1,0:T(8,128)(2,1)} %param.10), channel_id=1, source_target_pairs={{1,24},{3,26},{5,28},{7,30},{9,16},{11,18},{13,20},{15,22},{16,9},... | collective-permute-start | bytes 1572872 | tf_op jit(solution)/shard_map/ppermute | solution.py:470
  1.5 26.8 %collective-permute-start.2 = (bf16[256,1024]{1,0:T(8,128)(2,1)}, bf16[256,1024]{1,0:T(8,128)(2,1)S(1)}, u32[]{:S(2)}, u32[]{:S(2)}) collective-permute-start(bf16[256,1024]{1,0:T(8,128)(2,1)} %param.10), channel_id=1, source_target_pairs={{0,8},{2,10},{4,12},{6,14},{8,0},{10,2},{12,4},{14,6},{17,25},{19,... | collective-permute-start | bytes 1572872 | tf_op jit(solution)/shard_map/ppermute | solution.py:470
  6.4 18.4 %collective-permute-start = (s32[1,3]{1,0:T(1,128)}, s32[1,3]{1,0:T(1,128)S(1)}, u32[]{:S(2)}, u32[]{:S(2)}) collective-permute-start(s32[1,3]{1,0:T(1,128)} %param.12), channel_id=1, source_target_pairs={{0,1},{1,0},{2,3},{3,2},{4,5},{5,4},{6,7},{7,6},{8,9},{9,8},{10,11... | collective-permute-start | bytes 44 | tf_op jit(solution)/shard_map/ppermute | solution.py:470
  10.0 15.4 %collective-permute-start.26 = (s32[1,256]{1,0:T(1,128)S(1)}, s32[1,256]{1,0:T(1,128)S(1)}, u32[]{:S(2)}, u32[]{:S(2)}) collective-permute-start(s32[1,256]{1,0:T(1,128)S(1)} %bitcast.83), channel_id=1, source_target_pairs={{1,24},{3,26},{5,28},{7,30},{9,16},{11,18},{13,20},{15,22},{16,9},... | collective-permute-start | bytes 3080 | tf_op jit(solution)/shard_map/ppermute | solution.py:470
  23.3 5.0 %collective-permute-start.3 = (bf16[256,1024]{1,0:T(8,128)(2,1)S(1)}, bf16[256,1024]{1,0:T(8,128)(2,1)S(1)}, u32[]{:S(2)}, u32[]{:S(2)}) collective-permute-start(bf16[256,1024]{1,0:T(8,128)(2,1)S(1)} %broadcast_select_fusion.3.refs_2_), channel_id=1, source_target_pairs={{1,9},{3,11},{5,13},{7,15},{9,1},{11,3},{13,5},{15,7},{16,24},{18,... | collective-permute-start | bytes 1572872 | tf_op jit(solution)/shard_map/ppermute | solution.py:470
  25.4 16.9 %collective-permute-start.4 = (bf16[256,1024]{1,0:T(8,128)(2,1)S(1)}, bf16[256,1024]{1,0:T(8,128)(2,1)S(1)}, u32[]{:S(2)}, u32[]{:S(2)}) collective-permute-start(bf16[256,1024]{1,0:T(8,128)(2,1)S(1)} %broadcast_select_fusion.3.refs_2_), channel_id=1, source_target_pairs={{0,1},{1,0},{2,3},{3,2},{4,5},{5,4},{6,7},{7,6},{8,9},{9,8},{10,11... | collective-permute-start | bytes 1572872 | tf_op jit(solution)/shard_map/ppermute | solution.py:470
  28.4 17.5 %collective-permute-start.5 = (bf16[256,1024]{1,0:T(8,128)(2,1)S(1)}, bf16[256,1024]{1,0:T(8,128)(2,1)S(1)}, u32[]{:S(2)}, u32[]{:S(2)}) collective-permute-start(bf16[256,1024]{1,0:T(8,128)(2,1)S(1)} %broadcast_select_fusion.2.refs_3_), channel_id=1, source_target_pairs={{0,1},{1,0},{2,3},{3,2},{4,5},{5,4},{6,7},{7,6},{8,9},{9,8},{10,11... | collective-permute-start | bytes 1572872 | tf_op jit(solution)/shard_map/ppermute | solution.py:470
  35.2 32.0 %collective-permute-start.6 = (bf16[256,256]{1,0:T(8,128)(2,1)S(1)}, bf16[256,256]{1,0:T(8,128)(2,1)S(1)}, u32[]{:S(2)}, u32[]{:S(2)}) collective-permute-start(bf16[256,256]{1,0:T(8,128)(2,1)S(1)} %get-tuple-element.57), channel_id=1, source_target_pairs={{0,0},{1,16},{2,2},{3,18},{4,4},{5,20},{6,6},{7,22},{8,1},{9,17},{... | collective-permute-start | bytes 393224 | tf_op jit(solution)/shard_map/ppermute | solution.py:470
  35.8 31.3 %collective-permute-start.7 = (bf16[256,256]{1,0:T(8,128)(2,1)S(1)}, bf16[256,256]{1,0:T(8,128)(2,1)S(1)}, u32[]{:S(2)}, u32[]{:S(2)}) collective-permute-start(bf16[256,256]{1,0:T(8,128)(2,1)S(1)} %get-tuple-element.56), channel_id=1, source_target_pairs={{0,1},{1,17},{2,3},{3,19},{4,5},{5,21},{6,7},{7,23},{8,8},{9,24},{... | collective-permute-start | bytes 393224 | tf_op jit(solution)/shard_map/ppermute | solution.py:470
  42.2 24.9 %collective-permute-start.8 = (bf16[256,256]{1,0:T(8,128)(2,1)S(1)}, bf16[256,256]{1,0:T(8,128)(2,1)S(1)}, u32[]{:S(2)}, u32[]{:S(2)}) collective-permute-start(bf16[256,256]{1,0:T(8,128)(2,1)S(1)} %get-tuple-element.55), channel_id=1, source_target_pairs={{0,8},{1,24},{2,10},{3,26},{4,12},{5,28},{6,14},{7,30},{8,9},{9,25... | collective-permute-start | bytes 393224 | tf_op jit(solution)/shard_map/ppermute | solution.py:470
  42.3 24.9 %collective-permute-start.9 = (bf16[256,256]{1,0:T(8,128)(2,1)S(1)}, bf16[256,256]{1,0:T(8,128)(2,1)S(1)}, u32[]{:S(2)}, u32[]{:S(2)}) collective-permute-start(bf16[256,256]{1,0:T(8,128)(2,1)S(1)} %get-tuple-element.54), channel_id=1, source_target_pairs={{0,9},{1,25},{2,11},{3,27},{4,13},{5,29},{6,15},{7,31},{8,0},{9,16... | collective-permute-start | bytes 393224 | tf_op jit(solution)/shard_map/ppermute | solution.py:470
  71.1 14.9 %collective-permute-start.10 = (f32[8,1024]{1,0:T(8,128)}, f32[8,1024]{1,0:T(8,128)S(1)}, u32[]{:S(2)}, u32[]{:S(2)}) collective-permute-start(f32[8,1024]{1,0:T(8,128)} %get-tuple-element.24.refs_1_), channel_id=1, source_target_pairs={{0,1},{1,0},{2,3},{3,2},{4,5},{5,4},{6,7},{7,6},{8,9},{9,8},{10,11... | collective-permute-start | bytes 98312 | tf_op jit(solution)/shard_map/ppermute | solution.py:470
  72.3 13.7 %collective-permute-start.11 = (f32[8,1024]{1,0:T(8,128)}, f32[8,1024]{1,0:T(8,128)S(1)}, u32[]{:S(2)}, u32[]{:S(2)}) collective-permute-start(f32[8,1024]{1,0:T(8,128)} %get-tuple-element.24.refs_1_), channel_id=1, source_target_pairs={{0,8},{1,9},{2,10},{3,11},{4,12},{5,13},{6,14},{7,15},{8,0},{9,1},... | collective-permute-start | bytes 98312 | tf_op jit(solution)/shard_map/ppermute | solution.py:470
  73.0 13.1 %collective-permute-start.12 = (f32[8,1024]{1,0:T(8,128)}, f32[8,1024]{1,0:T(8,128)S(1)}, u32[]{:S(2)}, u32[]{:S(2)}) collective-permute-start(f32[8,1024]{1,0:T(8,128)} %get-tuple-element.24.refs_1_), channel_id=1, source_target_pairs={{0,9},{1,8},{2,11},{3,10},{4,13},{5,12},{6,15},{7,14},{8,1},{9,0},... | collective-permute-start | bytes 98312 | tf_op jit(solution)/shard_map/ppermute | solution.py:470
  74.5 66.7 %all-to-all-start = ((s32[32,1,16]{2,1,0:T(1,128)}), s32[32,1,16]{2,1,0:T(1,128)S(1)}, u32[]{:S(2)}, u32[]{:S(2)}) async-start(s32[32,1,16]{2,1,0:T(1,128)} %bitcast.33), calls=%async_computation | async-start | bytes 32768 | tf_op jit(solution)/shard_map/all_to_all | solution.py:393
  81.5 30.5 %collective-permute-start.15 = (bf16[256,1024]{1,0:T(8,128)(2,1)}, bf16[256,1024]{1,0:T(8,128)(2,1)S(1)}, u32[]{:S(2)}, u32[]{:S(2)}) collective-permute-start(bf16[256,1024]{1,0:T(8,128)(2,1)} %param.11), channel_id=1, source_target_pairs={{1,24},{3,26},{5,28},{7,30},{9,16},{11,18},{13,20},{15,22},{16,9},... | collective-permute-start | bytes 1572872 | tf_op jit(solution)/shard_map/ppermute | solution.py:470
  82.2 38.5 %collective-permute-start.16 = (bf16[256,1024]{1,0:T(8,128)(2,1)}, bf16[256,1024]{1,0:T(8,128)(2,1)S(1)}, u32[]{:S(2)}, u32[]{:S(2)}) collective-permute-start(bf16[256,1024]{1,0:T(8,128)(2,1)} %param.11), channel_id=1, source_target_pairs={{0,8},{2,10},{4,12},{6,14},{8,0},{10,2},{12,4},{14,6},{17,25},{19,... | collective-permute-start | bytes 1572872 | tf_op jit(solution)/shard_map/ppermute | solution.py:470
  106.6 12.2 %collective-permute-start.28 = (bf16[256,1024]{1,0:T(8,128)(2,1)S(1)}, bf16[256,1024]{1,0:T(8,128)(2,1)S(1)}, u32[]{:S(2)}, u32[]{:S(2)}) collective-permute-start(bf16[256,1024]{1,0:T(8,128)(2,1)S(1)} %convolution_convert_fusion.2), channel_id=1, source_target_pairs={{0,1},{1,0},{2,3},{3,2},{4,5},{5,4},{6,7},{7,6},{8,9},{9,8},{10,11... | collective-permute-start | bytes 1572872 | tf_op jit(solution)/shard_map/ppermute | solution.py:470
  111.8 25.1 %collective-permute-start.27 = (bf16[256,1024]{1,0:T(8,128)(2,1)}, bf16[256,1024]{1,0:T(8,128)(2,1)}, u32[]{:S(2)}, u32[]{:S(2)}) collective-permute-start(bf16[256,1024]{1,0:T(8,128)(2,1)} %convolution_convert_fusion.3), channel_id=1, source_target_pairs={{0,1},{1,0},{2,3},{3,2},{4,5},{5,4},{6,7},{7,6},{8,9},{9,8},{10,11... | collective-permute-start | bytes 1572872 | tf_op jit(solution)/shard_map/ppermute | solution.py:470
  113.0 9.3 %collective-permute-start.17 = (bf16[256,1024]{1,0:T(8,128)(2,1)S(1)}, bf16[256,1024]{1,0:T(8,128)(2,1)S(1)}, u32[]{:S(2)}, u32[]{:S(2)}) collective-permute-start(bf16[256,1024]{1,0:T(8,128)(2,1)S(1)} %broadcast_select_fusion.1), channel_id=1, source_target_pairs={{1,9},{3,11},{5,13},{7,15},{9,1},{11,3},{13,5},{15,7},{16,24},{18,... | collective-permute-start | bytes 1572872 | tf_op jit(solution)/shard_map/ppermute | solution.py:470
  117.3 17.5 %collective-permute-start.13 = (bf16[2,256,640]{2,1,0:T(8,128)(2,1)}, bf16[2,256,640]{2,1,0:T(8,128)(2,1)}, u32[]{:S(2)}, u32[]{:S(2)}) collective-permute-start(bf16[2,256,640]{2,1,0:T(8,128)(2,1)} %dynamic-slice_bitcast_fusion), channel_id=1, source_target_pairs={{0,2},{1,3},{2,0},{3,1},{4,6},{5,7},{6,4},{7,5},{8,10},{9,11},{10,... | collective-permute-start | bytes 1966088 | tf_op jit(solution)/shard_map/ppermute | solution.py:470
  118.7 4.4 %collective-permute-start.18 = (bf16[256,1024]{1,0:T(8,128)(2,1)S(1)}, bf16[256,1024]{1,0:T(8,128)(2,1)S(1)}, u32[]{:S(2)}, u32[]{:S(2)}) collective-permute-start(bf16[256,1024]{1,0:T(8,128)(2,1)S(1)} %broadcast_select_fusion.1), channel_id=1, source_target_pairs={{0,1},{1,0},{2,3},{3,2},{4,5},{5,4},{6,7},{7,6},{8,9},{9,8},{10,11... | collective-permute-start | bytes 1572872 | tf_op jit(solution)/shard_map/ppermute | solution.py:470
  120.6 16.2 %collective-permute-start.29 = (bf16[256,1024]{1,0:T(8,128)(2,1)}, bf16[256,1024]{1,0:T(8,128)(2,1)}, u32[]{:S(2)}, u32[]{:S(2)}) collective-permute-start(bf16[256,1024]{1,0:T(8,128)(2,1)} %fusion.15), channel_id=1, source_target_pairs={{0,8},{1,9},{2,10},{3,11},{4,12},{5,13},{6,14},{7,15},{8,0},{9,1},... | collective-permute-start | bytes 1572872 | tf_op jit(solution)/shard_map/ppermute | solution.py:470
  122.4 2.0 %collective-permute-start.19 = (bf16[256,1024]{1,0:T(8,128)(2,1)S(1)}, bf16[256,1024]{1,0:T(8,128)(2,1)S(1)}, u32[]{:S(2)}, u32[]{:S(2)}) collective-permute-start(bf16[256,1024]{1,0:T(8,128)(2,1)S(1)} %broadcast_select_fusion), channel_id=1, source_target_pairs={{0,1},{1,0},{2,3},{3,2},{4,5},{5,4},{6,7},{7,6},{8,9},{9,8},{10,11... | collective-permute-start | bytes 1572872 | tf_op jit(solution)/shard_map/ppermute | solution.py:470
  130.3 22.4 %collective-permute-start.20 = (bf16[2,256,640]{2,1,0:T(8,128)(2,1)}, bf16[2,256,640]{2,1,0:T(8,128)(2,1)}, u32[]{:S(2)}, u32[]{:S(2)}) collective-permute-start(bf16[2,256,640]{2,1,0:T(8,128)(2,1)} %fusion.22), channel_id=1, source_target_pairs={{0,4},{1,5},{2,6},{3,7},{4,0},{5,1},{6,2},{7,3},{8,12},{9,13},{10,... | collective-permute-start | bytes 1966088 | tf_op jit(solution)/shard_map/ppermute | solution.py:470
  141.3 49.1 %all-to-all-start.1 = ((bf16[32,16,1024]{2,1,0:T(8,128)(2,1)}), bf16[32,16,1024]{2,1,0:T(8,128)(2,1)}, u32[]{:S(2)}, u32[]{:S(2)}) async-start(bf16[32,16,1024]{2,1,0:T(8,128)(2,1)} %bitcast.78), calls=%async_computation.1 | async-start | bytes 2097152 | tf_op jit(solution)/shard_map/all_to_all | solution.py:393
  145.7 19.8 %collective-permute-start.14 = (bf16[256,640]{1,0:T(8,128)(2,1)}, bf16[256,640]{1,0:T(8,128)(2,1)}, u32[]{:S(2)}, u32[]{:S(2)}) collective-permute-start(bf16[256,640]{1,0:T(8,128)(2,1)} %dynamic-slice_bitcast_fusion.2), channel_id=1, source_target_pairs={{0,4},{1,5},{2,6},{3,7},{4,0},{5,1},{6,2},{7,3},{8,12},{9,13},{10,... | collective-permute-start | bytes 983048 | tf_op jit(solution)/shard_map/ppermute | solution.py:470
  154.8 11.8 %collective-permute-start.21 = (bf16[256,640]{1,0:T(8,128)(2,1)S(1)}, bf16[256,640]{1,0:T(8,128)(2,1)S(1)}, u32[]{:S(2)}, u32[]{:S(2)}) collective-permute-start(bf16[256,640]{1,0:T(8,128)(2,1)S(1)} %dynamic-slice_bitcast_fusion.1), channel_id=1, source_target_pairs={{0,2},{1,3},{2,0},{3,1},{4,6},{5,7},{6,4},{7,5},{8,10},{9,11},{10,... | collective-permute-start | bytes 983048 | tf_op jit(solution)/shard_map/ppermute | solution.py:470
  168.1 10.9 %collective-permute-start.24 = (bf16[128,256]{0,1:T(8,128)(2,1)S(1)}, bf16[128,256]{0,1:T(8,128)(2,1)S(1)}, u32[]{:S(2)}, u32[]{:S(2)}) collective-permute-start(bf16[128,256]{0,1:T(8,128)(2,1)S(1)} %slice.38), channel_id=1, source_target_pairs={{0,0},{1,2},{2,8},{3,10},{4,16},{5,18},{6,24},{7,26},{8,4},{9,6},{... | collective-permute-start | bytes 196616 | tf_op jit(solution)/shard_map/ppermute | solution.py:470
  168.7 10.2 %collective-permute-start.25 = (bf16[128,256]{0,1:T(8,128)(2,1)S(1)}, bf16[128,256]{0,1:T(8,128)(2,1)S(1)}, u32[]{:S(2)}, u32[]{:S(2)}) collective-permute-start(bf16[128,256]{0,1:T(8,128)(2,1)S(1)} %slice.39), channel_id=1, source_target_pairs={{0,1},{1,3},{2,9},{3,11},{4,17},{5,19},{6,25},{7,27},{8,5},{9,7},{... | collective-permute-start | bytes 196616 | tf_op jit(solution)/shard_map/ppermute | solution.py:470
  170.9 8.8 %collective-permute-start.22 = (bf16[128,1024]{0,1:T(8,128)(2,1)S(1)}, bf16[128,1024]{0,1:T(8,128)(2,1)S(1)}, u32[]{:S(2)}, u32[]{:S(2)}) collective-permute-start(bf16[128,1024]{0,1:T(8,128)(2,1)S(1)} %slice.34), channel_id=1, source_target_pairs={{0,0},{1,8},{2,2},{3,10},{4,4},{5,12},{6,6},{7,14},{8,16},{9,24},{... | collective-permute-start | bytes 786440 | tf_op jit(solution)/shard_map/ppermute | solution.py:470
  171.6 16.9 %collective-permute-start.23 = (bf16[128,1024]{0,1:T(8,128)(2,1)S(1)}, bf16[128,1024]{0,1:T(8,128)(2,1)S(1)}, u32[]{:S(2)}, u32[]{:S(2)}) collective-permute-start(bf16[128,1024]{0,1:T(8,128)(2,1)S(1)} %slice.35), channel_id=1, source_target_pairs={{0,1},{1,9},{2,3},{3,11},{4,5},{5,13},{6,7},{7,15},{8,17},{9,25},{... | collective-permute-start | bytes 786440 | tf_op jit(solution)/shard_map/ppermute | solution.py:470
  (26 other events, 151.3 us)

commit v3 on v2

v3 whole, which is shorter than its diff:
```python
import functools

import jax
import jax.numpy as jnp
from jax import lax
from jax.experimental import pallas as pl
from jax.experimental.pallas import tpu as pltpu
from jax.sharding import PartitionSpec as P

D = 1024
H = 16
DH = 64
PAIR = 2 * DH

NORM_EPS = 1e-05
LEARN_RATE = 0.1
VMEM_LIMIT = 56 * 1024 * 1024
BF = jnp.bfloat16
F32 = jnp.float32


def dot_nn(a, b):
    return lax.dot_general(a, b, (((1,), (0,)), ((), ())), preferred_element_type=F32)


def dot_nt(a, b):
    return lax.dot_general(a, b, (((1,), (1,)), ((), ())), preferred_element_type=F32)


def history_start(lengths_ref, users, place):
    start = jnp.zeros_like(place)
    end = jnp.int32(0)
    for user in range(users - 1):
        end = end + lengths_ref[0, user]
        start = jnp.where(place >= end, end, start)
    return start


def head_columns(kind, head):
    first = head * 3 * DH + kind * DH
    return slice(first, first + DH)


def forward_kernel(*refs, blk, users, maxlen, count):
    lengths_ref, order_ref = refs[:2]
    x_refs = refs[2 : 2 + count]
    w_ref = refs[2 + count]
    outs = refs[3 + count :]
    if count > 1:
        x_out_ref, outs = outs[0], outs[1:]
    acts_ref, slopes_ref, gate_ref, weights_ref, score_slope_ref, heads_ref = outs
    i = pl.program_id(0)
    block_rows = x_refs[0].shape[0]

    @pl.when(i == 0)
    def _():
        for b in range(count):
            for r in range(block_rows // blk):
                at = pl.ds(pl.multiple_of(order_ref[b] * block_rows + r * blk, blk), blk)
                x = x_refs[b][r * blk : (r + 1) * blk, :]
                if count > 1:
                    x_out_ref[at, :] = x
                half = 0.5 * dot_nn(x, w_ref[...])
                t = jnp.tanh(half)
                p = half * t
                silu = half + p
                acts_ref[at, :] = silu[:, : 3 * PAIR].astype(BF)
                gate_ref[at, :] = silu[:, 3 * PAIR :]
                slopes_ref[at, :] = (0.5 * (1.0 + t) * (1.0 + half - p)).astype(BF)

    at_i = pl.ds(pl.multiple_of(i * blk, blk), blk)
    q_half = [acts_ref[at_i, head_columns(1, h)] * jnp.asarray(0.5 * DH**-0.5, BF) for h in range(2)]
    row = i * blk + lax.broadcasted_iota(jnp.int32, (blk, blk), 0)
    col0 = lax.broadcasted_iota(jnp.int32, (blk, blk), 1)
    start = history_start(lengths_ref, users, row)

    def column(j, acc):
        at_j = pl.ds(pl.multiple_of(j * blk, blk), blk)
        col = col0 + j * blk
        allowed = (col <= row) & (col >= start)
        outs = []
        for h in range(2):
            half = dot_nt(q_half[h], acts_ref[at_j, head_columns(2, h)])
            half = jnp.where(allowed, half, -64.0)
            t = jnp.tanh(half)
            p = half * t
            weights = (half + p).astype(BF)
            weights_ref[h, :, at_j] = weights
            score_slope_ref[h, :, at_j] = ((1.0 + t) * (1.0 + half - p)).astype(BF)
            outs.append(acc[h] + dot_nn(weights, acts_ref[at_j, head_columns(0, h)]))
        return tuple(outs)

    first = history_start(lengths_ref, users, i * blk) // blk
    zero = jnp.zeros((blk, DH), F32)
    acc = lax.fori_loop(first, i + 1, column, (zero, zero))
    heads_ref[...] = (jnp.concatenate(acc, axis=1) * (1.0 / maxlen)).astype(BF)


def forward_pair(lengths, order, x_blocks, w_pair, blk, maxlen):
    count = len(x_blocks)
    block_rows = x_blocks[0].shape[0]
    positions = count * block_rows
    users = lengths.shape[1]
    elements = positions * positions
    whole = lambda i: (0, 0)
    out_specs = [
        pl.BlockSpec((positions, 3 * PAIR), whole),
        pl.BlockSpec((positions, 4 * PAIR), whole),
        pl.BlockSpec((positions, PAIR), whole),
        pl.BlockSpec((2, blk, positions), lambda i: (0, i, 0)),
        pl.BlockSpec((2, blk, positions), lambda i: (0, i, 0)),
        pl.BlockSpec((blk, PAIR), lambda i: (i, 0)),
    ]
    out_shape = [
        jax.ShapeDtypeStruct((positions, 3 * PAIR), BF),
        jax.ShapeDtypeStruct((positions, 4 * PAIR), BF),
        jax.ShapeDtypeStruct((positions, PAIR), F32),
        jax.ShapeDtypeStruct((2, positions, positions), BF),
        jax.ShapeDtypeStruct((2, positions, positions), BF),
        jax.ShapeDtypeStruct((positions, PAIR), BF),
    ]
    if count > 1:
        out_specs = [pl.BlockSpec((positions, D), whole)] + out_specs
        out_shape = [jax.ShapeDtypeStruct((positions, D), BF)] + out_shape
    return pl.pallas_call(
        functools.partial(forward_kernel, blk=blk, users=users, maxlen=maxlen, count=count),
        grid=(positions // blk,),
        in_specs=[pl.BlockSpec(memory_space=pltpu.SMEM), pl.BlockSpec(memory_space=pltpu.SMEM)]
        + [pl.BlockSpec((block_rows, D), whole)] * count
        + [pl.BlockSpec((D, 4 * PAIR), whole)],
        out_specs=out_specs,
        out_shape=out_shape,
        compiler_params=pltpu.CompilerParams(vmem_limit_bytes=VMEM_LIMIT),
        cost_estimate=pl.CostEstimate(
            flops=2 * positions * D * 4 * PAIR + 4 * elements * 256,
            bytes_accessed=4 * positions * D + 4 * elements,
            transcendentals=elements,
        ),
        name="attention_forward",
    )(lengths, order, *x_blocks, w_pair)


def stats_kernel(*refs, count, pairs):
    order_ref = refs[0]
    og_refs = refs[1 : 1 + count]
    w_ref = refs[1 + count]
    gate_refs = refs[2 + count : 2 + count + pairs]
    heads_refs = refs[2 + count + pairs : 2 + count + 2 * pairs]
    outs = refs[2 + count + 2 * pairs :]
    if count > 1:
        og_out_ref, outs = outs[0], outs[1:]
    mg_ref, stats_ref = outs
    block_rows = og_refs[0].shape[0]
    step = min(256, block_rows)
    cols = pairs * PAIR
    for b in range(count):
        for r in range(block_rows // step):
            at = pl.ds(pl.multiple_of(order_ref[b] * block_rows + r * step, step), step)
            og = og_refs[b][r * step : (r + 1) * step, :]
            if count > 1:
                og_out_ref[at, :] = og
            mg = dot_nt(og, w_ref[...])
            mg_ref[at, :] = mg
            ng = [mg[:, p * PAIR : (p + 1) * PAIR] * gate_refs[p][at, :] for p in range(pairs)]
            heads = [heads_refs[p][at, :].astype(F32) for p in range(pairs)]
            mean = jnp.sum(sum(heads), axis=1, keepdims=True) * (1.0 / cols)
            centred = [h - mean for h in heads]
            square = jnp.sum(sum(h * h for h in centred), axis=1, keepdims=True)
            total = jnp.sum(sum(ng), axis=1, keepdims=True)
            cross = jnp.sum(sum(n * h for n, h in zip(ng, centred)), axis=1, keepdims=True)
            lane = lax.broadcasted_iota(jnp.int32, (step, 128), 1)
            packed = jnp.where(lane == 0, mean, jnp.where(lane == 1, square, jnp.where(lane == 2, total, cross)))
            stats_ref[:, at] = jnp.transpose(packed)[:8, :]


def event_stats(order, og_blocks, w_out_own, gates, heads):
    positions = heads[0].shape[0]
    pairs = len(heads)
    cols = pairs * PAIR
    count = len(og_blocks)
    vmem = pl.BlockSpec(memory_space=pltpu.VMEM)
    out_shape = [
        jax.ShapeDtypeStruct((positions, cols), F32),
        jax.ShapeDtypeStruct((8, positions), F32),
    ]
    if count > 1:
        out_shape = [jax.ShapeDtypeStruct((positions, D), BF)] + out_shape
    return pl.pallas_call(
        functools.partial(stats_kernel, count=count, pairs=pairs),
        in_specs=[pl.BlockSpec(memory_space=pltpu.SMEM)] + [vmem] * (count + 1 + 2 * pairs),
        out_specs=[vmem] * len(out_shape),
        out_shape=out_shape,
        compiler_params=pltpu.CompilerParams(vmem_limit_bytes=VMEM_LIMIT),
        cost_estimate=pl.CostEstimate(
            flops=2 * positions * cols * D, bytes_accessed=4 * positions * D + 10 * positions * cols, transcendentals=0
        ),
        name="event_stats",
    )(order, *og_blocks, w_out_own, *gates, *heads)


def norm_kernel(*refs, shards, pairs):
    stats_refs = refs[:shards]
    mg_ref = refs[shards]
    heads_refs = refs[shards + 1 : shards + 1 + pairs]
    gate_refs = refs[shards + 1 + pairs : shards + 1 + 2 * pairs]
    slope_refs = refs[shards + 1 + 2 * pairs : shards + 1 + 3 * pairs]
    o_ref, gate_grad_ref, mixed_ref = refs[shards + 1 + 3 * pairs :]
    positions = mg_ref.shape[0]
    cols = pairs * PAIR
    means = [ref[0:1, :] for ref in stats_refs]
    mean = sum(means) * (1.0 / shards)
    square = jnp.zeros_like(mean)
    total = jnp.zeros_like(mean)
    cross = jnp.zeros_like(mean)
    for s, ref in enumerate(stats_refs):
        shift = means[s] - mean
        part = ref[2:3, :]
        square = square + ref[1:2, :] + cols * shift * shift
        total = total + part
        cross = cross + ref[3:4, :] + shift * part
    inv_dev = lax.rsqrt(square * (1.0 / D) + NORM_EPS)
    row8 = lax.broadcasted_iota(jnp.int32, (128, positions), 0)
    packed = jnp.where(
        row8 == 0,
        mean,
        jnp.where(row8 == 1, inv_dev, jnp.where(row8 == 2, total * (1.0 / D), cross * inv_dev * (1.0 / D))),
    )
    per_event = jnp.transpose(packed)
    mean_c = per_event[:, 0:1]
    inv_c = per_event[:, 1:2]
    total_c = per_event[:, 2:3]
    cross_c = per_event[:, 3:4]
    for p in range(pairs):
        lanes = slice(p * PAIR, (p + 1) * PAIR)
        normed = (heads_refs[p][...].astype(F32) - mean_c) * inv_c
        gate = gate_refs[p][...]
        mg = mg_ref[:, lanes]
        mixed_ref[:, lanes] = (normed * gate).astype(BF)
        gate_grad_ref[:, lanes] = (mg * normed * slope_refs[p][...].astype(F32)).astype(BF)
        o_ref[:, lanes] = (inv_c * (mg * gate - total_c - normed * cross_c)).astype(BF)


def norm_backward(stats, mg, heads, gates, slopes):
    positions, cols = mg.shape
    pairs = len(heads)
    shards = len(stats)
    vmem = pl.BlockSpec(memory_space=pltpu.VMEM)
    gate_slopes = pl.BlockSpec((positions, PAIR), lambda i: (0, 3))
    whole = lambda shape: pl.BlockSpec(shape, lambda i: (0, 0))
    out = jax.ShapeDtypeStruct((positions, cols), BF)
    return pl.pallas_call(
        functools.partial(norm_kernel, shards=shards, pairs=pairs),
        grid=(1,),
        in_specs=[whole((8, positions))] * shards
        + [whole((positions, cols))]
        + [whole((positions, PAIR))] * (2 * pairs)
        + [gate_slopes] * pairs,
        out_specs=[whole((positions, cols))] * 3,
        out_shape=[out, out, out],
        compiler_params=pltpu.CompilerParams(vmem_limit_bytes=VMEM_LIMIT),
        cost_estimate=pl.CostEstimate(flops=20 * positions * cols, bytes_accessed=18 * positions * cols, transcendentals=0),
        name="norm_backward",
    )(*stats, mg, *heads, *gates, *slopes)


def backward_kernel(
    lengths_ref, o_ref, acts_ref, slopes_ref, weights_ref, score_slope_ref, grad_ref, o_t, q_t, vg_t, kg_t, qg,
    *, blk, users, maxlen
):
    i = pl.program_id(0)
    blocks = o_ref.shape[0] // blk
    scale = DH ** (-0.5)

    @pl.when(i == 0)
    def _():
        o_t[...] = jnp.transpose(o_ref[...])
        queries = [acts_ref[:, head_columns(1, h)] for h in range(2)]
        q_t[...] = jnp.transpose(jnp.concatenate(queries, axis=1))
        vg_t[...] = jnp.zeros_like(vg_t)
        kg_t[...] = jnp.zeros_like(kg_t)

    at_i = pl.ds(pl.multiple_of(i * blk, blk), blk)

    def column(j, acc):
        at_j = pl.ds(pl.multiple_of(j * blk, blk), blk)
        outs = []
        for h in range(2):
            lanes = slice(h * DH, (h + 1) * DH)
            weight_grad = dot_nt(o_ref[at_i, lanes], acts_ref[at_j, head_columns(0, h)])
            score_grad = (weight_grad * score_slope_ref[h, :, at_j].astype(F32)).astype(BF)
            vg_t[lanes, at_j] += dot_nn(o_t[lanes, at_i], weights_ref[h, :, at_j])
            kg_t[lanes, at_j] += dot_nn(q_t[lanes, at_i], score_grad)
            outs.append(acc[h] + dot_nn(score_grad, acts_ref[at_j, head_columns(2, h)]))
        return tuple(outs)

    first = history_start(lengths_ref, users, i * blk) // blk
    zero = jnp.zeros((blk, DH), F32)
    acc = lax.fori_loop(first, i + 1, column, (zero, zero))
    qg[at_i, :] = jnp.concatenate(acc, axis=1)

    @pl.when(i == blocks - 1)
    def _():
        factor = 0.5 * scale / maxlen
        grads = [jnp.transpose(vg_t[...]) * (1.0 / maxlen), qg[...] * factor, jnp.transpose(kg_t[...]) * factor]
        pieces = [grads[kind][:, h * DH : (h + 1) * DH] for h in range(2) for kind in range(3)]
        for n in range(3):
            lanes = slice(n * PAIR, (n + 1) * PAIR)
            grad = jnp.concatenate(pieces[2 * n : 2 * n + 2], axis=1).astype(BF).astype(F32)
            grad_ref[:, lanes] = (grad * slopes_ref[:, lanes].astype(F32)).astype(BF)


def backward_pair(lengths, pair, o, acts, slopes, weights, score_slope, blk, maxlen):
    positions = o.shape[0]
    users = lengths.shape[1]
    elements = positions * positions
    whole = lambda i: (0, 0)
    return pl.pallas_call(
        functools.partial(backward_kernel, blk=blk, users=users, maxlen=maxlen),
        grid=(positions // blk,),
        in_specs=[
            pl.BlockSpec(memory_space=pltpu.SMEM),
            pl.BlockSpec((positions, PAIR), lambda i: (0, pair)),
            pl.BlockSpec((positions, 3 * PAIR), whole),
            pl.BlockSpec((positions, 3 * PAIR), whole),
            pl.BlockSpec((2, blk, positions), lambda i: (0, i, 0)),
            pl.BlockSpec((2, blk, positions), lambda i: (0, i, 0)),
        ],
        out_specs=pl.BlockSpec((positions, 3 * PAIR), whole),
        out_shape=jax.ShapeDtypeStruct((positions, 3 * PAIR), BF),
        scratch_shapes=[
            pltpu.VMEM((PAIR, positions), BF),
            pltpu.VMEM((PAIR, positions), BF),
            pltpu.VMEM((PAIR, positions), F32),
            pltpu.VMEM((PAIR, positions), F32),
            pltpu.VMEM((positions, PAIR), F32),
        ],
        compiler_params=pltpu.CompilerParams(vmem_limit_bytes=VMEM_LIMIT),
        cost_estimate=pl.CostEstimate(
            flops=8 * elements * 256, bytes_accessed=4 * elements + 16 * positions * PAIR, transcendentals=0
        ),
        name="attention_backward",
    )(lengths, o, acts, slopes, weights, score_slope)


def update_kernel(rows_ref, table_ref, accum_ref, new_table_ref, new_accum_ref, ids):
    i = pl.program_id(0)
    blk = table_ref.shape[0]
    slots = rows_ref.shape[0]

    @pl.when(i == 0)
    def _():
        numbers = jnp.transpose(rows_ref[:, D:].astype(F32))
        ids[...] = (numbers[0:1, :] * 256.0 + numbers[1:2, :]).astype(jnp.int32)

    row = i * blk + lax.broadcasted_iota(jnp.int32, (blk, slots), 0)
    hits = jnp.where(row == ids[...], 1.0, 0.0).astype(BF)
    grad = dot_nn(hits, rows_ref[:, :D])
    accum_rows = jnp.broadcast_to(accum_ref[...], (128, blk))
    accum = jnp.transpose(accum_rows)[:, :1] + jnp.mean(grad * grad, axis=1, keepdims=True)
    new_accum_ref[...] = jnp.transpose(jnp.broadcast_to(accum, (blk, 128)))[:1, :]
    new_table_ref[...] = table_ref[...] - LEARN_RATE * grad * lax.rsqrt(accum)


def update_rows(got_rows, emb_table, row_accum):
    rows_own = emb_table.shape[0]
    slots = got_rows.shape[0]
    blk = min(128, rows_own)
    new_table, new_accum = pl.pallas_call(
        update_kernel,
        grid=(rows_own // blk,),
        in_specs=[
            pl.BlockSpec((slots, D + 128), lambda i: (0, 0)),
            pl.BlockSpec((blk, D), lambda i: (i, 0)),
            pl.BlockSpec((1, blk), lambda i: (0, i)),
        ],
        out_specs=[
            pl.BlockSpec((blk, D), lambda i: (i, 0)),
            pl.BlockSpec((1, blk), lambda i: (0, i)),
        ],
        out_shape=[
            jax.ShapeDtypeStruct((rows_own, D), F32),
            jax.ShapeDtypeStruct((1, rows_own), F32),
        ],
        scratch_shapes=[pltpu.VMEM((1, slots), jnp.int32)],
        compiler_params=pltpu.CompilerParams(vmem_limit_bytes=VMEM_LIMIT),
        cost_estimate=pl.CostEstimate(
            flops=2 * rows_own * slots * D, bytes_accessed=8 * rows_own * D + 2 * slots * D, transcendentals=rows_own
        ),
        name="update_rows",
    )(got_rows, emb_table, row_accum.reshape(1, rows_own))
    return new_table, new_accum.reshape(rows_own)


def pair_weights(w_attn, w_gate, part, pairs):
    out = []
    for p in range(pairs):
        at = part * pairs + p
        attn = lax.dynamic_slice_in_dim(w_attn, at * 3 * PAIR, 3 * PAIR, 1)
        gate = lax.dynamic_slice_in_dim(w_gate, at * PAIR, PAIR, 1)
        out.append(jnp.concatenate([attn, gate], axis=1))
    return out


def row_slots(owners, rows, devices, capacity):
    events = owners.shape[0]
    owner_hits = (owners[:, None] == jnp.arange(devices, dtype=jnp.int32)[None, :]).astype(BF)
    place = jnp.arange(events, dtype=jnp.int32)
    before = (place[:, None] > place[None, :]).astype(BF)
    earlier = jnp.dot(before, owner_hits, preferred_element_type=F32)
    slots = jnp.sum(earlier * owner_hits.astype(F32), axis=1).astype(jnp.int32)
    flat_slot = owners * capacity + slots
    slot_hits = jnp.arange(devices * capacity, dtype=jnp.int32)[:, None] == flat_slot[None, :]
    lane = jnp.arange(128, dtype=jnp.int32)[None, :]
    numbers = jnp.where(lane == 0, rows[:, None] // 256, jnp.where(lane == 1, rows[:, None] % 256, 0))
    return slot_hits.astype(BF), numbers.astype(BF)


def rows_to_owners(slot_matrix, input_grad, numbers, devices, capacity):
    rows = jnp.concatenate([input_grad.astype(BF), numbers], axis=1)
    rows = jnp.dot(slot_matrix, rows, preferred_element_type=F32).astype(BF)
    got = lax.all_to_all(
        rows.reshape(devices, capacity, D + 128), ("seq", "dp"), split_axis=0, concat_axis=0, tiled=True
    )
    return got.reshape(devices * capacity, D + 128)


TN = (((0,), (0,)), ((), ()))


def dot_tn(a, b):
    return lax.dot_general(a, b, TN, preferred_element_type=F32)


def body_whole(
    layer_input, out_grad, lengths, item_owner, item_row, w_attn, w_gate, w_out, emb_table, row_accum
):
    seq_count = lax.axis_size("seq")
    dp_count = lax.axis_size("dp")
    devices = seq_count * dp_count
    seq_id = lax.axis_index("seq")
    tokens_dev = layer_input.shape[0]
    positions = tokens_dev * seq_count
    maxlen = 2 * positions // 3
    blk = min(256, positions)
    cols = D // seq_count
    pairs = cols // PAIR
    capacity = max(2, 2 * tokens_dev // devices)

    w_pairs = pair_weights(w_attn, w_gate, seq_id, pairs)
    w_out_own = lax.dynamic_slice_in_dim(w_out, seq_id * cols, cols, 0)
    slot_matrix, numbers = row_slots(item_owner[:, 0], item_row, devices, capacity)

    x_full = lax.all_gather(layer_input, "seq", axis=0, tiled=True)
    og_full = lax.all_gather(out_grad, "seq", axis=0, tiled=True)
    order = jnp.zeros((1,), jnp.int32)
    forward = [forward_pair(lengths, order, [x_full], w, blk, maxlen) for w in w_pairs]
    acts, slopes, gates, weights, score_slopes, heads = zip(*forward)
    mg, stats_own = event_stats(order, [og_full], w_out_own, gates, heads)
    stats = lax.all_gather(stats_own, "seq", axis=0, tiled=False)
    o, gate_grad, mixed = norm_backward([stats[s] for s in range(seq_count)], mg, heads, gates, slopes)
    grads = [
        backward_pair(lengths, p, o, acts[p], slopes[p], weights[p], score_slopes[p], blk, maxlen)
        for p in range(pairs)
    ]

    input_part = sum(dot_nt(grads[p], w_pairs[p][:, : 3 * PAIR]) for p in range(pairs))
    w_gate_own = lax.dynamic_slice_in_dim(w_gate, seq_id * cols, cols, 1)
    input_part = (input_part + dot_nt(gate_grad, w_gate_own)).astype(BF)
    got = lax.all_to_all(
        input_part.reshape(seq_count, tokens_dev, D), "seq", split_axis=0, concat_axis=0, tiled=True
    )
    input_grad = jnp.sum(got.astype(F32), axis=0) + out_grad.astype(F32)
    got_rows = rows_to_owners(slot_matrix, input_grad, numbers, devices, capacity)
    new_table, new_accum = update_rows(got_rows, emb_table, row_accum)

    out_part = dot_tn(mixed, og_full).astype(BF)
    share = dp_count // seq_count
    out_part = out_part.reshape(share, D // dp_count, seq_count, cols).transpose(0, 2, 1, 3).reshape(D, cols)
    merged = [dot_tn(x_full, g).astype(BF) for g in grads] + [dot_tn(x_full, gate_grad).astype(BF), out_part]
    merged = lax.psum_scatter(jnp.concatenate(merged, axis=1), "dp", scatter_dimension=0, tiled=True)
    steps = []
    for s in range(seq_count):
        for piece in range(dp_count):
            part, target = divmod(piece, seq_count)
            steps.append((s * dp_count + piece, target * dp_count + s * share + part))
    grad_out = lax.ppermute(merged[:, 4 * cols :], ("seq", "dp"), steps).astype(F32)
    grad_attn = merged[:, : 3 * cols].astype(F32)
    grad_gate = merged[:, 3 * cols : 4 * cols].astype(F32)
    return (grad_attn, grad_gate, grad_out, new_table, new_accum)


SEQ = 4
PLANE = 4


def send(array, target):
    steps = []
    for s in range(SEQ):
        for e in range(PLANE):
            for c in range(2):
                to = target(s, e, c)
                if to is not None:
                    steps.append((s * 2 * PLANE + 2 * e + c, to[0] * 2 * PLANE + 2 * to[1] + to[2]))
    return lax.ppermute(array, ("seq", "dp"), steps)


def home(s, c):
    return c == s // 2


def swap_far(array):
    return send(array, lambda s, e, c: None if home(s, c) else (3 - s, e, 1 - c))


def swap_near_home(array):
    return send(array, lambda s, e, c: (s ^ 1, e, c) if home(s, c) else None)


def swap_near_far(array):
    return send(array, lambda s, e, c: None if home(s, c) else (s ^ 1, e, c))


def swap_near(array):
    return send(array, lambda s, e, c: (s ^ 1, e, c))


def swap_core(array):
    return send(array, lambda s, e, c: (s, e, 1 - c))


def swap_x(array):
    return send(array, lambda s, e, c: (s, e ^ 1, c))


def swap_y(array):
    return send(array, lambda s, e, c: (s, e ^ 2, c))


def tie(*arrays):
    return lax.optimization_barrier(arrays)


def halves(array, bit, axis):
    kept = lax.dynamic_index_in_dim(array, bit, axis, keepdims=False)
    sent = lax.dynamic_index_in_dim(array, 1 - bit, axis, keepdims=False)
    return kept, sent


def plane_blocks(part):
    return part.reshape(2, 2, part.shape[0] // PLANE, part.shape[1])


def body_pairs(
    layer_input, out_grad, lengths, item_owner, item_row, w_attn, w_gate, w_out, emb_table, row_accum
):
    devices = 2 * PLANE * SEQ
    s = lax.axis_index("seq")
    d = lax.axis_index("dp")
    e, c = d // 2, d % 2
    y, x = e // 2, e % 2
    tokens_dev = layer_input.shape[0]
    positions = tokens_dev * SEQ
    maxlen = 2 * positions // 3
    blk = min(256, positions)
    cols = D // SEQ
    pairs = cols // PAIR
    rows_own = emb_table.shape[0]
    capacity = max(2, 2 * tokens_dev // devices)
    at_home = c == s // 2
    part = 2 * (s % 2) + c

    def block_of(seq, core):
        return jnp.where(core == seq // 2, seq, 3 - seq)

    mine_at, near_at = block_of(s, c), block_of(s ^ 1, c)
    core_at, diag_at = block_of(s, 1 - c), block_of(s ^ 1, 1 - c)
    order = jnp.stack([mine_at, near_at, core_at, diag_at]).astype(jnp.int32)

    x_far = swap_far(layer_input)
    x_near_home = swap_near_home(layer_input)
    users = lengths.shape[1]
    keys = (item_owner[:, 0] * rows_own + item_row).reshape(1, tokens_dev)
    small = jnp.concatenate([keys, jnp.pad(lengths, ((0, 0), (0, 128 - users)))], axis=1)
    small = jnp.where(at_home, small, swap_far(small))
    keys, lengths = small[0, :tokens_dev], small[:, tokens_dev : tokens_dev + users]
    w_pairs = pair_weights(w_attn, w_gate, part, pairs)
    x_mine = jnp.where(at_home, layer_input, x_far)
    x_near_far = swap_near_far(x_mine)
    x_core = swap_core(x_mine)
    x_near_far, keys, w_out_here = tie(x_near_far, keys, w_out)
    x_near = jnp.where(at_home, x_near_home, x_near_far)
    x_diag = swap_core(x_near)
    w_out_own = lax.dynamic_slice_in_dim(w_out_here, part * cols, cols, 0)
    w_gate_own = jnp.concatenate([w[:, 3 * PAIR :] for w in w_pairs], axis=1)
    slot_matrix, numbers = row_slots(keys // rows_own, keys % rows_own, devices, capacity)

    x_near, og_own = tie(x_near, out_grad)
    og_far = swap_far(og_own)
    og_near_home = swap_near_home(og_own)
    x_full, *first = forward_pair(lengths, order, [x_mine, x_near, x_core, x_diag], w_pairs[0], blk, maxlen)
    og_far, og_near_home, x_full = tie(og_far, og_near_home, x_full)
    og_mine = jnp.where(at_home, og_own, og_far)
    og_near_far = swap_near_far(og_mine)
    og_core = swap_core(og_mine)
    forward = [first]
    for p in range(1, pairs):
        forward.append(forward_pair(lengths, jnp.zeros((1,), jnp.int32), [x_full], w_pairs[p], blk, maxlen))
    acts, slopes, gates, weights, score_slopes, heads = (list(kind) for kind in zip(*forward))
    og_near_far, heads[-1] = tie(og_near_far, heads[-1])
    og_near = jnp.where(at_home, og_near_home, og_near_far)
    og_diag = swap_core(og_near)

    og_full, mg, stats_own = event_stats(order, [og_mine, og_near, og_core, og_diag], w_out_own, gates, heads)
    stats = [
        stats_own,
        swap_core(stats_own),
        swap_near(stats_own),
        send(stats_own, lambda s, e, c: (s ^ 1, e, 1 - c)),
    ]
    o, gate_grad, mixed = norm_backward(stats, mg, heads, gates, slopes)

    out_part = dot_tn(mixed, og_full).astype(BF).reshape(cols, SEQ, cols).transpose(1, 0, 2).reshape(D, cols)
    early = jnp.concatenate([dot_tn(x_full, gate_grad).astype(BF), out_part], axis=1)
    early_kept, early_sent = halves(plane_blocks(early), x, 1)
    early_got = swap_x(early_sent)

    grads = [
        backward_pair(lengths, p, o, acts[p], slopes[p], weights[p], score_slopes[p], blk, maxlen)
        for p in range(pairs)
    ]

    def input_part(block):
        at = block * tokens_dev
        total = dot_nt(lax.dynamic_slice_in_dim(gate_grad, at, tokens_dev, 0), w_gate_own)
        for p in range(pairs):
            rows = lax.dynamic_slice_in_dim(grads[p], at, tokens_dev, 0)
            total = total + dot_nt(rows, w_pairs[p][:, : 3 * PAIR])
        return total

    early_got, grads[-1] = tie(early_got, grads[-1])
    from_diag = swap_core(input_part(diag_at).astype(BF))
    near_sum = (input_part(near_at) + from_diag.astype(F32)).astype(BF)
    from_near = swap_near(near_sum)
    core_part = input_part(core_at).astype(BF)
    from_core = swap_core(core_part)
    input_grad = input_part(mine_at) + from_core.astype(F32) + og_mine.astype(F32)

    early_mid = (early_kept.astype(F32) + early_got.astype(F32)).astype(BF)
    early_kept, early_sent = halves(early_mid, y, 0)
    early_got = swap_y(early_sent)

    x_full, core_part = tie(x_full, core_part)
    attn = [dot_tn(x_full, g).astype(BF) for g in grads]
    a_kept, a_sent = halves(plane_blocks(attn[0]), x, 1)
    b_kept, b_sent = halves(plane_blocks(attn[1]), y, 0)
    a_got = swap_x(a_sent)
    b_got = swap_y(b_sent)

    input_grad = input_grad + from_near.astype(F32)
    got_rows = rows_to_owners(slot_matrix, input_grad, numbers, devices, capacity)

    a = (a_kept.astype(F32) + a_got.astype(F32)).astype(BF)
    b = (b_kept.astype(F32) + b_got.astype(F32)).astype(BF)
    a_kept, a_sent = halves(a, y, 0)
    b_kept, b_sent = halves(b, x, 0)
    a = a_kept.astype(F32) + swap_y(a_sent).astype(F32)
    b = b_kept.astype(F32) + swap_x(b_sent).astype(F32)
    early = early_kept.astype(F32) + early_got.astype(F32)

    def last(array, target):
        pieces = array.astype(BF).reshape(2, D // (2 * PLANE), array.shape[1])
        one, other = halves(pieces, s // 2, 0)
        one = send(one, lambda s, e, c: target(s, e, c, s // 2)).astype(F32)
        return one + send(other, lambda s, e, c: target(s, e, c, 1 - s // 2)).astype(F32)

    grad_out = last(early[:, cols:], lambda s, e, c, half: (e, 2 * (s % 2) + c, half))
    proj = jnp.concatenate([a, b, early[:, :cols]], axis=1)
    proj = last(proj, lambda s, e, c, half: (2 * (s % 2) + c, e, half))
    new_table, new_accum = update_rows(got_rows, emb_table, row_accum)
    return (proj[:, : 3 * cols], proj[:, 3 * cols :], grad_out, new_table, new_accum)


def solution(mesh):
    placed = (
        P(("dp", "seq"), None),
        P(("dp", "seq"), None),
        P("dp", None),
        P(("dp", "seq"), None),
        P(("dp", "seq")),
        P(),
        P(),
        P(),
        P(("seq", "dp"), None),
        P(("seq", "dp")),
    )
    paired = mesh.shape["seq"] == SEQ and mesh.shape["dp"] == 2 * PLANE
    return jax.shard_map(
        body_pairs if paired else body_whole,
        mesh=mesh,
        in_specs=placed,
        out_specs=(
            P("dp", "seq"),
            P("dp", "seq"),
            P("dp", "seq"),
            P(("seq", "dp"), None),
            P(("seq", "dp")),
        ),
        check_vma=False,
    )
```

time: 196 us -> 209 us (1.066)
  waiting for transfers between devices: 24.3 us -> 43.7 us
  Pallas kernels: 45.9 us -> 56.5 us
  matrix products: 24.8 us -> 15.6 us
  starting transfers between devices: 70.4 us -> 64.9 us
  local copies, waits for them, and re-layouts: 16.7 us -> 11.5 us
  other arithmetic: 11.8 us -> 14.3 us
    ppermute x30 -> x27, waiting for transfers between devices: 24.3 us -> 43.7 us  [send(): return lax.ppermute(array, ('seq', 'dp'), steps)]
    pallas_call x3 -> x6, Pallas kernels: 40.8 us -> 51.2 us  [the longest x2 24.4 us: forward_pair(): pl.pallas_call(functools.partial(forward_kernel, blk=blk, users=users, ma...]
    all_to_all x2 -> x1, starting transfers between devices: 10.5 us -> 3.64 us  [rows_to_owners(): lax.all_to_all(rows.reshape(devices, capacity, D + 128), ('seq', 'dp'), s...]
    dot_general x8 -> x6, matrix products: 14 us -> 9.29 us  [the longest x4 7.54 us: dot_tn(): return lax.dot_general(a, b, TN, preferred_element_type=F32)]
    dot_general x4 -> x12, matrix products: 10.8 us -> 6.34 us  [dot_nt(): lax.dot_general(a, b, (((1,), (1,)), ((), ())), preferred_element_type=F32)]
    concatenate x0 -> x4, other arithmetic: none -> 4.07 us  [the longest x2 3.35 us: pair_weights(): out.append(jnp.concatenate([attn, gate], axis=1))]
    unnamed x55 -> x48, local copies, waits for them, and re-layouts: 5.46 us -> 1.83 us
    another operation x3, other arithmetic: 2.77 us -> 0.2 us
  transfers between devices with their start and end apart: 32 -> 28, of which waited for: 5 -> 8; matrix products, arithmetic and copies ran while one was open for 25% -> 15% of each run, Pallas kernels for 19% -> 20%
where the time goes in v3:
time: 209 us; the launch traced here: 208 us
  starting transfers between devices  64.9 us (31%)
  Pallas kernels  56.5 us (27%)
  waiting for transfers between devices  43.7 us (21%)
  matrix products  15.6 us (7%)
  other arithmetic  14.3 us (7%)
  local copies, waits for them, and re-layouts  11.5 us (6%)
    ppermute x27, starting transfers between devices, send(): return lax.ppermute(array, ('seq', 'dp'), steps)  61.3 us
    ppermute x27, waiting for transfers between devices, send(): return lax.ppermute(array, ('seq', 'dp'), steps)  43.7 us
    pallas_call x2, Pallas kernels, forward_pair(): pl.pallas_call(functools.partial(forward_kernel, blk=blk, users=users, ma...  24.4 us
    pallas_call x2, Pallas kernels, backward_pair(): pl.pallas_call(functools.partial(backward_kernel, blk=blk, users=users, m...  18 us
    dot_general x4, matrix products, dot_tn(): return lax.dot_general(a, b, TN, preferred_element_type=F32)  7.54 us
    dot_general x12, matrix products, dot_nt(): lax.dot_general(a, b, (((1,), (1,)), ((), ())), preferred_element_type=F32)  6.34 us
    pallas_call x1, Pallas kernels, update_rows(): pl.pallas_call(update_kernel, grid=(rows_own // blk,), in_specs=[pl.Block...  5.28 us
    pallas_call x1, Pallas kernels, event_stats(): pl.pallas_call(functools.partial(stats_kernel, count=count, pairs=pairs),...  4.54 us
  transfers between devices with their start and end apart: 28, of which 8 were waited for; matrix products, arithmetic and copies ran while one was open for 15% of the time, Pallas kernels for 20%

profile of v3, /device:TPU:0, one launch (start us, length us, event | category | flops | bytes accessed | tf_op | source)
XLA Modules:
  0.0 207.8 jit_solution(9776152078145913642)
XLA Ops:
  1.5 4.9 %collective-permute-start = (bf16[256,1024]{1,0:T(8,128)(2,1)}, bf16[256,1024]{1,0:T(8,128)(2,1)S(1)}, u32[]{:S(2)}, u32[]{:S(2)}) collective-permute-start(bf16[256,1024]{1,0:T(8,128)(2,1)} %param.10), channel_id=1, source_target_pairs={{0,8},{2,10},{4,12},{6,14},{8,0},{10,2},{12,4},{14,6},{17,25},{19,... | collective-permute-start | bytes 1572872 | tf_op jit(solution)/shard_map/ppermute | solution.py:504
  6.5 1.9 broadcast_select_fusion.3.refs_2_
  12.6 2.4 %constant_dynamic-slice_fusion.2 = (bf16[1024,384]{1,0:T(8,128)(2,1)S(1)}, bf16[1024,384]{1,0:T(8,128)(2,1)}) fusion(bf16[1024,3072]{1,0:T(8,128)(2,1)} %param.15, s32[]{:T(128)S(6)} %select_n.189, s32[]{:T(128)S(6)} %select_n.186), kind=kLoop, calls=%fused_computation.106 | loop fusion | bytes 3145736 | tf_op jit(solution)/shard_map/dynamic_slice | solution.py:398
  15.0 18.3 %collective-permute-start.6 = (bf16[256,1024]{1,0:T(8,128)(2,1)}, bf16[256,1024]{1,0:T(8,128)(2,1)}, u32[]{:S(2)}, u32[]{:S(2)}) collective-permute-start(bf16[256,1024]{1,0:T(8,128)(2,1)} %broadcast_select_fusion.3.refs_2_), channel_id=1, source_target_pairs={{0,1},{1,0},{2,3},{3,2},{4,5},{5,4},{6,7},{7,6},{8,9},{9,8},{10,11... | collective-permute-start | bytes 1572872 | tf_op jit(solution)/shard_map/ppermute | solution.py:504
  37.8 2.3 %collective-permute-start.5 = (bf16[256,1024]{1,0:T(8,128)(2,1)}, bf16[256,1024]{1,0:T(8,128)(2,1)}, u32[]{:S(2)}, u32[]{:S(2)}) collective-permute-start(bf16[256,1024]{1,0:T(8,128)(2,1)} %param.11), channel_id=1, source_target_pairs={{0,8},{2,10},{4,12},{6,14},{8,0},{10,2},{12,4},{14,6},{17,25},{19,... | collective-permute-start | bytes 1572872 | tf_op jit(solution)/shard_map/ppermute | solution.py:504
  40.8 2.2 %pad_maximum_fusion.refs_6_ = bf16[1024,512]{1,0:T(8,128)(2,1)} fusion(bf16[1024,128]{1,0:T(8,128)(2,1)S(1)} %get-tuple-element.78, bf16[1024,384]{1,0:T(8,128)(2,1)} %get-tuple-element.76), kind=kLoop, calls=%fused_computation.27 | loop fusion | flops 2097152 | bytes 2097152 | tf_op jit(solution)/shard_map/concatenate | solution.py:400
  44.7 12.6 %attention_forward.2 = (bf16[1024,1024]{1,0:T(8,128)(2,1)}, bf16[1024,384]{1,0:T(8,128)(2,1)}, bf16[1024,512]{1,0:T(8,128)(2,1)}, f32[1024,128]{1,0:T(8,128)}, b...) custom-call(s32[1,3]{1,0:T(1,128)} %slice.27.refs_0_.lengths_ref, ...), custom_call_target="tpu_custom_call" | custom-call | flops 2147483648 | bytes 8388608 | tf_op jit(solution)/shard_map/attention_forward/pallas_call | solution.py:125
  59.2 4.2 %collective-permute-start.9 = (bf16[256,1024]{1,0:T(8,128)(2,1)S(1)}, bf16[256,1024]{1,0:T(8,128)(2,1)S(1)}, u32[]{:S(2)}, u32[]{:S(2)}) collective-permute-start(bf16[256,1024]{1,0:T(8,128)(2,1)S(1)} %broadcast_select_fusion.1.refs_1_), channel_id=1, source_target_pairs={{0,1},{1,0},{2,3},{3,2},{4,5},{5,4},{6,7},{7,6},{8,9},{9,8},{10,11... | collective-permute-start | bytes 1572872 | tf_op jit(solution)/shard_map/ppermute | solution.py:504
  63.4 11.8 %attention_forward.3 = (bf16[1024,384]{1,0:T(8,128)(2,1)}, bf16[1024,512]{1,0:T(8,128)(2,1)}, f32[1024,128]{1,0:T(8,128)}, bf16[2,1024,1024]{2,1,0:T(8,128)(2,1)...) custom-call(s32[1,3]{1,0:T(1,128)} %slice.27.refs_0_.lengths_ref, s32[1]{0:T(128)} %constant.186.clone.1.refs_1_, ...), custom_call_target="tpu_custom_call" | custom-call | flops 2147483648 | bytes 8388608 | tf_op jit(solution)/shard_map/attention_forward/pallas_call | solution.py:125
  76.8 1.5 collective-permute-done.10.refs_4_
  79.1 4.5 %event_stats.1 = (bf16[1024,1024]{1,0:T(8,128)(2,1)}, f32[1024,256]{1,0:T(8,128)}, f32[8,1024]{1,0:T(8,128)}) custom-call(s32[4]{0:T(128)} %pad_add_fusion.1.refs_1_.refs_0_, bf16[256,1024]{1,0:T(8,128)(2,1)} %copy-done.3, bf16[256,1024]{1,0:T(8,128)(2,1)} %copy-done.7, bf16[256,1024]{1,0:T(8,128)(2,1)} %copy-done.15, bf16[256,1024]{1,0:T(8,128)(2,1)} %copy-done.16, ...), custom_call_target="tpu_custom_call" | custom-call | flops 536870912 | bytes 6815744 | tf_op jit(solution)/shard_map/event_stats/pallas_call | solution.py:188
  83.8 1.8 collective-permute-start.12
  85.6 2.3 %collective-permute-done.12.refs_2_ = f32[8,1024]{1,0:T(8,128)S(1)} collective-permute-done((f32[8,1024]{1,0:T(8,128)}, f32[8,1024]{1,0:T(8,128)S(1)}, u32[]{:S(2)}, u32[]{:S(2)}) %collective-permute-start.12) | collective-permute-done | bytes 32800 | tf_op jit(solution)/shard_map/ppermute | solution.py:504
  89.8 4.2 %norm_backward.1 = (bf16[1024,256]{1,0:T(8,128)(2,1)}, bf16[1024,256]{1,0:T(8,128)(2,1)}, bf16[1024,256]{1,0:T(8,128)(2,1)}) custom-call(f32[8,1024]{1,0:T(8,128)} %get-tuple-element.53.refs_0_, f32[8,1024]{1,0:T(8,128)} %copy-done.18, f32[8,1024]{1,0:T(8,128)} %copy-done.19, f32[8,1024]{1,0:T(8,128)} %copy-done.20, f32[1024,256]{1,0:T(8,128)} %get-tuple-element.54.refs_4_, ...), custom_call_target="tpu_custom_call" | custom-call | flops 5242880 | bytes 4718592 | tf_op jit(solution)/shard_map/norm_backward/pallas_call | solution.py:251
  94.0 2.6 %convolution_convert_fusion.3 = bf16[256,1024]{1,0:T(8,128)(2,1)} fusion(bf16[1024,256]{1,0:T(8,128)(2,1)} %get-tuple-element.62, bf16[1024,1024]{1,0:T(8,128)(2,1)S(1)} %copy-done.8), kind=kOutput, calls=%fused_computation.17 | convolution fusion | flops 537133056 | bytes 3145728 | tf_op jit(solution)/shard_map/dot_general | solution.py:431
  96.6 1.5 reshape.102
  98.2 2.4 %convolution_convert_fusion.4 = bf16[1024,256]{1,0:T(8,128)(2,1)S(1)} fusion(bf16[1024,1024]{1,0:T(8,128)(2,1)} %get-tuple-element.68.refs_2_, bf16[1024,256]{1,0:T(8,128)(2,1)S(1)} %copy-done.13), kind=kOutput, calls=%fused_computation.18 | convolution fusion | flops 537133056 | bytes 3145728 | tf_op jit(solution)/shard_map/dot_general | solution.py:431
  102.9 9.0 %attention_backward.2 = bf16[1024,384]{1,0:T(8,128)(2,1)} custom-call(s32[1,3]{1,0:T(1,128)} %slice.27.refs_0_.lengths_ref, bf16[1024,256]{1,0:T(8,128)(2,1)} %get-tuple-element.58.o_ref, bf16[1024,384]{1,0:T(8,128)(2,1)} %get-tuple-element.59.acts_ref, bf16[1024,512]{1,0:T(8,128)(2,1)} %get-tuple-element.55.refs_9_.slopes_ref, ...), custom_call_target="tpu_custom_call" | custom-call | flops 2147483648 | bytes 6291456 | tf_op jit(solution)/shard_map/attention_backward/pallas_call | solution.py:317
  113.9 9.0 %attention_backward.3 = bf16[1024,384]{1,0:T(8,128)(2,1)} custom-call(s32[1,3]{1,0:T(1,128)} %slice.27.refs_0_.lengths_ref, bf16[1024,256]{1,0:T(8,128)(2,1)} %get-tuple-element.58.o_ref, bf16[1024,384]{1,0:T(8,128)(2,1)} %get-tuple-element.64.acts_ref, bf16[1024,512]{1,0:T(8,128)(2,1)} %get-tuple-element.56.refs_10_.slopes_ref, ...), custom_call_target="tpu_custom_call" | custom-call | flops 2147483648 | bytes 6291456 | tf_op jit(solution)/shard_map/attention_backward/pallas_call | solution.py:317
  126.5 4.7 %collective-permute-start.19 = (bf16[256,512]{1,0:T(8,128)(2,1)S(1)}, bf16[256,512]{1,0:T(8,128)(2,1)S(1)}, u32[]{:S(2)}, u32[]{:S(2)}) collective-permute-start(bf16[256,512]{1,0:T(8,128)(2,1)S(1)} %dynamic-slice_bitcast_fusion.4), channel_id=1, source_target_pairs={{0,4},{1,5},{2,6},{3,7},{4,0},{5,1},{6,2},{7,3},{8,12},{9,13},{10,... | collective-permute-start | bytes 786440 | tf_op jit(solution)/shard_map/ppermute | solution.py:504
  138.7 10.8 %collective-permute-done.26 = bf16[256,1024]{1,0:T(8,128)(2,1)S(1)} collective-permute-done((bf16[256,1024]{1,0:T(8,128)(2,1)S(1)}, bf16[256,1024]{1,0:T(8,128)(2,1)S(1)}, u32[]{:S(2)}, u32[]{:S(2)}) %collective-permute-start.26) | collective-permute-done | bytes 524320 | tf_op jit(solution)/shard_map/ppermute | solution.py:504
  150.0 1.5 convolution_convert_fusion
  151.6 3.6 %all-to-all-start = ((bf16[32,16,1152]{2,1,0:T(8,128)(2,1)}), bf16[32,16,1152]{2,1,0:T(8,128)(2,1)}, u32[]{:S(2)}, u32[]{:S(2)}) async-start(bf16[32,16,1152]{2,1,0:T(8,128)(2,1)} %bitcast.32), calls=%async_computation | async-start | bytes 2359296 | tf_op jit(solution)/shard_map/all_to_all | solution.py:421
  155.9 3.1 %collective-permute-start.23 = (bf16[128,256]{1,0:T(8,128)(2,1)S(1)}, bf16[128,256]{1,0:T(8,128)(2,1)S(1)}, u32[]{:S(2)}, u32[]{:S(2)}) collective-permute-start(bf16[128,256]{1,0:T(8,128)(2,1)S(1)} %get-tuple-element.84), channel_id=1, source_target_pairs={{0,1},{1,3},{2,9},{3,11},{4,17},{5,19},{6,25},{7,27},{8,5},{9,7},{... | collective-permute-start | bytes 196616 | tf_op jit(solution)/shard_map/ppermute | solution.py:504
  160.2 3.2 %collective-permute-start.16 = (bf16[256,384]{1,0:T(8,128)(2,1)S(1)}, bf16[256,384]{1,0:T(8,128)(2,1)S(1)}, u32[]{:S(2)}, u32[]{:S(2)}) collective-permute-start(bf16[256,384]{1,0:T(8,128)(2,1)S(1)} %dynamic-slice_bitcast_fusion.6), channel_id=1, source_target_pairs={{0,4},{1,5},{2,6},{3,7},{4,0},{5,1},{6,2},{7,3},{8,12},{9,13},{10,... | collective-permute-start | bytes 589832 | tf_op jit(solution)/shard_map/ppermute | solution.py:504
  164.6 3.3 %collective-permute-start.18 = (bf16[256,384]{1,0:T(8,128)(2,1)S(1)}, bf16[256,384]{1,0:T(8,128)(2,1)S(1)}, u32[]{:S(2)}, u32[]{:S(2)}) collective-permute-start(bf16[256,384]{1,0:T(8,128)(2,1)S(1)} %dynamic-slice_bitcast_fusion.5), channel_id=1, source_target_pairs={{0,2},{1,3},{2,0},{3,1},{4,6},{5,7},{6,4},{7,5},{8,10},{9,11},{10,... | collective-permute-start | bytes 589832 | tf_op jit(solution)/shard_map/ppermute | solution.py:504
  167.9 5.6 %collective-permute-done.16 = bf16[256,384]{1,0:T(8,128)(2,1)S(1)} collective-permute-done((bf16[256,384]{1,0:T(8,128)(2,1)S(1)}, bf16[256,384]{1,0:T(8,128)(2,1)S(1)}, u32[]{:S(2)}, u32[]{:S(2)}) %collective-permute-start.16) | collective-permute-done | bytes 196640 | tf_op jit(solution)/shard_map/ppermute | solution.py:504
  173.5 1.7 collective-permute-done.18
  176.1 3.8 %collective-permute-start.21 = (bf16[128,1024]{1,0:T(8,128)(2,1)S(1)}, bf16[128,1024]{1,0:T(8,128)(2,1)S(1)}, u32[]{:S(2)}, u32[]{:S(2)}) collective-permute-start(bf16[128,1024]{1,0:T(8,128)(2,1)S(1)} %get-tuple-element.80), channel_id=1, source_target_pairs={{0,1},{1,9},{2,3},{3,11},{4,5},{5,13},{6,7},{7,15},{8,17},{9,25},{... | collective-permute-start | bytes 786440 | tf_op jit(solution)/shard_map/ppermute | solution.py:504
  180.0 10.3 %collective-permute-done.23 = bf16[128,256]{1,0:T(8,128)(2,1)S(1)} collective-permute-done((bf16[128,256]{1,0:T(8,128)(2,1)S(1)}, bf16[128,256]{1,0:T(8,128)(2,1)S(1)}, u32[]{:S(2)}, u32[]{:S(2)}) %collective-permute-start.23) | collective-permute-done | bytes 65568 | tf_op jit(solution)/shard_map/ppermute | solution.py:504
  190.9 10.1 %collective-permute-done.21 = bf16[128,1024]{1,0:T(8,128)(2,1)S(1)} collective-permute-done((bf16[128,1024]{1,0:T(8,128)(2,1)S(1)}, bf16[128,1024]{1,0:T(8,128)(2,1)S(1)}, u32[]{:S(2)}, u32[]{:S(2)}) %collective-permute-start.21) | collective-permute-done | bytes 262176 | tf_op jit(solution)/shard_map/ppermute | solution.py:504
  202.5 5.3 %update_rows.1 = (f32[512,1024]{1,0:T(8,128)}, f32[1,512]{1,0:T(1,128)}) custom-call(bf16[512,1152]{1,0:T(8,128)(2,1)} %bitcast.33.rows_ref, f32[512,1024]{1,0:T(8,128)} %table_ref.1, f32[1,512]{1,0:T(1,128)} %bitcast.93), custom_call_target="tpu_custom_call" | custom-call | flops 536870912 | bytes 5242880 | tf_op jit(solution)/shard_map/update_rows/pallas_call | solution.py:368
  (141 shorter events, 39.9 us)
Async XLA Ops:
  0.6 57.7 %copy-start = (bf16[1024,1024]{1,0:T(8,128)(2,1)S(1)}, bf16[1024,1024]{1,0:T(8,128)(2,1)}, u32[]{:S(2)}) copy-start(bf16[1024,1024]{1,0:T(8,128)(2,1)} %param.17) | copy-start | bytes 6291460
  0.6 5.8 %collective-permute-start.1 = (bf16[256,1024]{1,0:T(8,128)(2,1)}, bf16[256,1024]{1,0:T(8,128)(2,1)S(1)}, u32[]{:S(2)}, u32[]{:S(2)}) collective-permute-start(bf16[256,1024]{1,0:T(8,128)(2,1)} %param.10), channel_id=1, source_target_pairs={{1,24},{3,26},{5,28},{7,30},{9,16},{11,18},{13,20},{15,22},{16,9},... | collective-permute-start | bytes 1572872 | tf_op jit(solution)/shard_map/ppermute | solution.py:504
  1.5 31.8 %collective-permute-start = (bf16[256,1024]{1,0:T(8,128)(2,1)}, bf16[256,1024]{1,0:T(8,128)(2,1)S(1)}, u32[]{:S(2)}, u32[]{:S(2)}) collective-permute-start(bf16[256,1024]{1,0:T(8,128)(2,1)} %param.10), channel_id=1, source_target_pairs={{0,8},{2,10},{4,12},{6,14},{8,0},{10,2},{12,4},{14,6},{17,25},{19,... | collective-permute-start | bytes 1572872 | tf_op jit(solution)/shard_map/ppermute | solution.py:504
  8.4 24.9 %collective-permute-start.2 = (bf16[256,1024]{1,0:T(8,128)(2,1)}, bf16[256,1024]{1,0:T(8,128)(2,1)}, u32[]{:S(2)}, u32[]{:S(2)}) collective-permute-start(bf16[256,1024]{1,0:T(8,128)(2,1)} %broadcast_select_fusion.3.refs_2_), channel_id=1, source_target_pairs={{1,9},{3,11},{5,13},{7,15},{9,1},{11,3},{13,5},{15,7},{16,24},{18,... | collective-permute-start | bytes 1572872 | tf_op jit(solution)/shard_map/ppermute | solution.py:504
  11.9 3.1 %collective-permute-start.3 = (s32[1,384]{1,0:T(1,128)S(1)}, s32[1,384]{1,0:T(1,128)S(1)}, u32[]{:S(2)}, u32[]{:S(2)}) collective-permute-start(s32[1,384]{1,0:T(1,128)S(1)} %pad_add_fusion), channel_id=1, source_target_pairs={{1,24},{3,26},{5,28},{7,30},{9,16},{11,18},{13,20},{15,22},{16,9},... | collective-permute-start | bytes 4616 | tf_op jit(solution)/shard_map/ppermute | solution.py:504
  15.0 29.2 %copy-start.21 = (s32[1,384]{1,0:T(1,128)}, s32[1,384]{1,0:T(1,128)S(1)}, u32[]{:S(2)}) copy-start(s32[1,384]{1,0:T(1,128)S(1)} %broadcast_select_fusion.4) | copy-start | bytes 4612
  15.0 29.7 %collective-permute-start.6 = (bf16[256,1024]{1,0:T(8,128)(2,1)}, bf16[256,1024]{1,0:T(8,128)(2,1)}, u32[]{:S(2)}, u32[]{:S(2)}) collective-permute-start(bf16[256,1024]{1,0:T(8,128)(2,1)} %broadcast_select_fusion.3.refs_2_), channel_id=1, source_target_pairs={{0,1},{1,0},{2,3},{3,2},{4,5},{5,4},{6,7},{7,6},{8,9},{9,8},{10,11... | collective-permute-start | bytes 1572872 | tf_op jit(solution)/shard_map/ppermute | solution.py:504
  34.1 10.6 %collective-permute-start.7 = (bf16[256,1024]{1,0:T(8,128)(2,1)}, bf16[256,1024]{1,0:T(8,128)(2,1)}, u32[]{:S(2)}, u32[]{:S(2)}) collective-permute-start(bf16[256,1024]{1,0:T(8,128)(2,1)} %broadcast_select_fusion.2.refs_3_), channel_id=1, source_target_pairs={{0,1},{1,0},{2,3},{3,2},{4,5},{5,4},{6,7},{7,6},{8,9},{9,8},{10,11... | collective-permute-start | bytes 1572872 | tf_op jit(solution)/shard_map/ppermute | solution.py:504
  36.3 21.1 %collective-permute-start.4 = (bf16[256,1024]{1,0:T(8,128)(2,1)}, bf16[256,1024]{1,0:T(8,128)(2,1)}, u32[]{:S(2)}, u32[]{:S(2)}) collective-permute-start(bf16[256,1024]{1,0:T(8,128)(2,1)} %param.11), channel_id=1, source_target_pairs={{1,24},{3,26},{5,28},{7,30},{9,16},{11,18},{13,20},{15,22},{16,9},... | collective-permute-start | bytes 1572872 | tf_op jit(solution)/shard_map/ppermute | solution.py:504
  37.8 19.6 %collective-permute-start.5 = (bf16[256,1024]{1,0:T(8,128)(2,1)}, bf16[256,1024]{1,0:T(8,128)(2,1)}, u32[]{:S(2)}, u32[]{:S(2)}) collective-permute-start(bf16[256,1024]{1,0:T(8,128)(2,1)} %param.11), channel_id=1, source_target_pairs={{0,8},{2,10},{4,12},{6,14},{8,0},{10,2},{12,4},{14,6},{17,25},{19,... | collective-permute-start | bytes 1572872 | tf_op jit(solution)/shard_map/ppermute | solution.py:504
  57.4 17.7 %copy-start.3 = (bf16[256,1024]{1,0:T(8,128)(2,1)}, bf16[256,1024]{1,0:T(8,128)(2,1)S(1)}, u32[]{:S(2)}) copy-start(bf16[256,1024]{1,0:T(8,128)(2,1)S(1)} %broadcast_select_fusion.1.refs_1_) | copy-start | bytes 1572868
  57.5 17.7 %collective-permute-start.8 = (bf16[256,1024]{1,0:T(8,128)(2,1)S(1)}, bf16[256,1024]{1,0:T(8,128)(2,1)S(1)}, u32[]{:S(2)}, u32[]{:S(2)}) collective-permute-start(bf16[256,1024]{1,0:T(8,128)(2,1)S(1)} %broadcast_select_fusion.1.refs_1_), channel_id=1, source_target_pairs={{1,9},{3,11},{5,13},{7,15},{9,1},{11,3},{13,5},{15,7},{16,24},{18,... | collective-permute-start | bytes 1572872 | tf_op jit(solution)/shard_map/ppermute | solution.py:504
  59.2 17.5 %collective-permute-start.9 = (bf16[256,1024]{1,0:T(8,128)(2,1)S(1)}, bf16[256,1024]{1,0:T(8,128)(2,1)S(1)}, u32[]{:S(2)}, u32[]{:S(2)}) collective-permute-start(bf16[256,1024]{1,0:T(8,128)(2,1)S(1)} %broadcast_select_fusion.1.refs_1_), channel_id=1, source_target_pairs={{0,1},{1,0},{2,3},{3,2},{4,5},{5,4},{6,7},{7,6},{8,9},{9,8},{10,11... | collective-permute-start | bytes 1572872 | tf_op jit(solution)/shard_map/ppermute | solution.py:504
  76.3 2.0 collective-permute-start.10
  83.6 1.9 collective-permute-start.11
  83.8 4.1 %collective-permute-start.12 = (f32[8,1024]{1,0:T(8,128)}, f32[8,1024]{1,0:T(8,128)S(1)}, u32[]{:S(2)}, u32[]{:S(2)}) collective-permute-start(f32[8,1024]{1,0:T(8,128)} %get-tuple-element.53.refs_0_), channel_id=1, source_target_pairs={{0,8},{1,9},{2,10},{3,11},{4,12},{5,13},{6,14},{7,15},{8,0},{9,1},... | collective-permute-start | bytes 98312 | tf_op jit(solution)/shard_map/ppermute | solution.py:504
  85.6 3.7 %collective-permute-start.13 = (f32[8,1024]{1,0:T(8,128)}, f32[8,1024]{1,0:T(8,128)S(1)}, u32[]{:S(2)}, u32[]{:S(2)}) collective-permute-start(f32[8,1024]{1,0:T(8,128)} %get-tuple-element.53.refs_0_), channel_id=1, source_target_pairs={{0,9},{1,8},{2,11},{3,10},{4,13},{5,12},{6,15},{7,14},{8,1},{9,0},... | collective-permute-start | bytes 98312 | tf_op jit(solution)/shard_map/ppermute | solution.py:504
  101.4 22.4 %collective-permute-start.14 = (bf16[2,256,512]{2,1,0:T(8,128)(2,1)}, bf16[2,256,512]{2,1,0:T(8,128)(2,1)S(1)}, u32[]{:S(2)}, u32[]{:S(2)}) collective-permute-start(bf16[2,256,512]{2,1,0:T(8,128)(2,1)} %fusion.22), channel_id=1, source_target_pairs={{0,2},{1,3},{2,0},{3,1},{4,6},{5,7},{6,4},{7,5},{8,10},{9,11},{10,... | collective-permute-start | bytes 1572872 | tf_op jit(solution)/shard_map/ppermute | solution.py:504
  125.3 13.3 %collective-permute-start.24 = (bf16[256,1024]{1,0:T(8,128)(2,1)S(1)}, bf16[256,1024]{1,0:T(8,128)(2,1)S(1)}, u32[]{:S(2)}, u32[]{:S(2)}) collective-permute-start(bf16[256,1024]{1,0:T(8,128)(2,1)S(1)} %fusion.8), channel_id=1, source_target_pairs={{0,1},{1,0},{2,3},{3,2},{4,5},{5,4},{6,7},{7,6},{8,9},{9,8},{10,11... | collective-permute-start | bytes 1572872 | tf_op jit(solution)/shard_map/ppermute | solution.py:504
  125.8 9.5 %collective-permute-start.25 = (bf16[256,1024]{1,0:T(8,128)(2,1)S(1)}, bf16[256,1024]{1,0:T(8,128)(2,1)S(1)}, u32[]{:S(2)}, u32[]{:S(2)}) collective-permute-start(bf16[256,1024]{1,0:T(8,128)(2,1)S(1)} %fusion.9), channel_id=1, source_target_pairs={{0,1},{1,0},{2,3},{3,2},{4,5},{5,4},{6,7},{7,6},{8,9},{9,8},{10,11... | collective-permute-start | bytes 1572872 | tf_op jit(solution)/shard_map/ppermute | solution.py:504
  126.5 12.0 %collective-permute-start.19 = (bf16[256,512]{1,0:T(8,128)(2,1)S(1)}, bf16[256,512]{1,0:T(8,128)(2,1)S(1)}, u32[]{:S(2)}, u32[]{:S(2)}) collective-permute-start(bf16[256,512]{1,0:T(8,128)(2,1)S(1)} %dynamic-slice_bitcast_fusion.4), channel_id=1, source_target_pairs={{0,4},{1,5},{2,6},{3,7},{4,0},{5,1},{6,2},{7,3},{8,12},{9,13},{10,... | collective-permute-start | bytes 786440 | tf_op jit(solution)/shard_map/ppermute | solution.py:504
  133.5 25.5 %collective-permute-start.15 = (bf16[2,256,384]{2,1,0:T(8,128)(2,1)}, bf16[2,256,384]{2,1,0:T(8,128)(2,1)}, u32[]{:S(2)}, u32[]{:S(2)}) collective-permute-start(bf16[2,256,384]{2,1,0:T(8,128)(2,1)} %dynamic-slice_bitcast_fusion.1), channel_id=1, source_target_pairs={{0,2},{1,3},{2,0},{3,1},{4,6},{5,7},{6,4},{7,5},{8,10},{9,11},{10,... | collective-permute-start | bytes 1179656 | tf_op jit(solution)/shard_map/ppermute | solution.py:504
  135.8 13.7 %copy-start.4 = (bf16[256,1024]{1,0:T(8,128)(2,1)S(1)}, bf16[256,1024]{1,0:T(8,128)(2,1)}, u32[]{:S(2)}) copy-start(bf16[256,1024]{1,0:T(8,128)(2,1)} %copy-done.3) | copy-start | bytes 1572868
  135.8 13.7 %collective-permute-start.26 = (bf16[256,1024]{1,0:T(8,128)(2,1)S(1)}, bf16[256,1024]{1,0:T(8,128)(2,1)S(1)}, u32[]{:S(2)}, u32[]{:S(2)}) collective-permute-start(bf16[256,1024]{1,0:T(8,128)(2,1)S(1)} %fusion.11), channel_id=1, source_target_pairs={{0,8},{1,9},{2,10},{3,11},{4,12},{5,13},{6,14},{7,15},{8,0},{9,1},... | collective-permute-start | bytes 1572872 | tf_op jit(solution)/shard_map/ppermute | solution.py:504
  137.2 26.2 %collective-permute-start.17 = (bf16[2,256,384]{2,1,0:T(8,128)(2,1)}, bf16[2,256,384]{2,1,0:T(8,128)(2,1)}, u32[]{:S(2)}, u32[]{:S(2)}) collective-permute-start(bf16[2,256,384]{2,1,0:T(8,128)(2,1)} %dynamic-slice_bitcast_fusion), channel_id=1, source_target_pairs={{0,4},{1,5},{2,6},{3,7},{4,0},{5,1},{6,2},{7,3},{8,12},{9,13},{10,... | collective-permute-start | bytes 1179656 | tf_op jit(solution)/shard_map/ppermute | solution.py:504
  151.6 51.0 %all-to-all-start = ((bf16[32,16,1152]{2,1,0:T(8,128)(2,1)}), bf16[32,16,1152]{2,1,0:T(8,128)(2,1)}, u32[]{:S(2)}, u32[]{:S(2)}) async-start(bf16[32,16,1152]{2,1,0:T(8,128)(2,1)} %bitcast.32), calls=%async_computation | async-start | bytes 2359296 | tf_op jit(solution)/shard_map/all_to_all | solution.py:421
  155.2 24.7 %collective-permute-start.22 = (bf16[128,256]{1,0:T(8,128)(2,1)S(1)}, bf16[128,256]{1,0:T(8,128)(2,1)S(1)}, u32[]{:S(2)}, u32[]{:S(2)}) collective-permute-start(bf16[128,256]{1,0:T(8,128)(2,1)S(1)} %get-tuple-element.83), channel_id=1, source_target_pairs={{0,0},{1,2},{2,8},{3,10},{4,16},{5,18},{6,24},{7,26},{8,4},{9,6},{... | collective-permute-start | bytes 196616 | tf_op jit(solution)/shard_map/ppermute | solution.py:504
  155.9 34.3 %collective-permute-start.23 = (bf16[128,256]{1,0:T(8,128)(2,1)S(1)}, bf16[128,256]{1,0:T(8,128)(2,1)S(1)}, u32[]{:S(2)}, u32[]{:S(2)}) collective-permute-start(bf16[128,256]{1,0:T(8,128)(2,1)S(1)} %get-tuple-element.84), channel_id=1, source_target_pairs={{0,1},{1,3},{2,9},{3,11},{4,17},{5,19},{6,25},{7,27},{8,5},{9,7},{... | collective-permute-start | bytes 196616 | tf_op jit(solution)/shard_map/ppermute | solution.py:504
  160.2 13.3 %collective-permute-start.16 = (bf16[256,384]{1,0:T(8,128)(2,1)S(1)}, bf16[256,384]{1,0:T(8,128)(2,1)S(1)}, u32[]{:S(2)}, u32[]{:S(2)}) collective-permute-start(bf16[256,384]{1,0:T(8,128)(2,1)S(1)} %dynamic-slice_bitcast_fusion.6), channel_id=1, source_target_pairs={{0,4},{1,5},{2,6},{3,7},{4,0},{5,1},{6,2},{7,3},{8,12},{9,13},{10,... | collective-permute-start | bytes 589832 | tf_op jit(solution)/shard_map/ppermute | solution.py:504
  164.6 10.7 %collective-permute-start.18 = (bf16[256,384]{1,0:T(8,128)(2,1)S(1)}, bf16[256,384]{1,0:T(8,128)(2,1)S(1)}, u32[]{:S(2)}, u32[]{:S(2)}) collective-permute-start(bf16[256,384]{1,0:T(8,128)(2,1)S(1)} %dynamic-slice_bitcast_fusion.5), channel_id=1, source_target_pairs={{0,2},{1,3},{2,0},{3,1},{4,6},{5,7},{6,4},{7,5},{8,10},{9,11},{10,... | collective-permute-start | bytes 589832 | tf_op jit(solution)/shard_map/ppermute | solution.py:504
  175.5 15.5 %collective-permute-start.20 = (bf16[128,1024]{1,0:T(8,128)(2,1)S(1)}, bf16[128,1024]{1,0:T(8,128)(2,1)S(1)}, u32[]{:S(2)}, u32[]{:S(2)}) collective-permute-start(bf16[128,1024]{1,0:T(8,128)(2,1)S(1)} %get-tuple-element.79), channel_id=1, source_target_pairs={{0,0},{1,8},{2,2},{3,10},{4,4},{5,12},{6,6},{7,14},{8,16},{9,24},{... | collective-permute-start | bytes 786440 | tf_op jit(solution)/shard_map/ppermute | solution.py:504
  176.1 24.9 %collective-permute-start.21 = (bf16[128,1024]{1,0:T(8,128)(2,1)S(1)}, bf16[128,1024]{1,0:T(8,128)(2,1)S(1)}, u32[]{:S(2)}, u32[]{:S(2)}) collective-permute-start(bf16[128,1024]{1,0:T(8,128)(2,1)S(1)} %get-tuple-element.80), channel_id=1, source_target_pairs={{0,1},{1,9},{2,3},{3,11},{4,5},{5,13},{6,7},{7,15},{8,17},{9,25},{... | collective-permute-start | bytes 786440 | tf_op jit(solution)/shard_map/ppermute | solution.py:504
  (21 other events, 87.5 us)
